TPU v7x, 32 devices: a whole 2x2x4 slice. The times are simulated.
32 devices in a mesh: dp: 16 (over z, y, core), mlp: 2 (over x).
Axes of the slice: x: 2, y: 2, z: 4, core: 2. Of those that a mesh axis runs over, the one named last changes fastest.
Arguments:
- tokens: bfloat16 [125440, 768], P(('dp', 'mlp')), may hold values from -6 to 6
- window_extent: int32 [640, 2], P(('dp', 'mlp')), may hold values from 0 to 14, as said below
- ln1_gain: float32 [768], replicated, may hold values from 0.5 to 1.5
- ln1_bias: float32 [768], replicated, may hold values from -3 to 3
- qkv_weight: bfloat16 [768, 2304], replicated, may hold values from -0.21875 to 0.21875
- query_bias: float32 [768], replicated, may hold values from -3 to 3
- value_bias: float32 [768], replicated, may hold values from -3 to 3
- rel_h: float32 [27, 64], replicated, may hold values from -0.6 to 0.6
- rel_w: float32 [27, 64], replicated, may hold values from -0.6 to 0.6
- proj_weight: bfloat16 [768, 768], replicated, may hold values from -0.875 to 0.875
- proj_bias: float32 [768], replicated, may hold values from -3 to 3
- ln2_gain: float32 [768], replicated, may hold values from 0.5 to 1.5
- ln2_bias: float32 [768], replicated, may hold values from -3 to 3
- up_weight: bfloat16 [768, 3072], P(None, 'mlp'), may hold values from -0.21875 to 0.21875
- up_bias: float32 [3072], P('mlp'), may hold values from -3 to 3
- down_weight: bfloat16 [768, 3072], P(None, 'mlp'), may hold values from -0.109375 to 0.109375
- down_bias: float32 [768], replicated, may hold values from -3 to 3
- grad_out: bfloat16 [125440, 768], P(('dp', 'mlp')), may hold values from -6 to 6
Outputs:
- output: bfloat16 [125440, 768], P(('dp', 'mlp'))
- grad_tokens: bfloat16 [125440, 768], P(('dp', 'mlp'))
- grad_ln1_gain: float32 [768], replicated
- grad_ln1_bias: float32 [768], replicated
- grad_qkv_weight: float32 [768, 2304], P('dp', 'mlp')
- grad_query_bias: float32 [768], replicated
- grad_value_bias: float32 [768], replicated
- grad_rel_h: float32 [27, 64], replicated
- grad_rel_w: float32 [27, 64], replicated
- grad_proj_weight: float32 [768, 768], P('dp', 'mlp')
- grad_proj_bias: float32 [768], replicated
- grad_ln2_gain: float32 [768], replicated
- grad_ln2_bias: float32 [768], replicated
- grad_up_weight: float32 [768, 3072], P('dp', 'mlp')
- grad_up_bias: float32 [3072], replicated
- grad_down_weight: float32 [768, 3072], P('dp', 'mlp')
- grad_down_bias: float32 [768], replicated
Inputs may be any that keep to these rules, and one draw needn't show every extreme that they name: `window_extent`: each aligned group of 40 window slots (one index of dp) holds whole images placed in order from its first slot; an image of 48, 64 or 80 patches a side takes 16, 25 or 36 slots in row-major window order, with extents 14 except in its last window row or column (6, 8 or 10); slots after the group's last image have extents 0 and 0.
All inputs are finite; a program needn't handle non-finite values.
Results may differ from a plain program's by a relative error of at most 0.018.
Values may be sent and summed in bfloat16 or wider, within the bound.
No kernel may reach another device: no remote copies, remote signals or barrier semaphores. Data moves between devices by JAX's collectives and lax.ppermute only.
A program may use at most 960 MiB of HBM per device.

v0:
```python
import jax
import jax.numpy as jnp
from jax import lax
from jax.sharding import PartitionSpec as P

HEADS = 12
HEAD_DIM = 64
WIN = 14


NEGATIVE = -1e30
EPSILON = 1e-06
HIGHEST = lax.Precision.HIGHEST
CONTRACT_ROWS = (((0,), (0,)), ((), ()))
CONTRACT_LAST = (((1,), (1,)), ((), ()))


def shortened(shard):
    return jax.tree.map(lambda a: a.astype(jnp.bfloat16) if a.dtype == jnp.float32 else a, shard)


def layer_norm(values, scale_vec, offset_vec):
    centre = jnp.mean(values, axis=-1, keepdims=True)
    centred = values - centre
    second = jnp.mean(centred * centred, axis=-1, keepdims=True)
    return centred * lax.rsqrt(second + EPSILON) * scale_vec + offset_vec


def gelu_exact(values):
    return jax.nn.gelu(values, approximate=False)


def offset_picks(table_rows):
    places = jnp.arange(WIN)
    target = places[:, None] - places[None, :] + WIN - 1
    return (target[:, :, None] == jnp.arange(table_rows)[None, None, :]).astype(jnp.float32)


def window_valid(extent):
    places = jnp.arange(WIN * WIN)
    row_index = places // WIN
    col_index = places % WIN
    return (row_index[None, :] < extent[:, 0:1]) & (col_index[None, :] < extent[:, 1:2])


def attention_scores(queries_split, keys_split, queries_grid, usable, table_h, table_w):
    window_count = usable.shape[0]
    window_area = WIN * WIN
    scores = jnp.einsum(
        "wqhd,wkhd->whqk", queries_split, keys_split, preferred_element_type=jnp.float32
    ) * HEAD_DIM ** (-0.5)
    along_h = jnp.einsum("wrchd,rkd->whrck", queries_grid, table_h, precision=HIGHEST)
    along_w = jnp.einsum("wrchd,ckd->whrck", queries_grid, table_w, precision=HIGHEST)
    scores = (
        scores.reshape(window_count, HEADS, WIN, WIN, WIN, WIN)
        + along_h[..., :, None]
        + along_w[..., None, :]
    )
    scores = scores.reshape(window_count, HEADS, window_area, window_area)
    return jnp.where(usable[:, None, None, :], scores, NEGATIVE)


def per_device(
    tokens,
    window_extent,
    ln1_gain,
    ln1_bias,
    qkv_weight,
    query_bias,
    value_bias,
    rel_h,
    rel_w,
    proj_weight,
    proj_bias,
    ln2_gain,
    ln2_bias,
    up_weight,
    up_bias,
    down_weight,
    down_bias,
    grad_out,
):
    model_width = tokens.shape[1]
    window_count = window_extent.shape[0]
    window_area = WIN * WIN
    local_rows = window_count * window_area
    usable = window_valid(window_extent)
    row_mask = usable.reshape(local_rows, 1).astype(jnp.float32)
    inputs = tokens.astype(jnp.float32)
    normed, ln1_back = jax.vjp(layer_norm, inputs, ln1_gain, ln1_bias)
    normed_low = normed.astype(jnp.bfloat16)
    projected = jnp.dot(normed_low, qkv_weight, preferred_element_type=jnp.float32)
    queries = (projected[:, :model_width] + query_bias).astype(jnp.bfloat16)
    key_rows = projected[:, model_width : 2 * model_width].astype(jnp.bfloat16)
    value_rows = (projected[:, 2 * model_width :] + value_bias).astype(jnp.bfloat16)
    queries_split = queries.reshape(window_count, window_area, HEADS, HEAD_DIM)
    keys_split = key_rows.reshape(window_count, window_area, HEADS, HEAD_DIM)
    values_split = value_rows.reshape(window_count, window_area, HEADS, HEAD_DIM)
    queries_grid = queries.astype(jnp.float32).reshape(window_count, WIN, WIN, HEADS, HEAD_DIM)
    selector = offset_picks(rel_h.shape[0])
    table_h = jnp.einsum("rkj,jd->rkd", selector, rel_h, precision=HIGHEST)
    table_w = jnp.einsum("rkj,jd->rkd", selector, rel_w, precision=HIGHEST)
    scores = attention_scores(queries_split, keys_split, queries_grid, usable, table_h, table_w)
    row_top = jnp.max(scores, axis=-1, keepdims=True)
    raised = jnp.exp(scores - row_top)
    row_total = jnp.sum(raised, axis=-1, keepdims=True)
    log_total = row_top + jnp.log(row_total)
    weights_low = (raised / row_total).astype(jnp.bfloat16)
    attended = jnp.einsum(
        "whqk,wkhd->wqhd", weights_low, values_split, preferred_element_type=jnp.float32
    )
    attended = attended.reshape(local_rows, model_width).astype(jnp.bfloat16)
    branch = jnp.dot(attended, proj_weight, preferred_element_type=jnp.float32) + proj_bias
    middle = inputs + branch
    mlp_normed, ln2_back = jax.vjp(layer_norm, middle, ln2_gain, ln2_bias)
    mlp_input = mlp_normed.astype(jnp.bfloat16)
    up_full, down_full, up_bias_full = (
        lax.all_gather(up_weight, "mlp", axis=1, tiled=True),
        lax.all_gather(down_weight, "mlp", axis=1, tiled=True),
        lax.all_gather(up_bias.astype(jnp.bfloat16), "mlp", axis=0, tiled=True).astype(
            up_bias.dtype
        ),
    )
    hidden_pre = jnp.dot(mlp_input, up_full, preferred_element_type=jnp.float32) + up_bias_full
    hidden_act, gelu_back = jax.vjp(gelu_exact, hidden_pre)
    hidden_low = hidden_act.astype(jnp.bfloat16)
    mlp_out = (
        lax.dot_general(hidden_low, down_full, CONTRACT_LAST, preferred_element_type=jnp.float32)
        + down_bias
    )
    output = (row_mask * (middle + mlp_out)).astype(jnp.bfloat16)
    grad_rows = grad_out.astype(jnp.float32) * row_mask
    grad_low = grad_rows.astype(jnp.bfloat16)
    grad_down_bias = jnp.sum(grad_low.astype(jnp.float32), axis=0)
    grad_act = jnp.dot(grad_low, down_full, preferred_element_type=jnp.float32)
    (grad_pre,) = gelu_back(grad_act)
    grad_pre_low = grad_pre.astype(jnp.bfloat16)
    grad_down = lax.dot_general(
        grad_low, hidden_low, CONTRACT_ROWS, preferred_element_type=jnp.float32
    )
    grad_up = lax.dot_general(
        mlp_input, grad_pre_low, CONTRACT_ROWS, preferred_element_type=jnp.float32
    )
    grad_up_bias = jnp.sum(grad_pre_low.astype(jnp.float32), axis=0)
    grad_mlp_input = lax.dot_general(
        grad_pre_low, up_full, CONTRACT_LAST, preferred_element_type=jnp.float32
    )
    grad_middle_norm, grad_ln2_gain, grad_ln2_bias = ln2_back(grad_mlp_input)
    grad_middle = grad_rows + grad_middle_norm
    grad_branch_low = grad_middle.astype(jnp.bfloat16)
    grad_proj_bias = jnp.sum(grad_branch_low.astype(jnp.float32), axis=0)
    grad_proj = lax.dot_general(
        attended, grad_branch_low, CONTRACT_ROWS, preferred_element_type=jnp.float32
    )
    grad_attended = lax.dot_general(
        grad_branch_low, proj_weight, CONTRACT_LAST, preferred_element_type=jnp.float32
    ).astype(jnp.bfloat16)
    grad_split = grad_attended.reshape(window_count, window_area, HEADS, HEAD_DIM)
    scores = attention_scores(queries_split, keys_split, queries_grid, usable, table_h, table_w)
    weights = jnp.exp(scores - log_total)
    weights_low = weights.astype(jnp.bfloat16)
    grad_weights = jnp.einsum(
        "wqhd,wkhd->whqk", grad_split, values_split, preferred_element_type=jnp.float32
    )
    grad_values = jnp.einsum(
        "whqk,wqhd->wkhd", weights_low, grad_split, preferred_element_type=jnp.float32
    )
    grad_scores = weights * (grad_weights - jnp.sum(weights * grad_weights, axis=-1, keepdims=True))
    grad_scores = jnp.where(usable[:, None, None, :], grad_scores, 0.0)
    grad_scores_low = grad_scores.astype(jnp.bfloat16)
    score_scale = HEAD_DIM ** (-0.5)
    grad_queries = (
        jnp.einsum(
            "whqk,wkhd->wqhd", grad_scores_low, keys_split, preferred_element_type=jnp.float32
        )
        * score_scale
    )
    grad_keys = (
        jnp.einsum(
            "whqk,wqhd->wkhd", grad_scores_low, queries_split, preferred_element_type=jnp.float32
        )
        * score_scale
    )
    grad_grid = grad_scores_low.astype(jnp.float32).reshape(window_count, HEADS, WIN, WIN, WIN, WIN)
    grad_along_h = jnp.sum(grad_grid, axis=5)
    grad_along_w = jnp.sum(grad_grid, axis=4)
    grad_rel_part = jnp.einsum(
        "whrck,rkd->wrchd", grad_along_h, table_h, precision=HIGHEST
    ) + jnp.einsum("whrck,ckd->wrchd", grad_along_w, table_w, precision=HIGHEST)
    grad_queries = grad_queries + grad_rel_part.reshape(window_count, window_area, HEADS, HEAD_DIM)
    grad_table_h = jnp.einsum("whrck,wrchd->rkd", grad_along_h, queries_grid, precision=HIGHEST)
    grad_table_w = jnp.einsum("whrck,wrchd->ckd", grad_along_w, queries_grid, precision=HIGHEST)
    grad_rel_h = jnp.einsum("rkj,rkd->jd", selector, grad_table_h, precision=HIGHEST)
    grad_rel_w = jnp.einsum("rkj,rkd->jd", selector, grad_table_w, precision=HIGHEST)
    grad_mixed = jnp.concatenate(
        [
            grad_queries.reshape(local_rows, model_width).astype(jnp.bfloat16),
            grad_keys.reshape(local_rows, model_width).astype(jnp.bfloat16),
            grad_values.reshape(local_rows, model_width).astype(jnp.bfloat16),
        ],
        axis=1,
    )
    grad_query_bias = jnp.sum(grad_mixed[:, :model_width].astype(jnp.float32), axis=0)
    grad_value_bias = jnp.sum(grad_mixed[:, 2 * model_width :].astype(jnp.float32), axis=0)
    grad_qkv = lax.dot_general(
        normed_low, grad_mixed, CONTRACT_ROWS, preferred_element_type=jnp.float32
    )
    grad_normed = lax.dot_general(
        grad_mixed, qkv_weight, CONTRACT_LAST, preferred_element_type=jnp.float32
    )
    grad_input_norm, grad_ln1_gain, grad_ln1_bias = ln1_back(grad_normed)
    grad_tokens = (grad_middle + grad_input_norm).astype(jnp.bfloat16)
    spread = (grad_qkv, grad_proj, grad_up, grad_down)
    spread = tuple(
        (
            lax.psum_scatter(
                spread[0].astype(jnp.bfloat16), "mlp", scatter_dimension=1, tiled=True
            ).astype(jnp.float32),
            lax.psum_scatter(
                spread[1].astype(jnp.bfloat16), "mlp", scatter_dimension=1, tiled=True
            ).astype(jnp.float32),
            lax.psum_scatter(
                spread[2].astype(jnp.bfloat16), "mlp", scatter_dimension=1, tiled=True
            ).astype(jnp.float32),
            lax.psum_scatter(
                spread[3].astype(jnp.bfloat16), "mlp", scatter_dimension=1, tiled=True
            ).astype(jnp.float32),
        )
    )
    reduced = jax.tree.map(
        lambda part: part.astype(jnp.float32),
        lax.psum_scatter(shortened(spread), "dp", scatter_dimension=0, tiled=True),
    )
    vector_sums = lax.psum(
        (
            grad_ln1_gain,
            grad_ln1_bias,
            grad_query_bias,
            grad_value_bias,
            grad_rel_h,
            grad_rel_w,
            grad_proj_bias,
            grad_ln2_gain,
            grad_ln2_bias,
            grad_up_bias,
            grad_down_bias,
        ),
        ("dp", "mlp"),
    )
    return (
        output,
        grad_tokens,
        vector_sums[0],
        vector_sums[1],
        reduced[0],
        vector_sums[2],
        vector_sums[3],
        vector_sums[4],
        vector_sums[5],
        reduced[1],
        vector_sums[6],
        vector_sums[7],
        vector_sums[8],
        reduced[2],
        vector_sums[9],
        reduced[3],
        vector_sums[10],
    )


def solution(mesh):
    in_specs = (
        P(("dp", "mlp"), None),
        P(("dp", "mlp"), None),
        P(),
        P(),
        P(),
        P(),
        P(),
        P(),
        P(),
        P(),
        P(),
        P(),
        P(),
        P(None, "mlp"),
        P("mlp"),
        P(None, "mlp"),
        P(),
        P(("dp", "mlp"), None),
    )
    out_specs = (
        P(("dp", "mlp"), None),
        P(("dp", "mlp"), None),
        P(),
        P(),
        P("dp", "mlp"),
        P(),
        P(),
        P(),
        P(),
        P("dp", "mlp"),
        P(),
        P(),
        P(),
        P("dp", "mlp"),
        P(),
        P("dp", "mlp"),
        P(),
    )
    return jax.shard_map(
        per_device, mesh=mesh, in_specs=in_specs, out_specs=out_specs, check_vma=False
    )
```

profile of v0, /device:TPU:0, one launch (start us, length us, event | category | flops | bytes accessed | tf_op | source)
XLA Modules:
  0.0 3013.3 jit_solution(8573069239558531598)
XLA Ops:
  212.3 78.3 %fusion.51 = f32[20,12,14,14,14]{0,4,1,2,3:T(8,128)} fusion(bf16[20,14,14,12,64]{4,3,2,1,0:T(8,128)(2,1)} %reshape.272, f32[14,14,64]{2,1,0:T(8,128)} %fusion.75), kind=kOutput, calls=%fused_computation.85 | convolution fusion | flops 505774080 | bytes 8705536 | tf_op jit(solution)/shard_map/wrchd,ckd->whrck/dot_general | solution.py:53
  317.1 93.9 %fusion.48 = f32[20,12,14,14,14]{0,4,1,3,2:T(8,128)} fusion(f32[14,14,64,1,1]{2,1,4,3,0:T(8,128)} %convolution_bitcast_fusion, bf16[20,14,14,12,64]{4,3,2,1,0:T(8,128)(2,1)} %reshape.272), kind=kOutput, calls=%fused_computation.84 | convolution fusion | flops 505774080 | bytes 8705536 | tf_op jit(solution)/shard_map/wrchd,rkd->whrck/dot_general | solution.py:52
  437.6 132.3 %add.203 = f32[20,12,14,14,14,14]{5,4,3,2,1,0:T(8,128)} broadcast(f32[20,12,14,14,14]{4,3,2,1,0:T(8,128)} %copy.94), dimensions={0,1,2,3,4} | broadcast | bytes 39513600 | tf_op jit(solution)/shard_map/add | solution.py:55
  569.8 214.6 %add.204 = f32[20,12,196,196]{3,2,1,0:T(8,128)} reshape(f32[20,12,14,14,14,14]{5,4,3,2,1,0:T(8,128)} %add.203) | data formatting | bytes 73758720 | tf_op jit(solution)/shard_map/add | solution.py:55
  784.4 52.2 %copy.95 = f32[20,12,196,196]{2,3,1,0:T(8,128)} copy(f32[20,12,196,196]{3,2,1,0:T(8,128)} %add.204) | data formatting | bytes 73758720 | tf_op jit(solution)/shard_map/add | solution.py:55
  836.7 127.1 %add.206 = f32[20,12,14,14,14,14]{5,4,3,2,1,0:T(8,128)} broadcast(f32[20,12,14,14,14]{4,3,2,1,0:T(8,128)} %copy.98), dimensions={0,1,2,3,5} | broadcast | bytes 39513600 | tf_op jit(solution)/shard_map/add | solution.py:55
  963.8 214.6 %add.207 = f32[20,12,196,196]{3,2,1,0:T(8,128)} reshape(f32[20,12,14,14,14,14]{5,4,3,2,1,0:T(8,128)} %add.206) | data formatting | bytes 73758720 | tf_op jit(solution)/shard_map/add | solution.py:55
  1178.4 52.2 %copy.99 = f32[20,12,196,196]{2,3,1,0:T(8,128)} copy(f32[20,12,196,196]{3,2,1,0:T(8,128)} %add.207) | data formatting | bytes 73758720 | tf_op jit(solution)/shard_map/add | solution.py:55
  1230.5 55.0 %fusion.98 = (f32[20,12,196]{2,1,0:T(8,128)}, f32[20,12,196,196]{2,3,1,0:T(8,128)}) fusion(f32[20,12,196,196]{2,3,1,0:T(8,128)} %copy.99, f32[20,12,196,196]{2,3,1,0:T(8,128)} %copy.95, bf16[20,196,12,64]{1,3,2,0:T(8,128)(2,1)} %copy.90, bf16[20,196,12,64]{1,3,2,0:T(8,128)(2,1)} %copy.91, pred[20,196]{1,0:T(8,128)(4,1)S(1)} %copy-done.18), kind=kOutput, calls=%fused_computation.144 | convolution fusion | flops 1226191616 | bytes 122872400 | tf_op jit(solution)/shard_map/wqhd,wkhd->whqk/dot_general | solution.py:49
  1376.0 125.7 %multiply_convert_fusion = (bf16[3920,3072]{1,0:T(8,128)(2,1)}, f32[3920,3072]{1,0:T(8,128)}, f32[3920,3072]{1,0:T(8,128)}) fusion(f32[3072]{0:T(1024)} %bitcast.106, bf16[768,3072]{1,0:T(8,128)(2,1)} %all-gather.4.cloned.1.call-done, f32[3920,768]{1,0:T(8,128)} %copy-done.1, f32[768]{0:T(1024)} %param.30, f32[768]{0:T(1024)} %param.29, f32[3920]{0:T(1024)} %fusion.83, ...), kind=kOutput, calls=%fused_computation.12 | convolution fusion | flops 19306721280 | bytes 137233024 | tf_op jit(solution)/shard_map/dot_general | solution.py:124
  1501.7 50.6 %convert_reduce_fusion = (f32[3072]{0:T(1024)}, bf16[3920,3072]{1,0:T(8,128)(2,1)}) fusion(f32[3920,3072]{1,0:T(8,128)} %get-tuple-element.40, bf16[768,3072]{1,0:T(8,128)(2,1)} %all-gather.6.cloned.1.call-done, bf16[3920,768]{1,0:T(8,128)(2,1)} %param.35, f32[3920]{0:T(1024)} %reshape.277, f32[3920,3072]{1,0:T(8,128)} %get-tuple-element.52, f32[3072]{0:T(1024)} %bitcast.107), kind=kOutput, calls=%fused_computation.10 | convolution fusion | flops 18710626304 | bytes 131202368 | tf_op jit(solution)/shard_map/dot_general | solution.py:135
  1552.3 32.0 %multiply_reduce_fusion.1 = (f32[768]{0:T(1024)}, f32[3920]{0:T(1024)S(1)}, f32[768]{0:T(1024)}, f32[3920,768]{1,0:T(8,128)}) fusion(f32[3920,768]{1,0:T(8,128)} %copy-done.1, f32[3920]{0:T(1024)} %fusion.83, f32[3920]{0:T(1024)S(1)} %broadcast_multiply_fusion, f32[768]{0:T(1024)} %param.29, bf16[3920,3072]{1,0:T(8,128)(2,1)} %get-tuple-element.60, ...), kind=kOutput, calls=%fused_computation.74 | convolution fusion | flops 18520961024 | bytes 52943808 | tf_op jit(solution)/shard_map/dot_general | solution.py:145
  1686.5 61.6 %select_convert_fusion = bf16[20,12,196,196]{2,3,1,0:T(8,128)(2,1)} fusion(f32[20,12,196,196]{2,3,1,0:T(8,128)} %get-tuple-element.49, f32[20,12,196]{2,1,0:T(8,128)} %log_add_fusion, pred[20,196]{1,0:T(8,128)(4,1)S(1)} %copy-done.19, bf16[20,196,12,64]{1,3,2,0:T(8,128)(2,1)} %copy.104, bf16[20,196,12,64]{1,3,2,0:T(8,128)(2,1)} %copy.100), kind=kOutput, calls=%fused_computation.2 | convolution fusion | flops 2424865280 | bytes 67553360 | tf_op jit(solution)/shard_map/sub | solution.py:168
  1765.3 36.9 %copy.108 = f32[20,12,196,196]{3,2,1,0:T(8,128)} copy(bf16[20,12,196,196]{2,3,1,0:T(8,128)(2,1)} %select_convert_fusion) | data formatting | bytes 55319040 | tf_op jit(solution)/shard_map/reshape | solution.py:184
  1802.2 204.9 %reshape.279 = f32[20,12,14,14,14,14]{5,4,3,2,1,0:T(8,128)} reshape(f32[20,12,196,196]{3,2,1,0:T(8,128)} %copy.108) | data formatting | bytes 73758720 | tf_op jit(solution)/shard_map/reshape | solution.py:184
  2007.1 126.5 %reduce_sum.234 = f32[20,12,14,14,14]{4,3,2,1,0:T(8,128)} reduce(f32[20,12,14,14,14,14]{5,4,3,2,1,0:T(8,128)} %reshape.279, f32[]{:T(128)} %constant.46.clone.1), dimensions={4}, to_apply=%region_10.11 | reduce | flops 8561280 | bytes 39513604 | tf_op jit(solution)/shard_map/reduce_sum | solution.py:186
  2133.6 126.3 %reduce_sum.233 = f32[20,12,14,14,14]{4,3,2,1,0:T(8,128)} reduce(f32[20,12,14,14,14,14]{5,4,3,2,1,0:T(8,128)} %reshape.279, f32[]{:T(128)} %constant.46.clone.1), dimensions={5}, to_apply=%region_9.10 | reduce | flops 8561280 | bytes 39513604 | tf_op jit(solution)/shard_map/reduce_sum | solution.py:185
  2315.4 45.5 %fusion.16 = f32[14,64,20,12,14]{1,2,4,3,0:T(8,128)} fusion(f32[14,14,64,1,1]{2,1,4,3,0:T(8,128)} %convolution_bitcast_fusion, f32[20,12,14,14,14]{4,3,2,1,0:T(8,128)} %reduce_sum.233), kind=kOutput, calls=%fused_computation.33 | convolution fusion | flops 505774080 | bytes 14726656 | tf_op jit(solution)/shard_map/whrck,rkd->wrchd/dot_general | solution.py:187
  2360.9 47.1 %bitcast_add_fusion = f32[20,14,14,12,64]{4,0,2,3,1:T(8,128)} fusion(f32[14,64,20,12,14]{1,2,4,3,0:T(8,128)} %fusion.16, f32[20,12,14,14,14]{4,3,2,1,0:T(8,128)} %reduce_sum.234, f32[14,14,64]{2,1,0:T(8,128)S(1)} %copy-done.5), kind=kOutput, calls=%fused_computation.30 | convolution fusion | flops 508784640 | bytes 26768896 | tf_op jit(solution)/shard_map/whrck,ckd->wrchd/dot_general | solution.py:189
  2602.6 32.2 %convolution_convert_fusion.2 = bf16[768,3072]{1,0:T(8,128)(2,1)} fusion(bf16[3920,3072]{1,0:T(8,128)(2,1)} %get-tuple-element.60, f32[3920,768]{1,0:T(8,128)} %copy-done.1, f32[768]{0:T(1024)} %param.30, f32[768]{0:T(1024)} %param.29, f32[3920]{0:T(1024)} %fusion.83, f32[3920]{0:T(1024)} %copy-done.10), kind=kOutput, calls=%fused_computation.92 | convolution fusion | flops 18514292736 | bytes 40882816 | tf_op jit(solution)/shard_map/dot_general | solution.py:141
  2634.8 52.0 %fusion.66 = f32[14,14,64]{2,1,0:T(8,128)} fusion(bf16[20,14,14,12,64]{4,3,2,1,0:T(8,128)(2,1)} %reshape.272, f32[20,12,14,14,14]{4,3,2,1,0:T(8,128)} %reduce_sum.234), kind=kOutput, calls=%fused_computation.97 | convolution fusion | flops 505774080 | bytes 8705536 | tf_op jit(solution)/shard_map/whrck,wrchd->ckd/dot_general | solution.py:192
  2769.2 43.8 %all-reduce = (f32[768]{0:T(1024)}, f32[768]{0:T(1024)}, f32[768]{0:T(1024)}, f32[768]{0:T(1024)}, f32[27,64]{1,0:T(8,128)}, /*index=5*/f32[27,64]{1,0:T(8,128)}...) all-reduce(f32[768]{0:T(1024)} %get-tuple-element.19, ...), channel_id=1, replica_groups=mesh['dp'=16,'mlp'=2] {'dp','mlp'}, use_global_device_ids=true, to_apply=%region_14.15 | all-reduce | flops 12672 | bytes 101376 | tf_op jit(solution)/shard_map/psum | solution.py:234
  2874.4 64.6 %reduce-scatter.23.cloned.1.call-done = bf16[48,1536]{1,0:T(8,128)(2,1)} async-done(((bf16[768,1536]{1,0:T(8,128)(2,1)}), bf16[48,1536]{1,0:T(8,128)(2,1)}) %reduce-scatter.23.cloned.1.call-update) | async-done | bytes 147472 | tf_op jit(solution)/shard_map/reduce_scatter | solution.py:232
  2940.6 64.0 %reduce-scatter.19.cloned.1.call-done = bf16[48,1536]{1,0:T(8,128)(2,1)} async-done(((bf16[768,1536]{1,0:T(8,128)(2,1)}), bf16[48,1536]{1,0:T(8,128)(2,1)}) %reduce-scatter.19.cloned.1.call-update) | async-done | bytes 147472 | tf_op jit(solution)/shard_map/reduce_scatter | solution.py:232
  (170 shorter events, 864.9 us)
Async XLA Ops:
  7.2 1368.7 %all-gather.4.cloned.1.call-start = ((), (), s32[]{:S(2)}) async-start(), calls=%async_computation.8 | async-start | bytes 7077888 | tf_op jit(solution)/shard_map/all_gather | solution.py:118
  8.0 1493.7 %all-gather.6.cloned.1.call-start = ((), (), s32[]{:S(2)}) async-start(), calls=%async_computation.9 | async-start | bytes 7077888 | tf_op jit(solution)/shard_map/all_gather | solution.py:119
  8.7 2678.2 %reduce-scatter.27.cloned.1.call-start = ((), (), s32[]{:S(2)}) async-start(), calls=%async_computation.17 | async-start | bytes 1769472
  9.3 102.1 %copy-start.16 = (s32[14,14]{0,1:T(8,128)}, s32[14,14]{0,1:T(8,128)S(1)}, u32[]{:S(2)}) copy-start(s32[14,14]{0,1:T(8,128)S(1)} %subtract_add_fusion) | copy-start | bytes 2356
  12.9 29.6 copy-start.7
  18.1 24.4 copy-start.9
  82.7 19.9 copy-start.21
  1178.4 52.2 %copy-start.18 = (pred[20,196]{1,0:T(8,128)(4,1)S(1)}, pred[20,196]{1,0:T(8,128)(4,1)}, u32[]{:S(2)}) copy-start(pred[20,196]{1,0:T(8,128)(4,1)} %get-tuple-element.45) | copy-start | bytes 11764
  1285.5 21.0 copy-start.4
  1369.0 215.3 %copy-start.10 = (f32[3920]{0:T(1024)}, f32[3920]{0:T(1024)S(1)}, u32[]{:S(2)}) copy-start(f32[3920]{0:T(1024)S(1)} %broadcast_multiply_fusion) | copy-start | bytes 47044
  1552.3 32.0 %copy-start.13 = (f32[3920]{0:T(1024)S(1)}, f32[3920]{0:T(1024)}, u32[]{:S(2)}) copy-start(f32[3920]{0:T(1024)} %copy-done.12) | copy-start | bytes 47044
  1552.3 32.0 %copy-start.17 = (f32[3920]{0:T(1024)S(1)}, f32[3920]{0:T(1024)}, u32[]{:S(2)}) copy-start(f32[3920]{0:T(1024)} %fusion.83) | copy-start | bytes 47044
  1552.3 32.0 %copy-start.24 = (f32[768]{0:T(1024)S(1)}, f32[768]{0:T(1024)}, u32[]{:S(2)}) copy-start(f32[768]{0:T(1024)} %param.29) | copy-start | bytes 9220
  1584.3 14.5 copy-start.2
  1584.3 14.5 copy-start.14
  1657.8 28.7 copy-start.19
  2262.3 463.9 %reduce-scatter.25.cloned.1.call-start = ((), (), s32[]{:S(2)}) async-start(), calls=%async_computation.16 | async-start | bytes 5308416
  2315.4 45.5 %copy-start.5 = (f32[14,14,64]{2,1,0:T(8,128)S(1)}, f32[14,14,64]{2,1,0:T(8,128)}, u32[]{:S(2)}) copy-start(f32[14,14,64]{2,1,0:T(8,128)} %fusion.75) | copy-start | bytes 150532
  2575.4 181.6 %reduce-scatter.21.cloned.1.call-start = ((), (), s32[]{:S(2)}) async-start(), calls=%async_computation.14 | async-start | bytes 7077888 | tf_op jit(solution)/shard_map/reduce_scatter | solution.py:225
  2602.5 227.6 %reduce-scatter.17.cloned.1.call-start = ((), (), s32[]{:S(2)}) async-start(), calls=%async_computation.12 | async-start | bytes 7077888 | tf_op jit(solution)/shard_map/reduce_scatter | solution.py:222
  2634.8 222.5 %reduce-scatter.15.cloned.1.call-start = ((), (), s32[]{:S(2)}) async-start(), calls=%async_computation.11 | async-start | bytes 626688 | tf_op jit(solution)/shard_map/reduce_scatter | solution.py:232
  2689.1 183.6 %reduce-scatter.13.cloned.1.call-start = ((), (), s32[]{:S(2)}) async-start(), calls=%async_computation.10 | async-start | bytes 1880064 | tf_op jit(solution)/shard_map/reduce_scatter | solution.py:232
  2730.1 208.8 %reduce-scatter.23.cloned.1.call-start = ((), (), s32[]{:S(2)}) async-start(), calls=%async_computation.15 | async-start | bytes 2506752 | tf_op jit(solution)/shard_map/reduce_scatter | solution.py:232
  2757.0 247.5 %reduce-scatter.19.cloned.1.call-start = ((), (), s32[]{:S(2)}) async-start(), calls=%async_computation.13 | async-start | bytes 2506752 | tf_op jit(solution)/shard_map/reduce_scatter | solution.py:232
  (16 other events, 115.4 us)
Sparse Core Ops, SparseCore 0:
  9.6 65.3 all-gather.3
  76.5 62.8 all-gather.5
  2262.4 23.5 reduce-scatter.26
  2575.5 49.4 reduce-scatter.24
  2627.7 59.9 reduce-scatter.20
  2690.6 59.9 reduce-scatter.16
  2754.2 54.9 reduce-scatter.14
  2813.5 59.2 reduce-scatter.12
  2877.0 61.9 reduce-scatter.22
  2942.6 61.9 reduce-scatter.18
where the time goes:
time: 3040 us; the launch traced here: 3010 us
  local copies, waits for them, and re-layouts  1490 us (49%)
  matrix products  957 us (31%)
  other arithmetic  359 us (12%)
  waiting for transfers between devices  144 us (5%)
  blocking collectives  49.2 us (2%)
    add x6, local copies, waits for them, and re-layouts, attention_scores(): scores.reshape(window_count, HEADS, WIN, WIN, WIN, WIN)  793 us
    reshape x2, local copies, waits for them, and re-layouts, per_device(): grad_scores_low.astype(jnp.float32)  242 us
    reduce_scatter x4, waiting for transfers between devices, per_device(): lax.psum_scatter(shortened(spread), 'dp', scatter_dimension=0, tiled=True)  143 us
    reduce_sum x1, other arithmetic, per_device(): grad_along_w = jnp.sum(grad_grid, axis=4)  126 us
    reduce_sum x1, other arithmetic, per_device(): grad_along_h = jnp.sum(grad_grid, axis=5)  126 us
    dot_general x1, matrix products, per_device(): jnp.dot(mlp_input, up_full, preferred_element_type=jnp.float32)  126 us
    dot_general x1, matrix products, attention_scores(): jnp.einsum('wrchd,rkd->whrck', queries_grid, table_h, precision=HIGHEST)  93.9 us
    dot_general x1, matrix products, attention_scores(): jnp.einsum('wrchd,ckd->whrck', queries_grid, table_w, precision=HIGHEST)  78.3 us
  transfers between devices with their start and end apart: 10, of which 3 were waited for; matrix products, arithmetic and copies ran while one was open for 68% of the time, Pallas kernels for 0%

commit v1 on v0

v1 whole, which is shorter than its diff:
```python
import functools
import jax
import jax.numpy as jnp
from jax import lax
from jax.experimental import pallas as pl
from jax.experimental.pallas import tpu as pltpu
from jax.sharding import PartitionSpec as P

HEADS = 12
HEAD_DIM = 64
WIN = 14
AREA = WIN * WIN
PADDED = 208
PAIRS = HEADS // 2
MODEL = HEADS * HEAD_DIM
EPSILON = 1e-6
NEGATIVE = -1e30
SCALE = HEAD_DIM ** -0.5
F32 = jnp.float32
BF16 = jnp.bfloat16
NN = (((1,), (0,)), ((), ()))
NT = (((1,), (1,)), ((), ()))
TN = (((0,), (0,)), ((), ()))
VMEM_LIMIT = 60 * 1024 * 1024


def mm(a, b, dims=NN):
    return lax.dot_general(a, b, dims, preferred_element_type=F32)


def fold8(v):
    return jnp.sum(v.reshape(v.shape[0] // 8, 8, v.shape[1]), axis=0)


def norm(v):
    mu = jnp.mean(v, axis=-1, keepdims=True)
    c = v - mu
    return c, lax.rsqrt(jnp.mean(c * c, axis=-1, keepdims=True) + EPSILON)


def eye(n, value=1.0):
    r = lax.broadcasted_iota(jnp.int32, (n, n), 0)
    c = lax.broadcasted_iota(jnp.int32, (n, n), 1)
    return jnp.where(r == c, value, 0.0).astype(BF16)


def skew_bits(which):
    lane = lax.broadcasted_iota(jnp.int32, (1, PADDED), 1)
    r = lane // WIN
    return WIN - 1 - (jnp.minimum(r, WIN - 1) if which == 0 else lane - r * WIN)


def split(v):
    hi = v.astype(BF16)
    return hi, (v - hi.astype(F32)).astype(BF16)


def key_side(k, ohm):
    return jnp.concatenate([k, ohm], axis=1)


def query_side(qa, h):
    z = jnp.zeros((HEAD_DIM, PADDED), BF16)
    own = qa[h * 64:(h + 1) * 64]
    bias = qa[128 + 64 * h:192 + 64 * h]
    return jnp.concatenate(([own, z] if h == 0 else [z, own]) + [bias, z], axis=0)


def forward_kernel(x_ref, ohm_ref, gain_ref, bias_ref, wqkv_ref, qkvb_ref, mix_ref, shift_ref, wproj_ref, projb_ref,
                   x1_ref, h1_ref, qkv_ref, qaug_ref, o_ref, lse_ref, wide):
    wb = ohm_ref.shape[0]
    for w in range(wb):
        x = x_ref[AREA * w:AREA * (w + 1), :].astype(F32)
        c, r = norm(x)
        h1_ref[w, PADDED - 16:, :] = jnp.zeros((16, MODEL), BF16)
        h1_ref[w, 0:AREA, :] = (c * r * gain_ref[...] + bias_ref[...]).astype(BF16)

    @pl.loop(0, 3)
    def _(j):
        cs = pl.ds(pl.multiple_of(j * MODEL, MODEL), MODEL)
        p = mm(h1_ref[...].reshape(wb * PADDED, MODEL), wqkv_ref[:, cs]) + qkvb_ref[:, cs]
        qkv_ref[:, :, cs] = p.astype(BF16).reshape(wb, PADDED, MODEL)

    @pl.loop(0, wb * PAIRS)
    def _(it):
        w = it // PAIRS
        pair = it - w * PAIRS
        lanes = lambda part: pl.ds(pl.multiple_of(part * MODEL + pair * 128, 128), 128)
        q = qkv_ref[w, :, lanes(0)]
        k = qkv_ref[w, :, lanes(1)]
        v = qkv_ref[w, :, lanes(2)]
        u = mm(mix_ref[...], jnp.concatenate([q, q], axis=1), NT)
        vt = mm(eye(128), v, NT).astype(BF16)
        tabs = []
        for t in range(2):
            a = u[64 * t:64 * t + 64]
            for n, b in enumerate((8, 4, 2, 1)):
                cond = shift_ref[4 * t + n:4 * t + n + 1, :] > 0
                a = jnp.where(cond, pltpu.roll(a, 64 - b, 0), a)
            tabs.append(a)
        row = lax.broadcasted_iota(jnp.int32, (16, 1), 0)
        parts = [u[128:256].astype(BF16)]
        for h in range(2):
            ah = jnp.where(row == 14, 1.0, tabs[0][32 * h:32 * h + 16])
            aw = tabs[1][32 * h:32 * h + 16]
            hh, hl = split(ah)
            wh, wl = split(aw)
            parts += [hh, wh, hl, wl]
        qa = jnp.concatenate(parts, axis=0)
        qaug_ref[w, pair] = qa
        keys = key_side(k, ohm_ref[w])
        outs = []
        for h in range(2):
            s = mm(keys, query_side(qa, h))
            top = jnp.max(s, axis=0, keepdims=True)
            e = jnp.exp(s - top)
            total = jnp.sum(e, axis=0, keepdims=True)
            lse_ref[w, pair, h:h + 1, :] = top + jnp.log(total)
            outs.append(mm(vt[64 * h:64 * h + 64], e.astype(BF16)) * (1.0 / total))
        ot = jnp.concatenate(outs, axis=0).astype(BF16)
        o_ref[w, :, lanes(0)] = mm(eye(PADDED), ot, NT).astype(BF16)

    wide[...] = mm(o_ref[...].reshape(wb * PADDED, MODEL), wproj_ref[...]) + projb_ref[...]
    for w in range(wb):
        x1_ref[AREA * w:AREA * (w + 1), :] = x_ref[AREA * w:AREA * (w + 1), :].astype(F32) + wide[PADDED * w:PADDED * w + AREA, :]


def once(a):
    return pl.BlockSpec(a.shape, lambda i: (0,) * a.ndim, pipeline_mode=pl.Buffered(1))


def blocked(*shape):
    return pl.BlockSpec(shape, lambda i: (i,) + (0,) * (len(shape) - 1))


def block_windows(windows):
    return 4 if windows % 4 == 0 else windows


def attention_forward(x, ohm, gain, bias, wqkv, qkvb, mix, shift, wproj, projb):
    windows = ohm.shape[0]
    wb = block_windows(windows)
    outs = [((windows * AREA, MODEL), F32, (wb * AREA, MODEL)),
            ((windows, PADDED, MODEL), BF16, (wb, PADDED, MODEL)),
            ((windows, PADDED, 3 * MODEL), BF16, (wb, PADDED, 3 * MODEL)),
            ((windows, PAIRS, 256, PADDED), BF16, (wb, PAIRS, 256, PADDED)),
            ((windows, PADDED, MODEL), BF16, (wb, PADDED, MODEL)),
            ((windows, PAIRS, 2, PADDED), F32, (wb, PAIRS, 2, PADDED))]
    return pl.pallas_call(
        forward_kernel,
        grid=(windows // wb,),
        in_specs=[blocked(wb * AREA, MODEL), blocked(wb, PADDED, 128)] + [once(a) for a in (gain, bias, wqkv, qkvb, mix, shift, wproj, projb)],
        out_specs=[blocked(*b) for _, _, b in outs],
        out_shape=[jax.ShapeDtypeStruct(s, t) for s, t, _ in outs],
        scratch_shapes=[pltpu.VMEM((wb * PADDED, MODEL), F32)],
        compiler_params=pltpu.CompilerParams(vmem_limit_bytes=VMEM_LIMIT, dimension_semantics=("arbitrary",)),
        name="attention_forward",
    )(x, ohm, gain, bias, wqkv, qkvb, mix, shift, wproj, projb)


def backward_kernel(da_ref, ohm_ref, oht_ref, qkv_ref, qaug_ref, lse_ref, wproj_ref, relt_ref, shift_ref,
                    dap_ref, dp_ref, grel_ref, vec_ref, dos):
    wb = ohm_ref.shape[0]

    @pl.when(pl.program_id(0) == 0)
    def _():
        grel_ref[...] = jnp.zeros_like(grel_ref)
        vec_ref[...] = jnp.zeros_like(vec_ref)

    for w in range(wb):
        dap_ref[w, PADDED - 16:, :] = jnp.zeros((16, MODEL), BF16)
        dap_ref[w, 0:AREA, :] = da_ref[AREA * w:AREA * (w + 1), :]
    dos[...] = mm(dap_ref[...].reshape(wb * PADDED, MODEL), wproj_ref[...], NT).astype(BF16).reshape(wb, PADDED, MODEL)

    @pl.loop(0, wb * PAIRS)
    def _(it):
        w = it // PAIRS
        pair = it - w * PAIRS
        lanes = lambda part: pl.ds(pl.multiple_of(part * MODEL + pair * 128, 128), 128)
        q = qkv_ref[w, :, lanes(0)]
        k = qkv_ref[w, :, lanes(1)]
        v = qkv_ref[w, :, lanes(2)]
        do = dos[w, :, lanes(0)]
        qa = qaug_ref[w, pair]
        kt = mm(eye(128, SCALE), k, NT).astype(BF16)
        dot = mm(eye(128), do, NT).astype(BF16)
        keys = key_side(k, ohm_ref[w])
        z = jnp.zeros((HEAD_DIM, PADDED), BF16)
        dvs, dks, dqs = [], [], []
        for h in range(2):
            s = mm(keys, query_side(qa, h))
            a = jnp.exp(s - lse_ref[w, pair, h:h + 1, :])
            own = dot[64 * h:64 * h + 64]
            dw = mm(v, jnp.concatenate([own, z] if h == 0 else [z, own], axis=0))
            t = a * dw
            ds = t - a * jnp.sum(t, axis=0, keepdims=True)
            dsb = ds.astype(BF16)
            dvs.append(mm(a.astype(BF16), do))
            dks.append(mm(dsb, q))
            dqs.append(mm(jnp.concatenate([kt[64 * h:64 * h + 64], oht_ref[...]], axis=0), dsb))
        first = lax.broadcasted_iota(jnp.int32, (1, 128), 1) < 64
        dk = (jnp.where(first, dks[0], dks[1]) * SCALE).astype(BF16)
        dv = jnp.where(first, dvs[0], dvs[1]).astype(BF16)
        zz = jnp.zeros((16, PADDED), F32)
        tabs = []
        for t in range(2):
            lo = 64 + 16 * t
            a = jnp.concatenate([dqs[0][lo:lo + 16], zz, dqs[1][lo:lo + 16], zz], axis=0)
            for n, b in enumerate((8, 4, 2, 1)):
                cond = shift_ref[4 * t + n:4 * t + n + 1, :] > 0
                a = jnp.where(cond, pltpu.roll(a, b, 0), a)
            tabs.append(a.astype(BF16))
        dqt = []
        for h in range(2):
            du = jnp.concatenate([tabs[0][32 * h:32 * h + 32], tabs[1][32 * h:32 * h + 32]], axis=0)
            dqt.append(dqs[h][0:64] + mm(relt_ref[...], jnp.concatenate([du, du], axis=0)))
            grel_ref[h] += mm(du, q)
        dq = mm(eye(PADDED), jnp.concatenate(dqt, axis=0).astype(BF16), NT).astype(BF16)
        dp_ref[w, :, lanes(0)] = dq
        dp_ref[w, :, lanes(1)] = dk
        dp_ref[w, :, lanes(2)] = dv
        vec_ref[0:8, lanes(0)] += fold8(dq.astype(F32))
        vec_ref[8:16, lanes(0)] += fold8(dv.astype(F32))


def attention_backward(da, ohm, oht, qkv, qaug, lse, wproj, relt, shift):
    windows = ohm.shape[0]
    wb = block_windows(windows)
    return pl.pallas_call(
        backward_kernel,
        grid=(windows // wb,),
        in_specs=[blocked(wb * AREA, MODEL), blocked(wb, PADDED, 128), once(oht), blocked(wb, PADDED, 3 * MODEL),
                  blocked(wb, PAIRS, 256, PADDED), blocked(wb, PAIRS, 2, PADDED), once(wproj), once(relt), once(shift)],
        out_specs=[blocked(wb, PADDED, MODEL), blocked(wb, PADDED, 3 * MODEL),
                   pl.BlockSpec((2, 64, 128), lambda i: (0, 0, 0)), pl.BlockSpec((16, MODEL), lambda i: (0, 0))],
        out_shape=[jax.ShapeDtypeStruct((windows, PADDED, MODEL), BF16), jax.ShapeDtypeStruct((windows, PADDED, 3 * MODEL), BF16),
                   jax.ShapeDtypeStruct((2, 64, 128), F32), jax.ShapeDtypeStruct((16, MODEL), F32)],
        scratch_shapes=[pltpu.VMEM((wb, PADDED, MODEL), BF16)],
        compiler_params=pltpu.CompilerParams(vmem_limit_bytes=VMEM_LIMIT, dimension_semantics=("arbitrary",)),
        name="attention_backward",
    )(da, ohm, oht, qkv, qaug, lse, wproj, relt, shift)


def input_kernel(x_ref, da_ref, dp_ref, gain_ref, wqkv_ref, gx_ref, vec_ref, wide, tall):
    wb = dp_ref.shape[0]

    @pl.when(pl.program_id(0) == 0)
    def _():
        vec_ref[...] = jnp.zeros_like(vec_ref)

    wide[...] = mm(dp_ref[...].reshape(wb * PADDED, 3 * MODEL), wqkv_ref[...], NT)
    for w in range(wb):
        tall[AREA * w:AREA * (w + 1), :] = wide[PADDED * w:PADDED * w + AREA, :]
    rows = wb * AREA
    for lo in range(0, rows, 112):
        hi = min(lo + 112, rows)
        c, r = norm(x_ref[lo:hi, :].astype(F32))
        xhat = c * r
        dh = tall[lo:hi, :]
        pad = -(hi - lo) % 8
        both = jnp.concatenate([dh, jnp.zeros((pad, MODEL), F32)], axis=0) if pad else dh
        prod = dh * xhat
        bothx = jnp.concatenate([prod, jnp.zeros((pad, MODEL), F32)], axis=0) if pad else prod
        vec_ref[0:8, :] += fold8(bothx)
        vec_ref[8:16, :] += fold8(both)
        dx = dh * gain_ref[...]
        dx = r * (dx - jnp.mean(dx, axis=-1, keepdims=True) - xhat * jnp.mean(dx * xhat, axis=-1, keepdims=True))
        gx_ref[lo:hi, :] = (dx + da_ref[lo:hi, :].astype(F32)).astype(BF16)


def input_gradient(x, da, dp, gain, wqkv):
    windows = dp.shape[0]
    wb = block_windows(windows)
    return pl.pallas_call(
        input_kernel,
        grid=(windows // wb,),
        in_specs=[blocked(wb * AREA, MODEL), blocked(wb * AREA, MODEL), blocked(wb, PADDED, 3 * MODEL), once(gain), once(wqkv)],
        out_specs=[blocked(wb * AREA, MODEL), pl.BlockSpec((16, MODEL), lambda i: (0, 0))],
        out_shape=[jax.ShapeDtypeStruct((windows * AREA, MODEL), BF16), jax.ShapeDtypeStruct((16, MODEL), F32)],
        scratch_shapes=[pltpu.VMEM((wb * PADDED, MODEL), F32), pltpu.VMEM((wb * AREA, MODEL), F32)],
        compiler_params=pltpu.CompilerParams(vmem_limit_bytes=VMEM_LIMIT, dimension_semantics=("arbitrary",)),
        name="input_gradient",
    )(x, da, dp, gain, wqkv)


def small_tables(window_extent, rel_h, rel_w):
    place = jnp.arange(PADDED)
    r, c = place // WIN, place % WIN
    real = place < AREA
    hot_r = ((r[:, None] == jnp.arange(16)) & real[:, None]).astype(F32)
    hot_c = ((c[:, None] == jnp.arange(16)) & real[:, None]).astype(F32)
    valid = (r < window_extent[:, 0:1]) & (c < window_extent[:, 1:2]) & real
    first = jnp.where((jnp.arange(16) == 14)[None, None, :], jnp.where(valid, 0.0, NEGATIVE)[:, :, None], hot_r[None])
    rest = jnp.concatenate([hot_c, hot_r, hot_c, jnp.zeros((PADDED, 64), F32)], axis=1)
    rest = jnp.broadcast_to(rest[None], (valid.shape[0],) + rest.shape)
    ohm = jnp.concatenate([first, rest], axis=2).astype(BF16)
    oht = jnp.concatenate([hot_r, hot_c], axis=1).T.astype(BF16)
    sh = WIN - 1 - jnp.minimum(r, WIN - 1)
    sw = WIN - 1 - c
    shift = jnp.stack([jnp.where(real, (s >> b) & 1, 0) for s in (sh, sw) for b in (3, 2, 1, 0)]).astype(jnp.int32)
    flip = lambda t: jnp.concatenate([t[::-1], jnp.zeros((5, HEAD_DIM), F32)], axis=0)
    fh, fw = flip(rel_h), flip(rel_w)

    def hi_lo(v):
        hi = v.astype(BF16).astype(F32)
        return hi, v - hi

    def rows(th, tw):
        z = jnp.zeros((32, HEAD_DIM), F32)
        return jnp.concatenate([jnp.concatenate([th, z], 1), jnp.concatenate([z, th], 1),
                                jnp.concatenate([tw, z], 1), jnp.concatenate([z, tw], 1)], axis=0)
    (hh, hl), (wh, wl) = hi_lo(fh), hi_lo(fw)
    mix = jnp.concatenate([rows(hh, wh), rows(hl, wl)], axis=1)
    ident = jnp.concatenate([SCALE * jnp.eye(128, dtype=F32), jnp.zeros((128, 128), F32)], axis=1)
    mix = jnp.concatenate([mix, ident], axis=0).astype(BF16)
    relt = jnp.concatenate([hh, wh, hl, wl], axis=0).T.astype(BF16)
    valid_rows = valid[:, :AREA].reshape(-1, 1).astype(F32)
    return ohm, oht, shift, mix, relt, valid_rows


def gelu_parts(z):
    u = jnp.abs(z)
    t = 1.0 / (1.0 + 0.23164189 * u)
    e = jnp.exp(-0.5 * z * z)
    poly = t * (0.127414796 + t * (-0.142248368 + t * (0.7107068705 + t * (-0.7265760135 + t * 0.5307027145))))
    q = poly * e
    phi = jnp.where(z >= 0.0, 1.0 - q, q)
    return z * phi, phi + z * e * 0.3989422804


def mlp_kernel(rows, x1_ref, go_ref, mask_ref, gain_ref, bias_ref, up_ref, upb_ref, down_ref, downb_ref,
               out_ref, da_ref, dwu_ref, dwd_ref, dbu_ref, vec_ref,
               h2, dm, h2t, dmt, macc, dacc, accu, accd, stage, sems):
    rb = h2.shape[0]
    ff = up_ref.shape[1]
    hc = 1024
    ch = 256
    step = pl.program_id(0)

    @pl.when(step == 0)
    def _():
        accu[...] = jnp.zeros_like(accu)
        accd[...] = jnp.zeros_like(accd)
        dbu_ref[...] = jnp.zeros_like(dbu_ref)
        vec_ref[...] = jnp.zeros_like(vec_ref)

    def live(i):
        row = step * rb + i * ch + lax.broadcasted_iota(jnp.int32, (ch, 1), 0)
        return row < rows

    @pl.loop(0, rb // ch)
    def _(i):
        rs = pl.ds(pl.multiple_of(i * ch, ch), ch)
        x1 = jnp.where(live(i), x1_ref[rs, :], 0.0)
        c, r = norm(x1)
        h2[rs, :] = (c * r * gain_ref[...] + bias_ref[...]).astype(BF16)
        d = jnp.where(live(i) & (mask_ref[rs, :] > 0.0), go_ref[rs, :].astype(F32), 0.0)
        dm[rs, :] = d.astype(BF16)
        vec_ref[0:8, :] += fold8(d)

    h2t[...] = h2[...].T
    dmt[...] = dm[...].T
    macc[...] = jnp.zeros_like(macc)
    dacc[...] = jnp.zeros_like(dacc)

    @pl.loop(0, ff // hc)
    def _(j):
        cs = pl.ds(pl.multiple_of(j * hc, hc), hc)
        z = mm(h2[...], up_ref[:, cs]) + upb_ref[:, cs]
        dact = mm(dm[...], down_ref[:, cs])
        g, gp = gelu_parts(z)
        g = g.astype(BF16)
        dz = dact * gp
        dzb = dz.astype(BF16)
        dbu_ref[:, cs] += fold8(dzb.astype(F32))
        macc[...] += mm(g, down_ref[:, cs], NT)
        dacc[...] += mm(dzb, up_ref[:, cs], NT)
        accd[:, cs] += mm(dmt[...], g)
        accu[:, cs] += mm(h2t[...], dzb)

    @pl.loop(0, rb // ch)
    def _(i):
        rs = pl.ds(pl.multiple_of(i * ch, ch), ch)
        x1 = jnp.where(live(i), x1_ref[rs, :], 0.0)
        c, r = norm(x1)
        xhat = c * r
        valid = live(i) & (mask_ref[rs, :] > 0.0)
        out_ref[rs, :] = jnp.where(valid, x1 + macc[rs, :] + downb_ref[...], 0.0).astype(BF16)
        dh = dacc[rs, :]
        vec_ref[8:16, :] += fold8(dh * xhat)
        vec_ref[16:24, :] += fold8(dh)
        dx = dh * gain_ref[...]
        dx = r * (dx - jnp.mean(dx, axis=-1, keepdims=True) - xhat * jnp.mean(dx * xhat, axis=-1, keepdims=True))
        da = (dx + dm[rs, :].astype(F32)).astype(BF16)
        da_ref[rs, :] = da
        vec_ref[24:32, :] += fold8(da.astype(F32))

    @pl.when(step == pl.num_programs(0) - 1)
    def _():
        def copy(k):
            src, dst = ((accu, dwu_ref), (accd, dwd_ref))[k // (ff // hc)]
            j = k % (ff // hc)
            return src, pltpu.make_async_copy(stage.at[k % 2], dst.at[:, pl.ds(j * hc, hc)], sems.at[k % 2])
        n = 2 * (ff // hc)
        for k in range(n):
            src, cp = copy(k)
            if k >= 2:
                copy(k - 2)[1].wait()
            j = k % (ff // hc)
            stage[k % 2] = src[:, j * hc:(j + 1) * hc].astype(BF16)
            cp.start()
        copy(n - 2)[1].wait()
        copy(n - 1)[1].wait()


def mlp(x1, go, mask, gain, bias, up, upb, down, downb):
    rows, d = x1.shape
    ff = up.shape[1]
    rb = 512
    steps = pl.cdiv(rows, rb)
    full = lambda a: pl.BlockSpec(a.shape, lambda i: (0, 0), pipeline_mode=pl.Buffered(1))
    rowspec = lambda w: pl.BlockSpec((rb, w), lambda i: (i, 0))
    return pl.pallas_call(
        functools.partial(mlp_kernel, rows),
        grid=(steps,),
        in_specs=[rowspec(d), rowspec(d), rowspec(1), full(gain), full(bias), full(up), full(upb), full(down), full(downb)],
        out_specs=[rowspec(d), rowspec(d), pl.BlockSpec(memory_space=pl.ANY), pl.BlockSpec(memory_space=pl.ANY),
                   pl.BlockSpec((8, ff), lambda i: (0, 0)), pl.BlockSpec((32, d), lambda i: (0, 0))],
        out_shape=[jax.ShapeDtypeStruct((rows, d), BF16), jax.ShapeDtypeStruct((rows, d), BF16),
                   jax.ShapeDtypeStruct((d, ff), BF16), jax.ShapeDtypeStruct((d, ff), BF16),
                   jax.ShapeDtypeStruct((8, ff), F32), jax.ShapeDtypeStruct((32, d), F32)],
        scratch_shapes=[pltpu.VMEM((rb, d), BF16), pltpu.VMEM((rb, d), BF16), pltpu.VMEM((d, rb), BF16), pltpu.VMEM((d, rb), BF16),
                        pltpu.VMEM((rb, d), F32), pltpu.VMEM((rb, d), F32), pltpu.VMEM((d, ff), F32), pltpu.VMEM((d, ff), F32),
                        pltpu.VMEM((2, d, 1024), BF16), pltpu.SemaphoreType.DMA((2,))],
        compiler_params=pltpu.CompilerParams(vmem_limit_bytes=60 * 1024 * 1024, dimension_semantics=("arbitrary",)),
        name="mlp",
    )(x1, go, mask, gain, bias, up, upb, down, downb)


def bits(n):
    return n.bit_length() - 1


def exchange_order(dp, mlp):
    dp_bits = list(range(bits(dp)))
    order = [("dp", b) for b in dp_bits[:1]]
    order += [("mlp", b) for b in reversed(range(bits(mlp)))]
    order += [("dp", b) for b in dp_bits[1:2]]
    order += [("dp", b) for b in reversed(dp_bits[2:])]
    return order


def halve(parts, sizes):
    dp, mlp = sizes["dp"], sizes["mlp"]
    names = [("dp", b) for b in reversed(range(bits(dp)))] + [("mlp", b) for b in reversed(range(bits(mlp)))]
    held = parts.reshape((2,) * len(names) + parts.shape[2:])
    for step in exchange_order(dp, mlp):
        axis, bit = step
        at = names.index(step)
        names.pop(at)
        mine = (lax.axis_index(axis) >> bit) & 1
        keep = lax.dynamic_index_in_dim(held, mine, at, keepdims=False)
        send = lax.dynamic_index_in_dim(held, 1 - mine, at, keepdims=False)
        n = sizes[axis]
        got = lax.ppermute(send, axis, [(i, i ^ (1 << bit)) for i in range(n)])
        held = (keep.astype(F32) + got.astype(F32)).astype(BF16)
    return held


def by_owner(grad, dp, mlp):
    rows, cols = grad.shape
    return grad.reshape(dp, rows // dp, mlp, cols // mlp).transpose(0, 2, 1, 3)


def per_device(
    sizes,
    tokens,
    window_extent,
    ln1_gain,
    ln1_bias,
    qkv_weight,
    query_bias,
    value_bias,
    rel_h,
    rel_w,
    proj_weight,
    proj_bias,
    ln2_gain,
    ln2_bias,
    up_weight,
    up_bias,
    down_weight,
    down_bias,
    grad_out,
):
    dp, mlp_n = sizes["dp"], sizes["mlp"]
    line = lambda v: v.reshape(1, -1)
    up_full = lax.all_gather(up_weight, "mlp", axis=1, tiled=True)
    down_full = lax.all_gather(down_weight, "mlp", axis=1, tiled=True)
    up_bias_full = lax.all_gather(up_bias, "mlp", axis=0, tiled=True)
    ohm, oht, shift, mix, relt, valid_rows = small_tables(window_extent, rel_h, rel_w)
    qkv_bias = jnp.concatenate([query_bias, jnp.zeros_like(query_bias), value_bias])
    x1, h1, qkv, qaug, o, lse = attention_forward(
        tokens, ohm, line(ln1_gain), line(ln1_bias), qkv_weight, line(qkv_bias), mix, shift, proj_weight, line(proj_bias))
    output, da, dw_up, dw_down, up_sums, mid_sums = mlp(
        x1, grad_out, valid_rows, line(ln2_gain), line(ln2_bias), up_full, line(up_bias_full), down_full, line(down_bias))
    ff = dw_up.shape[1]
    both = jnp.concatenate([dw_up, dw_down], axis=1)
    both = lax.psum_scatter(both, "dp", scatter_dimension=0, tiled=True)
    both = both.reshape(-1, 2, mlp_n, ff // mlp_n).transpose(2, 1, 0, 3)
    both = lax.psum_scatter(both, "mlp", scatter_dimension=0, tiled=True)[0].astype(F32)
    dap, dp_all, grel, qv_sums = attention_backward(da, ohm, oht, qkv, qaug, lse, proj_weight, relt, shift)
    flat = lambda v: v.reshape(-1, v.shape[-1])
    dw_qkv = mm(flat(h1), flat(dp_all), TN).astype(BF16)
    dw_proj = mm(flat(o), flat(dap), TN).astype(BF16)
    late = jnp.concatenate([by_owner(dw_qkv, dp, mlp_n), by_owner(dw_proj, dp, mlp_n)], axis=3)
    late = halve(late, sizes).astype(F32)
    grad_tokens, in_sums = input_gradient(tokens, da, dp_all, line(ln1_gain), qkv_weight)
    rel = grel[0, :, :HEAD_DIM] + grel[1, :, HEAD_DIM:]
    fold = lambda v: jnp.sum(v.reshape(-1, 8, v.shape[1]), axis=1).reshape(-1)
    sums = jnp.concatenate([fold(in_sums), fold(qv_sums), rel.reshape(-1), fold(mid_sums), fold(up_sums)])
    sums = lax.psum(sums, ("dp", "mlp"))
    d = MODEL
    n_rel = 64 * HEAD_DIM
    rel = sums[4 * d:4 * d + n_rel].reshape(64, HEAD_DIM)
    mid = sums[4 * d + n_rel:]
    table = 2 * WIN - 1
    cols = dw_qkv.shape[1] // mlp_n
    return (
        output,
        grad_tokens,
        sums[0:d],
        sums[d:2 * d],
        late[:, :cols],
        sums[2 * d:3 * d],
        sums[3 * d:4 * d],
        rel[0:table][::-1],
        rel[32:32 + table][::-1],
        late[:, cols:],
        mid[3 * d:4 * d],
        mid[d:2 * d],
        mid[2 * d:3 * d],
        both[0],
        mid[4 * d:],
        both[1],
        mid[0:d],
    )


def solution(mesh):
    rows = P(("dp", "mlp"), None)
    in_specs = (rows, rows, P(), P(), P(), P(), P(), P(), P(), P(), P(), P(), P(),
                P(None, "mlp"), P("mlp"), P(None, "mlp"), P(), rows)
    block = P("dp", "mlp")
    out_specs = (rows, rows, P(), P(), block, P(), P(), P(), P(), block, P(), P(), P(), block, P(), block, P())
    sizes = {name: mesh.shape[name] for name in ("dp", "mlp")}
    return jax.shard_map(
        functools.partial(per_device, sizes), mesh=mesh, in_specs=in_specs, out_specs=out_specs, check_vma=False)
```

time: 3040 us -> 678 us (0.22)
  local copies, waits for them, and re-layouts: 1490 us -> 35.3 us
  matrix products: 957 us -> 29.5 us
  Pallas kernels: 0 us -> 497 us
  other arithmetic: 359 us -> 23 us
  waiting for transfers between devices: 144 us -> 25.7 us
    dot_general x27 -> x2, matrix products: 895 us -> 29.5 us  [mm(): return lax.dot_general(a, b, dims, preferred_element_type=F32)]
    add x7 -> x1, local copies, waits for them, and re-layouts: 818 us -> 0.83 us  [per_device(): rel = grel[0, :, :HEAD_DIM] + grel[1, :, HEAD_DIM:]]
    pallas_call x0 -> x4, Pallas kernels: none -> 497 us  [the longest x1 175 us: mlp(): pl.pallas_call(functools.partial(mlp_kernel, rows), grid=(steps,), in_spe...]
    reshape x13 -> x16, local copies, waits for them, and re-layouts: 464 us -> 17.2 us  [the longest x4 10.7 us: by_owner(): return grad.reshape(dp, rows // dp, mlp, cols // mlp).transpose(0, 2, 1, 3)]
    reduce_sum x9 -> x4, other arithmetic: 316 us -> 2.71 us  [per_device(): fold = lambda v: jnp.sum(v.reshape(-1, 8, v.shape[1]), axis=1).reshape(-1)]
    reduce_scatter x6 -> x2, waiting for transfers between devices: 143 us -> 8.6 us  [the longest x1 8.6 us: per_device(): lax.psum_scatter(both, 'mlp', scatter_dimension=0, tiled=True)[0]]
    convert_element_type x9 -> x4, local copies, waits for them, and re-layouts: 107 us -> 2.15 us  [the longest x1 1.9 us: small_tables(): valid_rows = valid[:, :AREA].reshape(-1, 1).astype(F32)]
    sub x1 -> x0, matrix products: 61.6 us -> none  [per_device(): grad_weights - jnp.sum(weights * grad_weights, axis=-1, keepdims=True)]
  transfers between devices with their start and end apart: 10 -> 9, of which waited for: 3 -> 4; matrix products, arithmetic and copies ran while one was open for 68% -> 11% of each run, Pallas kernels for 0% -> 48%
where the time goes in v1:
time: 678 us
  Pallas kernels  497 us (73%)
  blocking collectives  45.3 us (7%)
  local copies, waits for them, and re-layouts  35.3 us (5%)
  matrix products  29.5 us (4%)
  waiting for transfers between devices  25.7 us (4%)
  other arithmetic  23 us (3%)
  between operations  14.2 us (2%)
  starting transfers between devices  7.22 us (1%)
    pallas_call x1, Pallas kernels, mlp(): pl.pallas_call(functools.partial(mlp_kernel, rows), grid=(steps,), in_spe...  175 us
    pallas_call x1, Pallas kernels, attention_backward(): pl.pallas_call(backward_kernel, grid=(windows // wb,), in_specs=[blocked(...  158 us
    pallas_call x1, Pallas kernels, attention_forward(): pl.pallas_call(forward_kernel, grid=(windows // wb,), in_specs=[blocked(w...  138 us
    psum x1, blocking collectives, per_device(): sums = lax.psum(sums, ('dp', 'mlp'))  39.9 us
    dot_general x2, matrix products, mm(): return lax.dot_general(a, b, dims, preferred_element_type=F32)  29.5 us
    pallas_call x1, Pallas kernels, input_gradient(): pl.pallas_call(input_kernel, grid=(windows // wb,), in_specs=[blocked(wb...  26.4 us
    ppermute x5, waiting for transfers between devices, halve(): got = lax.ppermute(send, axis, [(i, i ^ 1 << bit) for i in range(n)])  15.7 us
  transfers between devices with their start and end apart: 9, of which 4 were waited for; matrix products, arithmetic and copies ran while one was open for 11% of the time, Pallas kernels for 48%

profile of v1, /device:TPU:0, one launch (start us, length us, event | category | flops | bytes accessed | tf_op | source)
XLA Modules:
  0.0 677.7 jit_solution(3873453066584739882)
XLA Ops:
  12.9 1.9 reshape.461.mask_ref
  18.3 1.6 pad_maximum_fusion.2.ohm_ref
  19.9 138.4 %attention_forward.1 = (f32[3920,768]{1,0:T(8,128)}, bf16[20,208,768]{2,1,0:T(8,128)(2,1)}, bf16[20,208,2304]{2,1,0:T(8,128)(2,1)}, bf16[20,6,256,208]{3,2,1,0:T...) custom-call(bf16[3920,768]{1,0:T(8,128)(2,1)} %x_ref.3, ...), custom_call_target="tpu_custom_call" | custom-call | tf_op jit(solution)/shard_map/attention_forward/pallas_call | solution.py:149
  158.3 5.3 all-gather
  163.6 174.8 %mlp.1 = (bf16[3920,768]{1,0:T(8,128)(2,1)}, bf16[3920,768]{1,0:T(8,128)(2,1)}, bf16[768,3072]{1,0:T(8,128)(2,1)}, bf16[768,3072]{1,0:T(8,128)(2,1)}, f32[8,3072]{1,0:T(8,128)}, /*index=5*/f32[32,768]{1,0:T(8,128)}) custom-call(f32[3920,768]{1,0:T(8,128)} %get-tuple-element.35.x1_ref, bf16[3920,768]{1,0:T(8,128)(2,1)} %go_ref.1, ...), custom_call_target="tpu_custom_call" | custom-call | tf_op jit(solution)/shard_map/mlp/pallas_call | solution.py:423
  338.4 9.0 %pad_maximum_fusion = bf16[768,6144]{1,0:T(8,128)(2,1)} fusion(bf16[768,3072]{1,0:T(8,128)(2,1)} %get-tuple-element.52, bf16[768,3072]{1,0:T(8,128)(2,1)} %get-tuple-element.51), kind=kLoop, calls=%fused_computation | loop fusion | flops 18874368 | bytes 18874368 | tf_op jit(solution)/shard_map/concatenate | solution.py:508
  349.0 157.8 %attention_backward.1 = (bf16[20,208,768]{2,1,0:T(8,128)(2,1)}, bf16[20,208,2304]{2,1,0:T(8,128)(2,1)}, f32[2,64,128]{2,1,0:T(8,128)}, f32[16,768]{1,0:T(8,128)}) custom-call(bf16[3920,768]{1,0:T(8,128)(2,1)} %get-tuple-element.37.da_ref, bf16[20,208,128]{2,1,0:T(8,128)(2,1)} %pad_maximum_fusion.2.ohm_ref, bf16[32,208]{1,0:T(8,128)(2,1)} %maximum_bitcast_fusion.oht_ref, ...), custom_call_target="tpu_custom_call" | custom-call | tf_op jit(solution)/shard_map/attention_backward/pallas_call | solution.py:229
  506.8 21.1 %bitcast_convert_fusion = bf16[768,2304]{1,0:T(8,128)(2,1)S(1)} fusion(bf16[20,208,768]{2,1,0:T(8,128)(2,1)} %get-tuple-element.48, bf16[20,208,2304]{2,1,0:T(8,128)(2,1)} %get-tuple-element.41.dp_ref), kind=kOutput, calls=%fused_computation.1 | convolution fusion | flops 14723776512 | bytes 29097984 | tf_op jit(solution)/shard_map/dot_general | solution.py:28
  527.9 3.1 reshape.446
  531.0 2.6 copy.68
  534.8 8.4 %bitcast_convert_fusion.1 = bf16[768,768]{1,0:T(8,128)(2,1)} fusion(bf16[20,208,768]{2,1,0:T(8,128)(2,1)} %get-tuple-element.49, bf16[20,208,768]{2,1,0:T(8,128)(2,1)S(1)} %copy-done.15), kind=kOutput, calls=%fused_computation.8 | convolution fusion | flops 4907925504 | bytes 13959168 | tf_op jit(solution)/shard_map/dot_general | solution.py:28
  543.3 3.6 reshape.447
  548.9 2.2 copy-done
  551.4 4.6 collective-permute-done
  556.1 3.1 fusion
  559.3 2.1 collective-permute-start.1
  561.4 26.4 %input_gradient.1 = (bf16[3920,768]{1,0:T(8,128)(2,1)}, f32[16,768]{1,0:T(8,128)}) custom-call(bf16[3920,768]{1,0:T(8,128)(2,1)} %x_ref.3, bf16[3920,768]{1,0:T(8,128)(2,1)} %get-tuple-element.37.da_ref, bf16[20,208,2304]{2,1,0:T(8,128)(2,1)} %get-tuple-element.41.dp_ref, f32[1,768]{1,0:T(1,128)} %reshape.432.gain_ref, bf16[768,2304]{1,0:T(8,128)(2,1)} %wqkv_ref.3), custom_call_target="tpu_custom_call" | custom-call | tf_op jit(solution)/shard_map/input_gradient/pallas_call | solution.py:274
  589.4 1.6 fusion.1
  591.0 1.6 collective-permute-start.2
  599.1 7.0 %collective-permute-done.2 = bf16[2,2,48,1536]{3,2,1,0:T(8,128)(2,1)S(1)} collective-permute-done((bf16[2,2,48,1536]{3,2,1,0:T(8,128)(2,1)S(1)}, bf16[2,2,48,1536]{3,2,1,0:T(8,128)(2,1)S(1)}, u32[]{:S(2)}, u32[]{:S(2)}) %collective-permute-start.2) | collective-permute-done | bytes 589856 | tf_op jit(solution)/shard_map/ppermute | solution.py:465
  606.3 2.6 collective-permute-start.3
  609.6 39.9 %psum.7 = f32[13312]{0:T(1024)S(1)} all-reduce(f32[13312]{0:T(1024)} %constant_dynamic-update-slice_fusion), channel_id=1, replica_groups=mesh['dp'=16,'mlp'=2] {'dp','mlp'}, use_global_device_ids=true, to_apply=%region_4.5 | all-reduce | flops 13312 | bytes 106496 | tf_op jit(solution)/shard_map/psum | solution.py:522
  655.2 4.1 collective-permute-done.4
  660.7 8.6 %reduce-scatter.5.cloned.1.call-done = bf16[1,2,48,1536]{3,2,1,0:T(8,128)(2,1)} async-done(((bf16[2,2,48,1536]{3,2,1,0:T(8,128)(2,1)}), bf16[1,2,48,1536]{3,2,1,0:T(8,128)(2,1)}) %reduce-scatter.5.cloned.1.call-update) | async-done | bytes 294928 | tf_op jit(solution)/shard_map/reduce_scatter | solution.py:511
  (125 shorter events, 32.1 us)
Async XLA Ops:
  7.2 2.1 copy-start.4
  7.2 3.2 copy-start.6
  7.2 3.8 copy-start.13
  7.2 3.8 copy-start.12
  7.2 4.4 copy-start.7
  7.3 5.0 copy-start.8
  7.3 5.5 copy-start.14
  7.3 7.5 %copy-start.5 = (f32[1536]{0:T(1024)S(1)}, f32[1536]{0:T(1024)}, u32[]{:S(2)}) copy-start(f32[1536]{0:T(1024)} %param.32) | copy-start | bytes 18436
  7.3 7.5 %copy-start.9 = (f32[768]{0:T(1024)S(1)}, f32[768]{0:T(1024)}, u32[]{:S(2)}) copy-start(f32[768]{0:T(1024)} %param.29) | copy-start | bytes 9220
  7.3 8.1 %copy-start.10 = (f32[768]{0:T(1024)S(1)}, f32[768]{0:T(1024)}, u32[]{:S(2)}) copy-start(f32[768]{0:T(1024)} %param.30) | copy-start | bytes 9220
  7.3 8.7 %copy-start.11 = (f32[768]{0:T(1024)S(1)}, f32[768]{0:T(1024)}, u32[]{:S(2)}) copy-start(f32[768]{0:T(1024)} %param.34) | copy-start | bytes 9220
  7.3 156.3 %all-gather.4.cloned.1.call-start = ((), (), s32[]{:S(2)}) async-start(), calls=%async_computation.2 | async-start | bytes 7077888 | tf_op jit(solution)/shard_map/all_gather | solution.py:498
  8.0 155.6 %all-gather.6.cloned.1.call-start = ((), (), s32[]{:S(2)}) async-start(), calls=%async_computation.3 | async-start | bytes 7077888 | tf_op jit(solution)/shard_map/all_gather | solution.py:499
  8.8 642.7 %reduce-scatter.3.cloned.1.call-start = ((), (), s32[]{:S(2)}) async-start(), calls=%async_computation.4 | async-start | bytes 10027008 | tf_op jit(solution)/shard_map/reduce_scatter | solution.py:509
  347.4 321.8 %reduce-scatter.5.cloned.1.call-start = ((), (), s32[]{:S(2)}) async-start(), calls=%async_computation.5 | async-start | bytes 884736 | tf_op jit(solution)/shard_map/reduce_scatter | solution.py:511
  531.0 3.9 copy-start.15
  548.9 2.2 copy-start
  551.3 4.7 collective-permute-start
  559.3 30.1 %collective-permute-start.1 = (bf16[2,2,2,48,1536]{4,3,2,1,0:T(8,128)(2,1)S(1)}, bf16[2,2,2,48,1536]{4,3,2,1,0:T(8,128)(2,1)}, u32[]{:S(2)}, u32[]{:S(2)}) collective-permute-start(bf16[2,2,2,48,1536]{4,3,2,1,0:T(8,128)(2,1)S(1)} %dynamic-slice_bitcast_fusion.1), channel_id=1, source_target_pairs={{0,1},{1,0},{2,3},{3,2},{4,5},{5,4},{6,7},{7,6},{8,9},{9,8},{10,11... | collective-permute-start | bytes 3538952 | tf_op jit(solution)/shard_map/ppermute | solution.py:465
  561.4 27.3 %copy-start.1 = (f32[2,64,128]{2,1,0:T(8,128)S(1)}, f32[2,64,128]{2,1,0:T(8,128)}, u32[]{:S(2)}) copy-start(f32[2,64,128]{2,1,0:T(8,128)} %get-tuple-element.45) | copy-start | bytes 196612
  587.8 4.7 copy-start.2
  591.0 15.2 %collective-permute-start.2 = (bf16[2,2,48,1536]{3,2,1,0:T(8,128)(2,1)S(1)}, bf16[2,2,48,1536]{3,2,1,0:T(8,128)(2,1)S(1)}, u32[]{:S(2)}, u32[]{:S(2)}) collective-permute-start(bf16[2,2,48,1536]{3,2,1,0:T(8,128)(2,1)S(1)} %dynamic-slice_bitcast_fusion.2), channel_id=1, source_target_pairs={{0,4},{2,6},{4,0},{6,2},{8,12},{10,14},{12,8},{14,10},{16,20},{18,... | collective-permute-start | bytes 1769480 | tf_op jit(solution)/shard_map/ppermute | solution.py:465
  606.3 47.6 %collective-permute-start.3 = (bf16[2,48,1536]{2,1,0:T(8,128)(2,1)S(1)}, bf16[2,48,1536]{2,1,0:T(8,128)(2,1)S(1)}, u32[]{:S(2)}, u32[]{:S(2)}) collective-permute-start(bf16[2,48,1536]{2,1,0:T(8,128)(2,1)S(1)} %dynamic-slice_bitcast_fusion.3), channel_id=1, source_target_pairs={{0,16},{2,18},{4,20},{6,22},{8,24},{10,26},{12,28},{14,30},{16,0},... | collective-permute-start | bytes 884744 | tf_op jit(solution)/shard_map/ppermute | solution.py:465
  654.1 5.2 collective-permute-start.4
  (1 other events, 1.9 us)
Sparse Core Ops, SparseCore 0:
  9.7 65.3 all-gather.3
  76.6 62.7 all-gather.5
  347.6 113.1 reduce-scatter.2
  654.1 15.1 reduce-scatter.4

commit v2 on v1

v2 whole, which is shorter than its diff:
```python
import functools
import jax
import jax.numpy as jnp
from jax import lax
from jax.experimental import pallas as pl
from jax.experimental.pallas import tpu as pltpu
from jax.sharding import PartitionSpec as P

HEADS = 12
HEAD_DIM = 64
WIN = 14
AREA = WIN * WIN
PADDED = 208
PAIRS = HEADS // 2
MODEL = HEADS * HEAD_DIM
EPSILON = 1e-6
NEGATIVE = -1e30
SCALE = HEAD_DIM ** -0.5
F32 = jnp.float32
BF16 = jnp.bfloat16
NN = (((1,), (0,)), ((), ()))
NT = (((1,), (1,)), ((), ()))
TN = (((0,), (0,)), ((), ()))
TOGETHER = 6
TOGETHER_BACK = 6
VMEM_LIMIT = 60 * 1024 * 1024


def mm(a, b, dims=NN):
    return lax.dot_general(a, b, dims, preferred_element_type=F32)


def fold8(v):
    return jnp.sum(v.reshape(v.shape[0] // 8, 8, v.shape[1]), axis=0)


def norm(v):
    mu = jnp.mean(v, axis=-1, keepdims=True)
    c = v - mu
    return c, lax.rsqrt(jnp.mean(c * c, axis=-1, keepdims=True) + EPSILON)


def eye(n, value=1.0):
    r = lax.broadcasted_iota(jnp.int32, (n, n), 0)
    c = lax.broadcasted_iota(jnp.int32, (n, n), 1)
    return jnp.where(r == c, value, 0.0).astype(BF16)


def skew_bits(which):
    lane = lax.broadcasted_iota(jnp.int32, (1, PADDED), 1)
    r = lane // WIN
    return WIN - 1 - (jnp.minimum(r, WIN - 1) if which == 0 else lane - r * WIN)


def split(v):
    hi = v.astype(BF16)
    return hi, (v - hi.astype(F32)).astype(BF16)


def key_side(k, ohm):
    return jnp.concatenate([k, ohm], axis=1)


def query_side(qa, h):
    z = jnp.zeros((HEAD_DIM, PADDED), BF16)
    own = qa[h * 64:(h + 1) * 64]
    bias = qa[128 + 64 * h:192 + 64 * h]
    return jnp.concatenate(([own, z] if h == 0 else [z, own]) + [bias, z], axis=0)


def forward_kernel(x_ref, ohm_ref, gain_ref, bias_ref, wqkv_ref, qkvb_ref, mix_ref, shift_ref, wproj_ref, projb_ref,
                   x1_ref, xhat_ref, qkv_ref, qaug_ref, o_ref, lse_ref, h1_ref, wide):
    wb = ohm_ref.shape[0]
    for w in range(wb):
        x = x_ref[AREA * w:AREA * (w + 1), :].astype(F32)
        c, r = norm(x)
        xhat = c * r
        h1_ref[w, PADDED - 16:, :] = jnp.zeros((16, MODEL), BF16)
        xhat_ref[w, PADDED - 16:, :] = jnp.zeros((16, MODEL), BF16)
        h1_ref[w, 0:AREA, :] = (xhat * gain_ref[...] + bias_ref[...]).astype(BF16)
        xhat_ref[w, 0:AREA, :] = xhat.astype(BF16)

    @pl.loop(0, 3)
    def _(j):
        cs = pl.ds(pl.multiple_of(j * MODEL, MODEL), MODEL)
        p = mm(h1_ref[...].reshape(wb * PADDED, MODEL), wqkv_ref[:, cs]) + qkvb_ref[:, cs]
        qkv_ref[:, :, cs] = p.astype(BF16).reshape(wb, PADDED, MODEL)

    groups = PAIRS // TOGETHER

    @pl.loop(0, wb * groups)
    def _(it):
        w = it // groups
        base = (it - w * groups) * TOGETHER
        pairs = [base + n for n in range(TOGETHER)]
        lanes = lambda part, pair: pl.ds(pl.multiple_of(part * MODEL + pair * 128, 128), 128)
        qs = [qkv_ref[w, :, lanes(0, p)] for p in pairs]
        us = [mm(mix_ref[...], jnp.concatenate([q, q], axis=1), NT) for q in qs]
        vts = [mm(eye(128), qkv_ref[w, :, lanes(2, p)], NT).astype(BF16) for p in pairs]
        row = lax.broadcasted_iota(jnp.int32, (16, 1), 0)
        qas = []
        for p, u in zip(pairs, us):
            tabs = []
            for t in range(2):
                a = u[64 * t:64 * t + 64]
                for n, b in enumerate((8, 4, 2, 1)):
                    cond = shift_ref[4 * t + n:4 * t + n + 1, :] > 0
                    a = jnp.where(cond, pltpu.roll(a, 64 - b, 0), a)
                tabs.append(a)
            parts = [u[128:256].astype(BF16)]
            for h in range(2):
                ah = jnp.where(row == 14, 1.0, tabs[0][32 * h:32 * h + 16])
                aw = tabs[1][32 * h:32 * h + 16]
                hh, hl = split(ah)
                wh, wl = split(aw)
                parts += [hh, wh, hl, wl]
            qa = jnp.concatenate(parts, axis=0)
            qaug_ref[w, p] = qa
            qas.append(qa)
        keys = [key_side(qkv_ref[w, :, lanes(1, p)], ohm_ref[w]) for p in pairs]
        scores = [mm(key, query_side(qa, h)) for key, qa in zip(keys, qas) for h in range(2)]
        ots = []
        for n, s in enumerate(scores):
            p, h = pairs[n // 2], n % 2
            top = jnp.max(s, axis=0, keepdims=True)
            e = jnp.exp(s - top)
            total = jnp.sum(e, axis=0, keepdims=True)
            lse_ref[w, p, h:h + 1, :] = top + jnp.log(total)
            ots.append(mm(vts[n // 2][64 * h:64 * h + 64], e.astype(BF16)) * (1.0 / total))
        for n, p in enumerate(pairs):
            ot = jnp.concatenate(ots[2 * n:2 * n + 2], axis=0).astype(BF16)
            o_ref[w, :, lanes(0, p)] = mm(eye(PADDED), ot, NT).astype(BF16)

    wide[...] = mm(o_ref[...].reshape(wb * PADDED, MODEL), wproj_ref[...]) + projb_ref[...]
    for w in range(wb):
        x1_ref[AREA * w:AREA * (w + 1), :] = x_ref[AREA * w:AREA * (w + 1), :].astype(F32) + wide[PADDED * w:PADDED * w + AREA, :]


def cost(us):
    return pl.CostEstimate(flops=int(us * 1.0e9), bytes_accessed=1 << 20, transcendentals=0)


def once(a):
    return pl.BlockSpec(a.shape, lambda i: (0,) * a.ndim, pipeline_mode=pl.Buffered(1))


def blocked(*shape):
    return pl.BlockSpec(shape, lambda i: (i,) + (0,) * (len(shape) - 1))


def block_windows(windows):
    return 4 if windows % 4 == 0 else windows


def attention_forward(x, ohm, gain, bias, wqkv, qkvb, mix, shift, wproj, projb):
    windows = ohm.shape[0]
    wb = block_windows(windows)
    outs = [((windows * AREA, MODEL), F32, (wb * AREA, MODEL)),
            ((windows, PADDED, MODEL), BF16, (wb, PADDED, MODEL)),
            ((windows, PADDED, 3 * MODEL), BF16, (wb, PADDED, 3 * MODEL)),
            ((windows, PAIRS, 256, PADDED), BF16, (wb, PAIRS, 256, PADDED)),
            ((windows, PADDED, MODEL), BF16, (wb, PADDED, MODEL)),
            ((windows, PAIRS, 2, PADDED), F32, (wb, PAIRS, 2, PADDED))]
    return pl.pallas_call(
        forward_kernel,
        grid=(windows // wb,),
        in_specs=[blocked(wb * AREA, MODEL), blocked(wb, PADDED, 128)] + [once(a) for a in (gain, bias, wqkv, qkvb, mix, shift, wproj, projb)],
        out_specs=[blocked(*b) for _, _, b in outs],
        out_shape=[jax.ShapeDtypeStruct(s, t) for s, t, _ in outs],
        scratch_shapes=[pltpu.VMEM((wb, PADDED, MODEL), BF16), pltpu.VMEM((wb * PADDED, MODEL), F32)],
        cost_estimate=cost(70),
        compiler_params=pltpu.CompilerParams(vmem_limit_bytes=VMEM_LIMIT, dimension_semantics=("arbitrary",)),
        name="attention_forward",
    )(x, ohm, gain, bias, wqkv, qkvb, mix, shift, wproj, projb)


def backward_kernel(da_ref, ohm_ref, oht_ref, qkv_ref, qaug_ref, lse_ref, wproj_ref, relt_ref, shift_ref,
                    dap_ref, dp_ref, grel_ref, do_ref):
    wb = ohm_ref.shape[0]

    @pl.when(pl.program_id(0) == 0)
    def _():
        grel_ref[...] = jnp.zeros_like(grel_ref)

    for w in range(wb):
        dap_ref[w, PADDED - 16:, :] = jnp.zeros((16, MODEL), BF16)
        dap_ref[w, 0:AREA, :] = da_ref[AREA * w:AREA * (w + 1), :]
    do_ref[...] = mm(dap_ref[...].reshape(wb * PADDED, MODEL), wproj_ref[...], NT).astype(BF16).reshape(wb, PADDED, MODEL)

    groups = PAIRS // TOGETHER_BACK

    @pl.loop(0, wb * groups)
    def _(it):
        w = it // groups
        base = (it - w * groups) * TOGETHER_BACK
        pairs = [base + n for n in range(TOGETHER_BACK)]
        lanes = lambda part, pair: pl.ds(pl.multiple_of(part * MODEL + pair * 128, 128), 128)
        both = [(n, p, h) for n, p in enumerate(pairs) for h in range(2)]
        qs = [qkv_ref[w, :, lanes(0, p)] for p in pairs]
        ks = [qkv_ref[w, :, lanes(1, p)] for p in pairs]
        vs = [qkv_ref[w, :, lanes(2, p)] for p in pairs]
        dos = [do_ref[w, :, lanes(0, p)] for p in pairs]
        scores = [mm(key_side(ks[n], ohm_ref[w]), query_side(qaug_ref[w, p], h)) for n, p, h in both]
        dots = [mm(eye(128), do, NT).astype(BF16) for do in dos]
        kts = [mm(eye(128, SCALE), k, NT).astype(BF16) for k in ks]
        z = jnp.zeros((HEAD_DIM, PADDED), BF16)
        dws = []
        for n, p, h in both:
            own = dots[n][64 * h:64 * h + 64]
            dws.append(mm(vs[n], jnp.concatenate([own, z] if h == 0 else [z, own], axis=0)))
        dvs, dks, dqs = [], [], []
        for s, dw, (n, p, h) in zip(scores, dws, both):
            a = jnp.exp(s - lse_ref[w, p, h:h + 1, :])
            t = a * dw
            dsb = (t - a * jnp.sum(t, axis=0, keepdims=True)).astype(BF16)
            dvs.append(mm(a.astype(BF16), dos[n]))
            dks.append(mm(dsb, qs[n]))
            dqs.append(mm(jnp.concatenate([kts[n][64 * h:64 * h + 64], oht_ref[...]], axis=0), dsb))
        first = lax.broadcasted_iota(jnp.int32, (1, 128), 1) < 64
        zz = jnp.zeros((16, PADDED), F32)
        dqts = []
        for n, p in enumerate(pairs):
            tabs = []
            for t in range(2):
                lo = 64 + 16 * t
                a = jnp.concatenate([dqs[2 * n][lo:lo + 16], zz, dqs[2 * n + 1][lo:lo + 16], zz], axis=0)
                for i, b in enumerate((8, 4, 2, 1)):
                    cond = shift_ref[4 * t + i:4 * t + i + 1, :] > 0
                    a = jnp.where(cond, pltpu.roll(a, b, 0), a)
                tabs.append(a.astype(BF16))
            dqt = []
            for h in range(2):
                du = jnp.concatenate([tabs[0][32 * h:32 * h + 32], tabs[1][32 * h:32 * h + 32]], axis=0)
                dqt.append(dqs[2 * n + h][0:64] + mm(relt_ref[...], jnp.concatenate([du, du], axis=0)))
                grel_ref[h] += mm(du, qs[n])
            dqts.append(jnp.concatenate(dqt, axis=0).astype(BF16))
        for n, p in enumerate(pairs):
            dq = mm(eye(PADDED), dqts[n], NT).astype(BF16)
            dk = (jnp.where(first, dks[2 * n], dks[2 * n + 1]) * SCALE).astype(BF16)
            dv = jnp.where(first, dvs[2 * n], dvs[2 * n + 1]).astype(BF16)
            dp_ref[w, :, lanes(0, p)] = dq
            dp_ref[w, :, lanes(1, p)] = dk
            dp_ref[w, :, lanes(2, p)] = dv


def attention_backward(da, ohm, oht, qkv, qaug, lse, wproj, relt, shift):
    windows = ohm.shape[0]
    wb = block_windows(windows)
    return pl.pallas_call(
        backward_kernel,
        grid=(windows // wb,),
        in_specs=[blocked(wb * AREA, MODEL), blocked(wb, PADDED, 128), once(oht), blocked(wb, PADDED, 3 * MODEL),
                  blocked(wb, PAIRS, 256, PADDED), blocked(wb, PAIRS, 2, PADDED), once(wproj), once(relt), once(shift)],
        out_specs=[blocked(wb, PADDED, MODEL), blocked(wb, PADDED, 3 * MODEL),
                   pl.BlockSpec((2, 64, 128), lambda i: (0, 0, 0))],
        out_shape=[jax.ShapeDtypeStruct((windows, PADDED, MODEL), BF16), jax.ShapeDtypeStruct((windows, PADDED, 3 * MODEL), BF16),
                   jax.ShapeDtypeStruct((2, 64, 128), F32)],
        scratch_shapes=[pltpu.VMEM((wb, PADDED, MODEL), BF16)],
        cost_estimate=cost(70),
        compiler_params=pltpu.CompilerParams(vmem_limit_bytes=VMEM_LIMIT, dimension_semantics=("arbitrary",)),
        name="attention_backward",
    )(da, ohm, oht, qkv, qaug, lse, wproj, relt, shift)


def input_kernel(x_ref, da_ref, dp_ref, gain_ref, wqkv_ref, *rest):
    gx_ref, wide, tall = rest[-3:]
    wb = dp_ref.shape[0]
    wide[...] = mm(dp_ref[...].reshape(wb * PADDED, 3 * MODEL), wqkv_ref[...], NT)
    for w in range(wb):
        tall[AREA * w:AREA * (w + 1), :] = wide[PADDED * w:PADDED * w + AREA, :]
    rows = wb * AREA
    for lo in range(0, rows, 112):
        hi = min(lo + 112, rows)
        c, r = norm(x_ref[lo:hi, :].astype(F32))
        xhat = c * r
        dx = tall[lo:hi, :] * gain_ref[...]
        dx = r * (dx - jnp.mean(dx, axis=-1, keepdims=True) - xhat * jnp.mean(dx * xhat, axis=-1, keepdims=True))
        gx_ref[lo:hi, :] = (dx + da_ref[lo:hi, :].astype(F32)).astype(BF16)


def input_gradient(x, da, dp, gain, wqkv, at, count, held):
    windows = dp.shape[0]
    wb = block_windows(windows)
    part = lambda *shape: pl.BlockSpec(shape, lambda i: (i + at,) + (0,) * (len(shape) - 1))
    extra = [] if held is None else [held]
    return pl.pallas_call(
        input_kernel,
        grid=(count,),
        in_specs=[part(wb * AREA, MODEL), part(wb * AREA, MODEL), part(wb, PADDED, 3 * MODEL), once(gain), once(wqkv)]
        + [pl.BlockSpec(memory_space=pl.ANY)] * len(extra),
        out_specs=part(wb * AREA, MODEL),
        out_shape=jax.ShapeDtypeStruct((windows * AREA, MODEL), BF16),
        input_output_aliases={5: 0} if extra else {},
        scratch_shapes=[pltpu.VMEM((wb * PADDED, MODEL), F32), pltpu.VMEM((wb * AREA, MODEL), F32)],
        cost_estimate=cost(5 * count),
        compiler_params=pltpu.CompilerParams(vmem_limit_bytes=VMEM_LIMIT, dimension_semantics=("arbitrary",)),
        name="input_gradient",
    )(x, da, dp, gain, wqkv, *extra)


BAND = 384


def weight_kernel(xhat_ref, o_ref, dp_ref, dap_ref, w_ref, gain_ref, bias_ref, dw_ref, sum_ref, gvec_ref, bvec_ref, turned):
    step = pl.program_id(0)
    qkv_bands = 3 * MODEL // BAND

    @pl.when(step == 0)
    def _():
        turned[...] = xhat_ref[...].T
        gvec_ref[...] = jnp.zeros_like(gvec_ref)
        bvec_ref[...] = jnp.zeros_like(bvec_ref)

    @pl.when(step == qkv_bands)
    def _():
        turned[...] = o_ref[...].T

    @pl.when(step < qkv_bands)
    def _():
        m = mm(turned[...], dp_ref[...])
        s = jnp.sum(dp_ref[...].astype(F32), axis=0, keepdims=True)
        sum_ref[...] = jnp.broadcast_to(s, sum_ref.shape)
        dw_ref[...] = (m * gain_ref[...] + bias_ref[...] * s).astype(BF16)
        w = w_ref[...].astype(F32)
        g, b = w * m, w * s
        for n in range(BAND // 128):
            gvec_ref[...] += g[:, 128 * n:128 * (n + 1)]
            bvec_ref[...] += b[:, 128 * n:128 * (n + 1)]

    @pl.when(step >= qkv_bands)
    def _():
        dw_ref[...] = mm(turned[...], dap_ref[...]).astype(BF16)


def weight_gradients(xhat, o, dp, dap, wqkv, gain, bias, owners):
    rows = xhat.shape[0]
    nq, np_ = 3 * MODEL // BAND, MODEL // BAND
    oq, op = nq // owners, np_ // owners
    last = lambda i: jnp.minimum(i, nq - 1)

    def place(i):
        j = i - nq
        q = (i // oq) * (oq + op) + i % oq
        p = (j // op) * (oq + op) + oq + j % op
        return (0, jnp.where(i < nq, q, p))
    return pl.pallas_call(
        weight_kernel,
        grid=(nq + np_,),
        in_specs=[once(xhat), once(o), pl.BlockSpec((rows, BAND), lambda i: (0, last(i))),
                  pl.BlockSpec((rows, BAND), lambda i: (0, jnp.maximum(i - nq, 0))),
                  pl.BlockSpec((MODEL, BAND), lambda i: (0, last(i))), once(gain), once(bias)],
        out_specs=[pl.BlockSpec((MODEL, BAND), place), pl.BlockSpec((8, BAND), lambda i: (0, last(i))),
                   pl.BlockSpec((MODEL, 128), lambda i: (0, 0)), pl.BlockSpec((MODEL, 128), lambda i: (0, 0))],
        out_shape=[jax.ShapeDtypeStruct((MODEL, 4 * MODEL), BF16), jax.ShapeDtypeStruct((8, 3 * MODEL), F32),
                   jax.ShapeDtypeStruct((MODEL, 128), F32), jax.ShapeDtypeStruct((MODEL, 128), F32)],
        scratch_shapes=[pltpu.VMEM((MODEL, rows), BF16)],
        cost_estimate=cost(20),
        compiler_params=pltpu.CompilerParams(vmem_limit_bytes=VMEM_LIMIT, dimension_semantics=("arbitrary",)),
        name="weight_gradients",
    )(xhat, o, dp, dap, wqkv, gain, bias)


def small_tables(window_extent, rel_h, rel_w):
    place = jnp.arange(PADDED)
    r, c = place // WIN, place % WIN
    real = place < AREA
    hot_r = ((r[:, None] == jnp.arange(16)) & real[:, None]).astype(F32)
    hot_c = ((c[:, None] == jnp.arange(16)) & real[:, None]).astype(F32)
    valid = (r < window_extent[:, 0:1]) & (c < window_extent[:, 1:2]) & real
    first = jnp.where((jnp.arange(16) == 14)[None, None, :], jnp.where(valid, 0.0, NEGATIVE)[:, :, None], hot_r[None])
    rest = jnp.concatenate([hot_c, hot_r, hot_c, jnp.zeros((PADDED, 64), F32)], axis=1)
    rest = jnp.broadcast_to(rest[None], (valid.shape[0],) + rest.shape)
    ohm = jnp.concatenate([first, rest], axis=2).astype(BF16)
    oht = jnp.concatenate([hot_r, hot_c], axis=1).T.astype(BF16)
    sh = WIN - 1 - jnp.minimum(r, WIN - 1)
    sw = WIN - 1 - c
    shift = jnp.stack([jnp.where(real, (s >> b) & 1, 0) for s in (sh, sw) for b in (3, 2, 1, 0)]).astype(jnp.int32)
    flip = lambda t: jnp.concatenate([t[::-1], jnp.zeros((5, HEAD_DIM), F32)], axis=0)
    fh, fw = flip(rel_h), flip(rel_w)

    def hi_lo(v):
        hi = v.astype(BF16).astype(F32)
        return hi, v - hi

    def rows(th, tw):
        z = jnp.zeros((32, HEAD_DIM), F32)
        return jnp.concatenate([jnp.concatenate([th, z], 1), jnp.concatenate([z, th], 1),
                                jnp.concatenate([tw, z], 1), jnp.concatenate([z, tw], 1)], axis=0)
    (hh, hl), (wh, wl) = hi_lo(fh), hi_lo(fw)
    mix = jnp.concatenate([rows(hh, wh), rows(hl, wl)], axis=1)
    ident = jnp.concatenate([SCALE * jnp.eye(128, dtype=F32), jnp.zeros((128, 128), F32)], axis=1)
    mix = jnp.concatenate([mix, ident], axis=0).astype(BF16)
    relt = jnp.concatenate([hh, wh, hl, wl], axis=0).T.astype(BF16)
    valid_rows = valid[:, :AREA].reshape(-1, 1).astype(F32)
    return ohm, oht, shift, mix, relt, valid_rows


def gelu_parts(z):
    u = jnp.abs(z)
    t = 1.0 / (1.0 + 0.23164189 * u)
    e = jnp.exp(-0.5 * z * z)
    poly = t * (0.127414796 + t * (-0.142248368 + t * (0.7107068705 + t * (-0.7265760135 + t * 0.5307027145))))
    q = poly * e
    phi = jnp.where(z >= 0.0, 1.0 - q, q)
    return z * phi, phi + z * e * 0.3989422804


ROWS = 512
CHUNK = 64 * 12


def mlp_kernel(rows, widths, offset_ref, x1_ref, go_ref, mask_ref, gain_ref, bias_ref, upb_ref, downb_ref, *rest):
    n = len(widths)
    ups, downs = rest[:n], rest[n:2 * n]
    out_ref, da_ref, dw_ref, dbu_ref, vec_ref, h2, dm, h2t, dmt, macc, dacc, accu, accd, stage, sems = rest[2 * n:]
    rb = h2.shape[0]
    ch = 256
    step = pl.program_id(0)

    @pl.when(step == 0)
    def _():
        accu[...] = jnp.zeros_like(accu)
        accd[...] = jnp.zeros_like(accd)
        dbu_ref[...] = jnp.zeros_like(dbu_ref)
        vec_ref[...] = jnp.zeros_like(vec_ref)

    def live(i):
        row = step * rb + i * ch + lax.broadcasted_iota(jnp.int32, (ch, 1), 0)
        return row < rows

    @pl.loop(0, rb // ch)
    def _(i):
        rs = pl.ds(pl.multiple_of(i * ch, ch), ch)
        x1 = jnp.where(live(i), x1_ref[rs, :], 0.0)
        c, r = norm(x1)
        h2[rs, :] = (c * r * gain_ref[...] + bias_ref[...]).astype(BF16)
        d = jnp.where(live(i) & (mask_ref[rs, :] > 0.0), go_ref[rs, :].astype(F32), 0.0)
        dm[rs, :] = d.astype(BF16)
        vec_ref[0:8, :] += fold8(d)

    h2t[...] = h2[...].T
    dmt[...] = dm[...].T

    at = 0
    for up_ref, down_ref, width in zip(ups, downs, widths):
        size = min(CHUNK, width)
        for lo in range(0, width, size):
            here, there = slice(lo, lo + size), slice(at, at + size)
            z = mm(h2[...], up_ref[:, here]) + upb_ref[:, there]
            dact = mm(dm[...], down_ref[:, here])
            g, gp = gelu_parts(z)
            g = g.astype(BF16)
            dz = (dact * gp).astype(BF16)
            dbu_ref[:, there] += fold8(dz.astype(F32))
            m = mm(g, down_ref[:, here], NT)
            macc[...] = m if at == 0 else macc[...] + m
            d = mm(dz, up_ref[:, here], NT)
            dacc[...] = d if at == 0 else dacc[...] + d
            accd[:, there] += mm(dmt[...], g)
            accu[:, there] += mm(h2t[...], dz)
            at += size

    @pl.loop(0, rb // ch)
    def _(i):
        rs = pl.ds(pl.multiple_of(i * ch, ch), ch)
        x1 = jnp.where(live(i), x1_ref[rs, :], 0.0)
        c, r = norm(x1)
        xhat = c * r
        valid = live(i) & (mask_ref[rs, :] > 0.0)
        out_ref[rs, :] = jnp.where(valid, x1 + macc[rs, :] + downb_ref[...], 0.0).astype(BF16)
        dh = dacc[rs, :]
        vec_ref[8:16, :] += fold8(dh * xhat)
        vec_ref[16:24, :] += fold8(dh)
        dx = dh * gain_ref[...]
        dx = r * (dx - jnp.mean(dx, axis=-1, keepdims=True) - xhat * jnp.mean(dx * xhat, axis=-1, keepdims=True))
        da = (dx + dm[rs, :].astype(F32)).astype(BF16)
        da_ref[rs, :] = da
        vec_ref[24:32, :] += fold8(da.astype(F32))

    @pl.when(step == pl.num_programs(0) - 1)
    def _():
        size = stage.shape[2]
        each = accu.shape[1] // size

        def copy(k):
            to = pl.multiple_of(offset_ref[k], 128)
            return pltpu.make_async_copy(stage.at[k % 2], dw_ref.at[:, pl.ds(to, size)], sems.at[k % 2])
        for k in range(2 * each):
            if k >= 2:
                copy(k - 2).wait()
            src = (accu, accd)[k // each]
            stage[k % 2] = src[:, (k % each) * size:(k % each + 1) * size].astype(BF16)
            copy(k).start()
        copy(2 * each - 2).wait()
        copy(2 * each - 1).wait()


def mlp(x1, go, mask, gain, bias, upb, downb, ups, downs, offsets):
    rows, d = x1.shape
    widths = tuple(u.shape[1] for u in ups)
    ff = sum(widths)
    size = 2 * ff // offsets.shape[0]
    rb = ROWS
    full = lambda a: pl.BlockSpec(a.shape, lambda i, _: (0, 0), pipeline_mode=pl.Buffered(1))
    rowspec = lambda w: pl.BlockSpec((rb, w), lambda i, _: (i, 0))
    return pl.pallas_call(
        functools.partial(mlp_kernel, rows, widths),
        grid_spec=pltpu.PrefetchScalarGridSpec(
            num_scalar_prefetch=1,
            grid=(pl.cdiv(rows, rb),),
            in_specs=[rowspec(d), rowspec(d), rowspec(1)] + [full(a) for a in (gain, bias, upb, downb, *ups, *downs)],
            out_specs=[rowspec(d), rowspec(d), pl.BlockSpec(memory_space=pl.ANY),
                       pl.BlockSpec((8, ff), lambda i, _: (0, 0)), pl.BlockSpec((32, d), lambda i, _: (0, 0))],
            scratch_shapes=[pltpu.VMEM((rb, d), BF16), pltpu.VMEM((rb, d), BF16), pltpu.VMEM((d, rb), BF16), pltpu.VMEM((d, rb), BF16),
                            pltpu.VMEM((rb, d), F32), pltpu.VMEM((rb, d), F32), pltpu.VMEM((d, ff), F32), pltpu.VMEM((d, ff), F32),
                            pltpu.VMEM((2, d, size), BF16), pltpu.SemaphoreType.DMA((2,))]),
        out_shape=[jax.ShapeDtypeStruct((rows, d), BF16), jax.ShapeDtypeStruct((rows, d), BF16),
                   jax.ShapeDtypeStruct((d, 2 * ff), BF16), jax.ShapeDtypeStruct((8, ff), F32), jax.ShapeDtypeStruct((32, d), F32)],
        cost_estimate=cost(170),
        compiler_params=pltpu.CompilerParams(vmem_limit_bytes=VMEM_LIMIT, dimension_semantics=("arbitrary",)),
        name="mlp",
    )(offsets, x1, go, mask, gain, bias, upb, downb, *ups, *downs)


def bits(n):
    return n.bit_length() - 1


def swap(value, axis, bit, sizes):
    return lax.ppermute(value, axis, [(i, i ^ (1 << bit)) for i in range(sizes[axis])])


def bit_of(axis, bit):
    return (lax.axis_index(axis) >> bit) & 1


def add(a, b):
    return (a.astype(F32) + b.astype(F32)).astype(BF16)


def halve_rows(held, at, bit, sizes):
    mine = bit_of("dp", bit)
    keep = lax.dynamic_index_in_dim(held, mine, at, keepdims=False)
    send = lax.dynamic_index_in_dim(held, 1 - mine, at, keepdims=False)
    return add(keep, swap(send, "dp", bit, sizes))


def halve_columns(held, bit, sizes):
    mine = bit_of("mlp", bit) == 1
    half = held.shape[-1] // 2
    low, high = held[..., :half], held[..., half:]
    return add(jnp.where(mine, high, low), swap(jnp.where(mine, low, high), "mlp", bit, sizes))


def reduce_scatter(grad, sizes):
    nb, nm = bits(sizes["dp"]), bits(sizes["mlp"])
    held = grad.reshape((2,) * nb + (grad.shape[0] // sizes["dp"], grad.shape[1]))
    held = halve_rows(held, nb - 1, 0, sizes)
    columns = lambda v: functools.reduce(lambda u, b: halve_columns(u, b, sizes), reversed(range(nm)), v)
    if nb < 3:
        return functools.reduce(lambda u, b: halve_rows(u, b - 1, b, sizes), reversed(range(1, nb)), columns(held))
    first, second = held[0], held[1]
    at = nb - 3
    first = columns(first)
    second = halve_rows(second, at, 1, sizes)
    first = halve_rows(first, at, 1, sizes)
    second = columns(second)
    for b in range(2, nb - 1):
        first, second = (halve_rows(v, nb - 2 - b, b, sizes) for v in (first, second))
    mine = bit_of("dp", nb - 1) == 1
    return add(jnp.where(mine, second, first), swap(jnp.where(mine, first, second), "dp", nb - 1, sizes))


def sum_everywhere(v, sizes):
    for axis in ("dp", "mlp"):
        for b in range(bits(sizes[axis])):
            v = v + swap(v, axis, b, sizes)
    return v


def feed_forward_weights(up, up_bias, down, sizes):
    width = up.shape[1]
    if sizes["mlp"] != 2:
        gather = lambda v: lax.all_gather(v, "mlp", axis=v.ndim - 1, tiled=True)
        count = sizes["mlp"]
        return [gather(up)], [gather(down)], gather(up_bias), jnp.arange(count, dtype=jnp.int32) * width, width
    half = width // 2
    core, me = bit_of("dp", 0), lax.axis_index("mlp")
    cut = lambda v: jnp.where(core == 1, v[:, half:], v[:, :half])
    far_up, far_down = swap(cut(up), "mlp", 0, sizes), swap(cut(down), "mlp", 0, sizes)
    far_bias = swap(up_bias, "mlp", 0, sizes)
    bias = jnp.concatenate([up_bias, jnp.roll(far_bias, -core * half)])
    places = jnp.stack([me * width, me * width + half, (1 - me) * width + core * half, (1 - me) * width + (1 - core) * half])
    return (up, far_up), (down, far_down), bias, places.astype(jnp.int32), half


def per_device(
    sizes,
    tokens,
    window_extent,
    ln1_gain,
    ln1_bias,
    qkv_weight,
    query_bias,
    value_bias,
    rel_h,
    rel_w,
    proj_weight,
    proj_bias,
    ln2_gain,
    ln2_bias,
    up_weight,
    up_bias,
    down_weight,
    down_bias,
    grad_out,
):
    owners = sizes["mlp"]
    line = lambda v: v.reshape(1, -1)
    ups, downs, up_bias_here, places, piece = feed_forward_weights(up_weight, up_bias, down_weight, sizes)
    ohm, oht, shift, mix, relt, valid_rows = small_tables(window_extent, rel_h, rel_w)
    qkv_bias = jnp.concatenate([query_bias, jnp.zeros_like(query_bias), value_bias])
    x1, xhat, qkv, qaug, o, lse = attention_forward(
        tokens, ohm, line(ln1_gain), line(ln1_bias), qkv_weight, line(qkv_bias), mix, shift, proj_weight, line(proj_bias))
    if owners == 2:
        (ups, downs, x1) = lax.optimization_barrier((ups, downs, x1))
        ups, downs = list(ups) + [swap(ups[1], "dp", 0, sizes)], list(downs) + [swap(downs[1], "dp", 0, sizes)]
    width = up_weight.shape[1]
    ff = width * owners
    by_owner = (places // width) * (2 * width) + places % width
    output, da, dw_mlp, up_sums, mid_sums = mlp(
        x1, grad_out, valid_rows, line(ln2_gain), line(ln2_bias), line(up_bias_here), line(down_bias), ups, downs,
        jnp.concatenate([by_owner, by_owner + width]))
    dw_mlp = lax.psum_scatter(dw_mlp, "dp", scatter_dimension=0, tiled=True)
    dw_mlp = lax.psum_scatter(dw_mlp, "mlp", scatter_dimension=1, tiled=True)
    dap, dp_all, grel = attention_backward(da, ohm, oht, qkv, qaug, lse, proj_weight, relt, shift)
    flat = lambda v: v.reshape(-1, v.shape[-1])
    up_sum = jnp.sum(up_sums, axis=0).reshape(-1, piece)
    up_sum = sum(jnp.where(jnp.arange(ff) // piece == places[n] // piece, jnp.tile(up_sum[n], ff // piece), 0.0)
                 for n in range(ff // piece))
    column = lambda v: v.reshape(-1, 1)
    direct = MODEL % (BAND * owners) == 0
    dw_late, dp_sums, gain_sums, bias_sums = weight_gradients(
        flat(xhat), flat(o), flat(dp_all), flat(dap), qkv_weight, column(ln1_gain), column(ln1_bias), owners if direct else 1)
    if not direct:
        split_owner = lambda v: v.reshape(MODEL, owners, -1)
        dw_late = jnp.concatenate([split_owner(dw_late[:, :3 * MODEL]), split_owner(dw_late[:, 3 * MODEL:])], axis=2).reshape(MODEL, -1)
    rel = grel[0, :, :HEAD_DIM] + grel[1, :, HEAD_DIM:]
    mid = jnp.sum(mid_sums.reshape(4, 8, MODEL), axis=1)
    sums = jnp.concatenate([jnp.sum(gain_sums, axis=1), jnp.sum(bias_sums, axis=1), dp_sums[0], rel.reshape(-1), mid.reshape(-1), up_sum])
    sums = sum_everywhere(sums, sizes)
    late = reduce_scatter(dw_late, sizes).astype(F32)
    grad_tokens = None
    blocks = dp_all.shape[0] // block_windows(dp_all.shape[0])
    for n in range(blocks):
        grad_tokens = input_gradient(tokens, da, dp_all, line(ln1_gain), qkv_weight, n, 1, grad_tokens)
    d = MODEL
    table = 2 * WIN - 1
    n_rel = 64 * HEAD_DIM
    rel = sums[5 * d:5 * d + n_rel].reshape(64, HEAD_DIM)
    mid = sums[5 * d + n_rel:]
    cols = 3 * MODEL // owners
    dw_mlp = dw_mlp.astype(F32)
    return (
        output,
        grad_tokens,
        sums[0:d],
        sums[d:2 * d],
        late[:, :cols],
        sums[2 * d:3 * d],
        sums[4 * d:5 * d],
        rel[0:table][::-1],
        rel[32:32 + table][::-1],
        late[:, cols:],
        mid[3 * d:4 * d],
        mid[d:2 * d],
        mid[2 * d:3 * d],
        dw_mlp[:, :width],
        mid[4 * d:],
        dw_mlp[:, width:],
        mid[0:d],
    )


def solution(mesh):
    rows = P(("dp", "mlp"), None)
    in_specs = (rows, rows, P(), P(), P(), P(), P(), P(), P(), P(), P(), P(), P(),
                P(None, "mlp"), P("mlp"), P(None, "mlp"), P(), rows)
    block = P("dp", "mlp")
    out_specs = (rows, rows, P(), P(), block, P(), P(), P(), P(), block, P(), P(), P(), block, P(), block, P())
    sizes = {name: mesh.shape[name] for name in ("dp", "mlp")}
    return jax.shard_map(
        functools.partial(per_device, sizes), mesh=mesh, in_specs=in_specs, out_specs=out_specs, check_vma=False)
```

time: 678 us -> 522 us (0.77)
  Pallas kernels: 497 us -> 415 us
  blocking collectives: 45.3 us -> 0 us
  matrix products: 29.5 us -> 0 us
  local copies, waits for them, and re-layouts: 35.3 us -> 24.8 us
  starting transfers between devices: 7.22 us -> 17.7 us
  other arithmetic: 23 us -> 13 us
    pallas_call x1, Pallas kernels: 158 us -> 70.6 us  [attention_backward(): pl.pallas_call(backward_kernel, grid=(windows // wb,), in_specs=[blocked(...]
    pallas_call x2 -> x7, Pallas kernels: 201 us -> 272 us  [the longest x1 185 us: mlp(): pl.pallas_call(functools.partial(mlp_kernel, rows, widths), grid_spec=plt...]
    pallas_call x1, Pallas kernels: 138 us -> 71.8 us  [attention_forward(): pl.pallas_call(forward_kernel, grid=(windows // wb,), in_specs=[blocked(w...]
    psum x1 -> x0, blocking collectives: 39.9 us -> none  [per_device(): sums = lax.psum(sums, ('dp', 'mlp'))]
    dot_general x2 -> x0, matrix products: 29.5 us -> none  [mm(): return lax.dot_general(a, b, dims, preferred_element_type=F32)]
    ppermute x5 -> x18, waiting for transfers between devices: 15.7 us -> 30.2 us  [swap(): lax.ppermute(value, axis, [(i, i ^ 1 << bit) for i in range(sizes[axis])])]
    reshape x9 -> x3, local copies, waits for them, and re-layouts: 13.1 us -> 1.85 us  [the longest x2 1.84 us: per_device(): column = lambda v: v.reshape(-1, 1)]
    ppermute x5 -> x18, starting transfers between devices: 6.84 us -> 17.6 us  [swap(): lax.ppermute(value, axis, [(i, i ^ 1 << bit) for i in range(sizes[axis])])]
  transfers between devices with their start and end apart: 9 -> 20, of which waited for: 4 -> 6; matrix products, arithmetic and copies ran while one was open for 11% -> 6% of each run, Pallas kernels for 48% -> 45%
where the time goes in v2:
time: 522 us; the launch traced here: 515 us
  Pallas kernels  415 us (80%)
  waiting for transfers between devices  30.2 us (6%)
  local copies, waits for them, and re-layouts  24.8 us (5%)
  starting transfers between devices  17.7 us (3%)
  between operations  15.1 us (3%)
  other arithmetic  13 us (2%)
    pallas_call x1, Pallas kernels, mlp(): pl.pallas_call(functools.partial(mlp_kernel, rows, widths), grid_spec=plt...  185 us
    pallas_call x1, Pallas kernels, attention_forward(): pl.pallas_call(forward_kernel, grid=(windows // wb,), in_specs=[blocked(w...  71.8 us
    pallas_call x1, Pallas kernels, attention_backward(): pl.pallas_call(backward_kernel, grid=(windows // wb,), in_specs=[blocked(...  70.6 us
    pallas_call x5, Pallas kernels, input_gradient(): pl.pallas_call(input_kernel, grid=(count,), in_specs=[part(wb * AREA, MOD...  44.9 us
    pallas_call x1, Pallas kernels, weight_gradients(): pl.pallas_call(weight_kernel, grid=(nq + np_,), in_specs=[once(xhat), onc...  42 us
    ppermute x18, waiting for transfers between devices, swap(): lax.ppermute(value, axis, [(i, i ^ 1 << bit) for i in range(sizes[axis])])  30.2 us
    ppermute x18, starting transfers between devices, swap(): lax.ppermute(value, axis, [(i, i ^ 1 << bit) for i in range(sizes[axis])])  17.6 us
  transfers between devices with their start and end apart: 20, of which 6 were waited for; matrix products, arithmetic and copies ran while one was open for 6% of the time, Pallas kernels for 45%

profile of v2, /device:TPU:0, one launch (start us, length us, event | category | flops | bytes accessed | tf_op | source)
XLA Modules:
  0.0 515.4 jit_solution(11230717099444964137)
XLA Ops:
  7.3 1.9 slice_select_fusion.1
  9.2 3.0 collective-permute-start
  23.8 71.8 %attention_forward.1 = (f32[3920,768]{1,0:T(8,128)}, bf16[20,208,768]{2,1,0:T(8,128)(2,1)}, bf16[20,208,2304]{2,1,0:T(8,128)(2,1)}, bf16[20,6,256,208]{3,2,1,0:T...) custom-call(bf16[3920,768]{1,0:T(8,128)(2,1)} %x_ref.11, ...), custom_call_target="tpu_custom_call" | custom-call | flops 70000001024 | bytes 1048576 | tf_op jit(solution)/shard_map/attention_forward/pallas_call | solution.py:164
  96.3 1.7 collective-permute-start.2
  101.9 1.9 reshape.458.mask_ref
  107.2 185.2 %mlp.1 = (bf16[3920,768]{1,0:T(8,128)(2,1)}, bf16[3920,768]{1,0:T(8,128)(2,1)}, bf16[768,6144]{1,0:T(8,128)(2,1)}, f32[8,3072]{1,0:T(8,128)}, f32[32,768]{1,0:T(8,128)}) custom-call(s32[8]{0:T(128)} %pad_add_fusion.1.offset_ref, f32[3920,768]{1,0:T(8,128)} %get-tuple-element.41.x1_ref, bf16[3920,768]{1,0:T(8,128)(2,1)} %go_ref.1, ...), custom_call_target="tpu_custom_call" | custom-call | flops 170000007168 | bytes 1048576 | tf_op jit(solution)/shard_map/mlp/pallas_call | solution.py:506
  292.5 70.6 %attention_backward.1 = (bf16[20,208,768]{2,1,0:T(8,128)(2,1)}, bf16[20,208,2304]{2,1,0:T(8,128)(2,1)}, f32[2,64,128]{2,1,0:T(8,128)}) custom-call(bf16[3920,768]{1,0:T(8,128)(2,1)} %get-tuple-element.47.da_ref, bf16[20,208,128]{2,1,0:T(8,128)(2,1)} %pad_maximum_fusion.ohm_ref, bf16[32,208]{1,0:T(8,128)(2,1)} %maximum_bitcast_fusion.oht_ref, ...), custom_call_target="tpu_custom_call" | custom-call | flops 70000001024 | bytes 1048576 | tf_op jit(solution)/shard_map/attention_backward/pallas_call | solution.py:249
  363.1 42.0 %weight_gradients.1 = (bf16[768,3072]{1,0:T(8,128)(2,1)}, f32[8,2304]{1,0:T(8,128)}, f32[768,128]{1,0:T(8,128)}, f32[768,128]{1,0:T(8,128)}) custom-call(bf16[4160,768]{1,0:T(8,128)(2,1)} %bitcast.61, bf16[4160,768]{1,0:T(8,128)(2,1)} %bitcast.62, bf16[4160,2304]{1,0:T(8,128)(2,1)} %bitcast.58, bf16[4160,768]{1,0:T(8,128)(2,1)} %bitcast.63, ...), custom_call_target="tpu_custom_call" | custom-call | flops 20000000000 | bytes 1048576 | tf_op jit(solution)/shard_map/weight_gradients/pallas_call | solution.py:346
  405.1 2.8 constant_dynamic-slice_fusion.1
  411.9 8.9 %input_gradient.5.rest_0_ = bf16[3920,768]{1,0:T(8,128)(2,1)} custom-call(bf16[3920,768]{1,0:T(8,128)(2,1)} %x_ref.11, bf16[3920,768]{1,0:T(8,128)(2,1)} %get-tuple-element.47.da_ref, bf16[20,208,2304]{2,1,0:T(8,128)(2,1)} %get-tuple-element.51.dp_ref, f32[1,768]{1,0:T(1,128)} %reshape.435.gain_ref, bf16[768,2304]{1,0:T(8,128)(2,1)} %w_ref.1), custom_call_target="tpu_custom_call" | custom-call | flops 5000000000 | bytes 1048576 | tf_op jit(solution)/shard_map/input_gradient/pallas_call | solution.py:286
  420.8 1.6 collective-permute-start.6
  422.5 8.9 %input_gradient.6.rest_0_ = bf16[3920,768]{1,0:T(8,128)(2,1)} custom-call(bf16[3920,768]{1,0:T(8,128)(2,1)} %x_ref.11, bf16[3920,768]{1,0:T(8,128)(2,1)} %get-tuple-element.47.da_ref, bf16[20,208,2304]{2,1,0:T(8,128)(2,1)} %get-tuple-element.51.dp_ref, f32[1,768]{1,0:T(1,128)} %reshape.435.gain_ref, ...), custom_call_target="tpu_custom_call", output_to_operand_aliasing={{}: (5, {})} | custom-call | flops 5000000000 | bytes 1048576 | tf_op jit(solution)/shard_map/input_gradient/pallas_call | solution.py:286
  432.9 8.9 %input_gradient.7.rest_0_ = bf16[3920,768]{1,0:T(8,128)(2,1)} custom-call(bf16[3920,768]{1,0:T(8,128)(2,1)} %x_ref.11, bf16[3920,768]{1,0:T(8,128)(2,1)} %get-tuple-element.47.da_ref, bf16[20,208,2304]{2,1,0:T(8,128)(2,1)} %get-tuple-element.51.dp_ref, f32[1,768]{1,0:T(1,128)} %reshape.435.gain_ref, ...), custom_call_target="tpu_custom_call", output_to_operand_aliasing={{}: (5, {})} | custom-call | flops 5000000000 | bytes 1048576 | tf_op jit(solution)/shard_map/input_gradient/pallas_call | solution.py:286
  441.8 2.6 collective-permute-start.8
  444.5 9.2 %input_gradient.8.rest_0_ = bf16[3920,768]{1,0:T(8,128)(2,1)} custom-call(bf16[3920,768]{1,0:T(8,128)(2,1)} %x_ref.11, bf16[3920,768]{1,0:T(8,128)(2,1)} %get-tuple-element.47.da_ref, bf16[20,208,2304]{2,1,0:T(8,128)(2,1)} %get-tuple-element.51.dp_ref, f32[1,768]{1,0:T(1,128)} %reshape.435.gain_ref, ...), custom_call_target="tpu_custom_call", output_to_operand_aliasing={{}: (5, {})} | custom-call | flops 5000000000 | bytes 1048576 | tf_op jit(solution)/shard_map/input_gradient/pallas_call | solution.py:286
  454.3 2.6 fusion
  458.6 8.9 %input_gradient.9 = bf16[3920,768]{1,0:T(8,128)(2,1)} custom-call(bf16[3920,768]{1,0:T(8,128)(2,1)} %x_ref.11, bf16[3920,768]{1,0:T(8,128)(2,1)} %get-tuple-element.47.da_ref, bf16[20,208,2304]{2,1,0:T(8,128)(2,1)} %get-tuple-element.51.dp_ref, f32[1,768]{1,0:T(1,128)} %reshape.435.gain_ref, ...), custom_call_target="tpu_custom_call", output_to_operand_aliasing={{}: (5, {})} | custom-call | flops 5000000000 | bytes 1048576 | tf_op jit(solution)/shard_map/input_gradient/pallas_call | solution.py:286
  468.2 3.1 collective-permute-done.14
  472.2 11.8 %collective-permute-done.11 = bf16[2,48,3072]{2,1,0:T(8,128)(2,1)S(1)} collective-permute-done((bf16[2,48,3072]{2,1,0:T(8,128)(2,1)S(1)}, bf16[2,48,3072]{2,1,0:T(8,128)(2,1)S(1)}, u32[]{:S(2)}, u32[]{:S(2)}) %collective-permute-start.11) | collective-permute-done | bytes 589856 | tf_op jit(solution)/shard_map/ppermute | solution.py:530
  484.8 3.1 collective-permute-done.15
  488.7 2.3 collective-permute-done.12
  493.8 3.7 collective-permute-done.13
  498.6 6.2 %collective-permute-done.17 = bf16[48,1536]{1,0:T(8,128)(2,1)S(1)} collective-permute-done((bf16[48,1536]{1,0:T(8,128)(2,1)S(1)}, bf16[48,1536]{1,0:T(8,128)(2,1)S(1)}, u32[]{:S(2)}, u32[]{:S(2)}) %collective-permute-start.17) | collective-permute-done | bytes 147488 | tf_op jit(solution)/shard_map/ppermute | solution.py:530
  506.2 1.8 fusion.59
  (166 shorter events, 35.6 us)
Async XLA Ops:
  7.2 484.6 %reduce-scatter.3.cloned.1.call-start = ((), (), s32[]{:S(2)}) async-start(), calls=%async_computation.2 | async-start | bytes 10027008 | tf_op jit(solution)/shard_map/reduce_scatter | solution.py:634
  9.2 10.2 %copy-start.8 = (f32[768]{0:T(1024)S(1)}, f32[768]{0:T(1024)}, u32[]{:S(2)}) copy-start(f32[768]{0:T(1024)} %param.21) | copy-start | bytes 9220
  9.2 10.8 %copy-start.10 = (f32[768]{0:T(1024)S(1)}, f32[768]{0:T(1024)}, u32[]{:S(2)}) copy-start(f32[768]{0:T(1024)} %param.28) | copy-start | bytes 9220
  9.2 86.5 %collective-permute-start = (bf16[768,768]{1,0:T(8,128)(2,1)S(1)}, bf16[768,768]{1,0:T(8,128)(2,1)}, u32[]{:S(2)}, u32[]{:S(2)}) collective-permute-start(bf16[768,768]{1,0:T(8,128)(2,1)S(1)} %slice_select_fusion.1), channel_id=1, source_target_pairs={{0,1},{1,0},{2,3},{3,2},{4,5},{5,4},{6,7},{7,6},{8,9},{9,8},{10,11... | collective-permute-start | bytes 3538952 | tf_op jit(solution)/shard_map/ppermute | solution.py:530
  13.3 82.3 %collective-permute-start.1 = (bf16[768,768]{1,0:T(8,128)(2,1)}, bf16[768,768]{1,0:T(8,128)(2,1)S(1)}, u32[]{:S(2)}, u32[]{:S(2)}) collective-permute-start(bf16[768,768]{1,0:T(8,128)(2,1)} %slice_select_fusion), channel_id=1, source_target_pairs={{0,1},{1,0},{2,3},{3,2},{4,5},{5,4},{6,7},{7,6},{8,9},{9,8},{10,11... | collective-permute-start | bytes 3538952 | tf_op jit(solution)/shard_map/ppermute | solution.py:530
  23.8 72.5 %copy-start.9 = (f32[1536]{0:T(1024)S(1)}, f32[1536]{0:T(1024)}, u32[]{:S(2)}) copy-start(f32[1536]{0:T(1024)} %param.32) | copy-start | bytes 18436
  95.7 10.6 %copy-start.15 = (bf16[768,768]{1,0:T(8,128)(2,1)}, bf16[768,768]{1,0:T(8,128)(2,1)S(1)}, u32[]{:S(2)}) copy-start(bf16[768,768]{1,0:T(8,128)(2,1)S(1)} %collective-permute-done.1.rest_4_) | copy-start | bytes 3538948
  95.7 10.5 %collective-permute-start.3 = (bf16[768,768]{1,0:T(8,128)(2,1)}, bf16[768,768]{1,0:T(8,128)(2,1)S(1)}, u32[]{:S(2)}, u32[]{:S(2)}) collective-permute-start(bf16[768,768]{1,0:T(8,128)(2,1)} %collective-permute-done.rest_1_), channel_id=1, source_target_pairs={{0,2},{2,0},{4,6},{6,4},{8,10},{10,8},{12,14},{14,12},{16,18},{18,... | collective-permute-start | bytes 3538952 | tf_op jit(solution)/shard_map/ppermute | solution.py:530
  95.8 10.5 %collective-permute-start.4 = (bf16[768,768]{1,0:T(8,128)(2,1)S(1)}, bf16[768,768]{1,0:T(8,128)(2,1)}, u32[]{:S(2)}, u32[]{:S(2)}) collective-permute-start(bf16[768,768]{1,0:T(8,128)(2,1)S(1)} %collective-permute-done.1.rest_4_), channel_id=1, source_target_pairs={{0,2},{2,0},{4,6},{6,4},{8,10},{10,8},{12,14},{14,12},{16,18},{18,... | collective-permute-start | bytes 3538952 | tf_op jit(solution)/shard_map/ppermute | solution.py:530
  96.3 9.3 %collective-permute-start.2 = (f32[1536]{0:T(1024)S(1)}, f32[1536]{0:T(1024)S(1)}, u32[]{:S(2)}, u32[]{:S(2)}) collective-permute-start(f32[1536]{0:T(1024)S(1)} %copy-done.9), channel_id=1, source_target_pairs={{0,1},{1,0},{2,3},{3,2},{4,5},{5,4},{6,7},{7,6},{8,9},{9,8},{10,11... | collective-permute-start | bytes 18440 | tf_op jit(solution)/shard_map/ppermute | solution.py:530
  292.4 213.8 %reduce-scatter.5.cloned.1.call-start = ((), (), s32[]{:S(2)}) async-start(), calls=%async_computation.3 | async-start | bytes 884736 | tf_op jit(solution)/shard_map/reduce_scatter | solution.py:635
  409.5 44.8 %collective-permute-start.10 = (bf16[2,2,2,48,3072]{4,3,1,2,0:T(8,128)(2,1)}, bf16[2,2,2,48,3072]{4,3,1,2,0:T(8,128)(2,1)}, u32[]{:S(2)}, u32[]{:S(2)}) collective-permute-start(bf16[2,2,2,48,3072]{4,3,1,2,0:T(8,128)(2,1)} %bitcast.57), channel_id=1, source_target_pairs={{0,2},{2,0},{4,6},{6,4},{8,10},{10,8},{12,14},{14,12},{16,18},{18,... | collective-permute-start | bytes 7077896 | tf_op jit(solution)/shard_map/ppermute | solution.py:530
  411.3 9.5 %collective-permute-start.5 = (f32[14080]{0:T(1024)S(1)}, f32[14080]{0:T(1024)S(1)}, u32[]{:S(2)}, u32[]{:S(2)}) collective-permute-start(f32[14080]{0:T(1024)S(1)} %add_dynamic-update-slice_fusion), channel_id=1, source_target_pairs={{0,2},{2,0},{4,6},{6,4},{8,10},{10,8},{12,14},{14,12},{16,18},{18,... | collective-permute-start | bytes 168968 | tf_op jit(solution)/shard_map/ppermute | solution.py:530
  420.8 10.6 %collective-permute-start.6 = (f32[14080]{0:T(1024)S(1)}, f32[14080]{0:T(1024)S(1)}, u32[]{:S(2)}, u32[]{:S(2)}) collective-permute-start(f32[14080]{0:T(1024)S(1)} %add.235), channel_id=1, source_target_pairs={{0,4},{2,6},{4,0},{6,2},{8,12},{10,14},{12,8},{14,10},{16,20},{18,... | collective-permute-start | bytes 168968 | tf_op jit(solution)/shard_map/ppermute | solution.py:530
  431.4 10.4 %collective-permute-start.7 = (f32[14080]{0:T(1024)S(1)}, f32[14080]{0:T(1024)S(1)}, u32[]{:S(2)}, u32[]{:S(2)}) collective-permute-start(f32[14080]{0:T(1024)S(1)} %add.236), channel_id=1, source_target_pairs={{0,8},{2,10},{4,12},{6,14},{8,0},{10,2},{12,4},{14,6},{16,24},{18,... | collective-permute-start | bytes 168968 | tf_op jit(solution)/shard_map/ppermute | solution.py:530
  441.8 11.8 %collective-permute-start.8 = (f32[14080]{0:T(1024)S(1)}, f32[14080]{0:T(1024)S(1)}, u32[]{:S(2)}, u32[]{:S(2)}) collective-permute-start(f32[14080]{0:T(1024)S(1)} %add.237), channel_id=1, source_target_pairs={{0,16},{2,18},{4,20},{6,22},{8,24},{10,26},{12,28},{14,30},{16,0},... | collective-permute-start | bytes 168968 | tf_op jit(solution)/shard_map/ppermute | solution.py:530
  453.7 13.9 %collective-permute-start.9 = (f32[14080]{0:T(1024)S(1)}, f32[14080]{0:T(1024)S(1)}, u32[]{:S(2)}, u32[]{:S(2)}) collective-permute-start(f32[14080]{0:T(1024)S(1)} %add.238), channel_id=1, source_target_pairs={{0,1},{1,0},{2,3},{3,2},{4,5},{5,4},{6,7},{7,6},{8,9},{9,8},{10,11... | collective-permute-start | bytes 168968 | tf_op jit(solution)/shard_map/ppermute | solution.py:530
  457.1 14.2 %collective-permute-start.14 = (bf16[2,2,48,1536]{3,2,0,1:T(8,128)(2,1)S(1)}, bf16[2,2,48,1536]{3,2,0,1:T(8,128)(2,1)S(1)}, u32[]{:S(2)}, u32[]{:S(2)}) collective-permute-start(bf16[2,2,48,1536]{3,2,0,1:T(8,128)(2,1)S(1)} %broadcast_select_fusion), channel_id=1, source_target_pairs={{0,1},{1,0},{2,3},{3,2},{4,5},{5,4},{6,7},{7,6},{8,9},{9,8},{10,11... | collective-permute-start | bytes 1769480 | tf_op jit(solution)/shard_map/ppermute | solution.py:530
  467.6 16.3 %collective-permute-start.11 = (bf16[2,48,3072]{2,1,0:T(8,128)(2,1)S(1)}, bf16[2,48,3072]{2,1,0:T(8,128)(2,1)S(1)}, u32[]{:S(2)}, u32[]{:S(2)}) collective-permute-start(bf16[2,48,3072]{2,1,0:T(8,128)(2,1)S(1)} %dynamic-slice_bitcast_fusion), channel_id=1, source_target_pairs={{0,4},{2,6},{4,0},{6,2},{8,12},{10,14},{12,8},{14,10},{16,20},{18,... | collective-permute-start | bytes 1769480 | tf_op jit(solution)/shard_map/ppermute | solution.py:530
  471.6 16.3 %collective-permute-start.15 = (bf16[2,48,1536]{2,1,0:T(8,128)(2,1)S(1)}, bf16[2,48,1536]{2,1,0:T(8,128)(2,1)S(1)}, u32[]{:S(2)}, u32[]{:S(2)}) collective-permute-start(bf16[2,48,1536]{2,1,0:T(8,128)(2,1)S(1)} %dynamic-slice_bitcast_fusion.1), channel_id=1, source_target_pairs={{0,4},{2,6},{4,0},{6,2},{8,12},{10,14},{12,8},{14,10},{16,20},{18,... | collective-permute-start | bytes 884744 | tf_op jit(solution)/shard_map/ppermute | solution.py:530
  484.2 6.8 %collective-permute-start.12 = (bf16[2,48,1536]{2,1,0:T(8,128)(2,1)S(1)}, bf16[2,48,1536]{2,1,0:T(8,128)(2,1)S(1)}, u32[]{:S(2)}, u32[]{:S(2)}) collective-permute-start(bf16[2,48,1536]{2,1,0:T(8,128)(2,1)S(1)} %broadcast_select_fusion.1), channel_id=1, source_target_pairs={{0,1},{1,0},{2,3},{3,2},{4,5},{5,4},{6,7},{7,6},{8,9},{9,8},{10,11... | collective-permute-start | bytes 884744 | tf_op jit(solution)/shard_map/ppermute | solution.py:530
  488.0 5.8 %collective-permute-start.16 = (bf16[48,1536]{1,0:T(8,128)(2,1)S(1)}, bf16[48,1536]{1,0:T(8,128)(2,1)S(1)}, u32[]{:S(2)}, u32[]{:S(2)}) collective-permute-start(bf16[48,1536]{1,0:T(8,128)(2,1)S(1)} %dynamic-slice_bitcast_fusion.2), channel_id=1, source_target_pairs={{0,8},{2,10},{4,12},{6,14},{8,0},{10,2},{12,4},{14,6},{16,24},{18,... | collective-permute-start | bytes 442376 | tf_op jit(solution)/shard_map/ppermute | solution.py:530
  491.1 6.4 %collective-permute-start.13 = (bf16[48,1536]{1,0:T(8,128)(2,1)S(1)}, bf16[48,1536]{1,0:T(8,128)(2,1)S(1)}, u32[]{:S(2)}, u32[]{:S(2)}) collective-permute-start(bf16[48,1536]{1,0:T(8,128)(2,1)S(1)} %dynamic-slice_bitcast_fusion.3), channel_id=1, source_target_pairs={{0,8},{2,10},{4,12},{6,14},{8,0},{10,2},{12,4},{14,6},{16,24},{18,... | collective-permute-start | bytes 442376 | tf_op jit(solution)/shard_map/ppermute | solution.py:530
  497.6 7.2 %collective-permute-start.17 = (bf16[48,1536]{1,0:T(8,128)(2,1)S(1)}, bf16[48,1536]{1,0:T(8,128)(2,1)S(1)}, u32[]{:S(2)}, u32[]{:S(2)}) collective-permute-start(bf16[48,1536]{1,0:T(8,128)(2,1)S(1)} %broadcast_select_fusion.2), channel_id=1, source_target_pairs={{0,16},{2,18},{4,20},{6,22},{8,24},{10,26},{12,28},{14,30},{16,0},... | collective-permute-start | bytes 442376 | tf_op jit(solution)/shard_map/ppermute | solution.py:530
  (13 other events, 62.7 us)
Sparse Core Ops, SparseCore 0:
  292.6 111.7 reduce-scatter.2
  491.9 12.4 reduce-scatter.4

commit v3 on v2

--- a/solution.py
+++ b/solution.py
@@ -1,6 +1,7 @@
 import functools
 import jax
 import jax.numpy as jnp
+import numpy as np
 from jax import lax
 from jax.experimental import pallas as pl
 from jax.experimental.pallas import tpu as pltpu
@@ -23,6 +24,7 @@
 TN = (((0,), (0,)), ((), ()))
 TOGETHER = 6
 TOGETHER_BACK = 6
+LN1_GAIN, LN1_BIAS, QUERY_BIAS, VALUE_BIAS, PROJ_BIAS, LN2_GAIN, LN2_BIAS, DOWN_BIAS = (slice(n, n + 1) for n in range(8))
 VMEM_LIMIT = 60 * 1024 * 1024
 
 
@@ -68,8 +70,8 @@
     return jnp.concatenate(([own, z] if h == 0 else [z, own]) + [bias, z], axis=0)
 
 
-def forward_kernel(x_ref, ohm_ref, gain_ref, bias_ref, wqkv_ref, qkvb_ref, mix_ref, shift_ref, wproj_ref, projb_ref,
-                   x1_ref, xhat_ref, qkv_ref, qaug_ref, o_ref, lse_ref, h1_ref, wide):
+def forward_kernel(x_ref, ohm_ref, vec_ref, wqkv_ref, mix_ref, shift_ref, wproj_ref,
+                   x1_ref, xhat_ref, qkv_ref, qaug_ref, o_ref, lse_ref, mask_ref, h1_ref, wide):
     wb = ohm_ref.shape[0]
     for w in range(wb):
         x = x_ref[AREA * w:AREA * (w + 1), :].astype(F32)
@@ -77,13 +79,14 @@
         xhat = c * r
         h1_ref[w, PADDED - 16:, :] = jnp.zeros((16, MODEL), BF16)
         xhat_ref[w, PADDED - 16:, :] = jnp.zeros((16, MODEL), BF16)
-        h1_ref[w, 0:AREA, :] = (xhat * gain_ref[...] + bias_ref[...]).astype(BF16)
+        h1_ref[w, 0:AREA, :] = (xhat * vec_ref[LN1_GAIN] + vec_ref[LN1_BIAS]).astype(BF16)
+        mask_ref[AREA * w:AREA * (w + 1), :] = jnp.where(ohm_ref[w, 0:AREA, 14:15] < 0.0, 0.0, 1.0)
         xhat_ref[w, 0:AREA, :] = xhat.astype(BF16)
 
-    @pl.loop(0, 3)
-    def _(j):
-        cs = pl.ds(pl.multiple_of(j * MODEL, MODEL), MODEL)
-        p = mm(h1_ref[...].reshape(wb * PADDED, MODEL), wqkv_ref[:, cs]) + qkvb_ref[:, cs]
+    for j, offset in enumerate((QUERY_BIAS, None, VALUE_BIAS)):
+        cs = slice(j * MODEL, (j + 1) * MODEL)
+        p = mm(h1_ref[...].reshape(wb * PADDED, MODEL), wqkv_ref[:, cs])
+        p = p if offset is None else p + vec_ref[offset]
         qkv_ref[:, :, cs] = p.astype(BF16).reshape(wb, PADDED, MODEL)
 
     groups = PAIRS // TOGETHER
@@ -131,7 +134,7 @@
             ot = jnp.concatenate(ots[2 * n:2 * n + 2], axis=0).astype(BF16)
             o_ref[w, :, lanes(0, p)] = mm(eye(PADDED), ot, NT).astype(BF16)
 
-    wide[...] = mm(o_ref[...].reshape(wb * PADDED, MODEL), wproj_ref[...]) + projb_ref[...]
+    wide[...] = mm(o_ref[...].reshape(wb * PADDED, MODEL), wproj_ref[...]) + vec_ref[PROJ_BIAS]
     for w in range(wb):
         x1_ref[AREA * w:AREA * (w + 1), :] = x_ref[AREA * w:AREA * (w + 1), :].astype(F32) + wide[PADDED * w:PADDED * w + AREA, :]
 
@@ -152,7 +155,7 @@
     return 4 if windows % 4 == 0 else windows
 
 
-def attention_forward(x, ohm, gain, bias, wqkv, qkvb, mix, shift, wproj, projb):
+def attention_forward(x, ohm, vec, wqkv, mix, shift, wproj):
     windows = ohm.shape[0]
     wb = block_windows(windows)
     outs = [((windows * AREA, MODEL), F32, (wb * AREA, MODEL)),
@@ -160,32 +163,45 @@
             ((windows, PADDED, 3 * MODEL), BF16, (wb, PADDED, 3 * MODEL)),
             ((windows, PAIRS, 256, PADDED), BF16, (wb, PAIRS, 256, PADDED)),
             ((windows, PADDED, MODEL), BF16, (wb, PADDED, MODEL)),
-            ((windows, PAIRS, 2, PADDED), F32, (wb, PAIRS, 2, PADDED))]
+            ((windows, PAIRS, 2, PADDED), F32, (wb, PAIRS, 2, PADDED)),
+            ((windows * AREA, 1), F32, (wb * AREA, 1))]
     return pl.pallas_call(
         forward_kernel,
         grid=(windows // wb,),
-        in_specs=[blocked(wb * AREA, MODEL), blocked(wb, PADDED, 128)] + [once(a) for a in (gain, bias, wqkv, qkvb, mix, shift, wproj, projb)],
+        in_specs=[blocked(wb * AREA, MODEL), blocked(wb, PADDED, 128)] + [once(a) for a in (vec, wqkv, mix, shift, wproj)],
         out_specs=[blocked(*b) for _, _, b in outs],
         out_shape=[jax.ShapeDtypeStruct(s, t) for s, t, _ in outs],
         scratch_shapes=[pltpu.VMEM((wb, PADDED, MODEL), BF16), pltpu.VMEM((wb * PADDED, MODEL), F32)],
         cost_estimate=cost(70),
         compiler_params=pltpu.CompilerParams(vmem_limit_bytes=VMEM_LIMIT, dimension_semantics=("arbitrary",)),
         name="attention_forward",
-    )(x, ohm, gain, bias, wqkv, qkvb, mix, shift, wproj, projb)
-
-
-def backward_kernel(da_ref, ohm_ref, oht_ref, qkv_ref, qaug_ref, lse_ref, wproj_ref, relt_ref, shift_ref,
-                    dap_ref, dp_ref, grel_ref, do_ref):
+    )(x, ohm, vec, wqkv, mix, shift, wproj)
+
+
+BLOCK = 384
+BLOCKS = 4 * MODEL // BLOCK
+
+
+def backward_kernel(da_ref, ohm_ref, oht_ref, qkv_ref, qaug_ref, lse_ref, wproj_ref, relt_ref, shift_ref, xhat_ref, o_ref, vec_ref,
+                    wqkv_ref, dp_ref, grel_ref, dw_ref, sum_ref, gvec_ref, bvec_ref,
+                    do_ref, dap_ref, turned, acc, wstage, dstage, wsems, dsems):
     wb = ohm_ref.shape[0]
-
-    @pl.when(pl.program_id(0) == 0)
+    rows = wb * PADDED
+    step = pl.program_id(0)
+
+    @pl.when(step == 0)
     def _():
         grel_ref[...] = jnp.zeros_like(grel_ref)
+        acc[...] = jnp.zeros_like(acc)
+        turned[MODEL:, :] = jnp.ones((16, rows), BF16)
 
     for w in range(wb):
         dap_ref[w, PADDED - 16:, :] = jnp.zeros((16, MODEL), BF16)
         dap_ref[w, 0:AREA, :] = da_ref[AREA * w:AREA * (w + 1), :]
-    do_ref[...] = mm(dap_ref[...].reshape(wb * PADDED, MODEL), wproj_ref[...], NT).astype(BF16).reshape(wb, PADDED, MODEL)
+    dap = dap_ref[...].reshape(rows, MODEL)
+    do_ref[...] = mm(dap, wproj_ref[...], NT).astype(BF16).reshape(wb, PADDED, MODEL)
+    turned[0:MODEL, :] = o_ref[...].reshape(rows, MODEL).T
+    acc[0:MODEL, 3 * MODEL:] += mm(turned[0:MODEL, :], dap)
 
     groups = PAIRS // TOGETHER_BACK
 
@@ -242,27 +258,69 @@
             dp_ref[w, :, lanes(1, p)] = dk
             dp_ref[w, :, lanes(2, p)] = dv
 
-
-def attention_backward(da, ohm, oht, qkv, qaug, lse, wproj, relt, shift):
+    turned[0:MODEL, :] = xhat_ref[...].reshape(rows, MODEL).T
+    for j in range(3):
+        cs = slice(j * MODEL, (j + 1) * MODEL)
+        acc[:, cs] += mm(turned[...], dp_ref[:, :, cs].reshape(rows, MODEL))
+
+    @pl.when(step == pl.num_programs(0) - 1)
+    def _():
+        columns = jnp.concatenate([vec_ref[...]] * 16, axis=0).T
+        gain, bias = columns[:, 0:1], columns[:, 1:2]
+        nq = 3 * MODEL // BLOCK
+        sum_ref[...] = acc[MODEL:MODEL + 8, 0:3 * MODEL]
+        gvec_ref[...] = jnp.zeros_like(gvec_ref)
+        bvec_ref[...] = jnp.zeros_like(bvec_ref)
+        take = lambda n: pltpu.make_async_copy(wqkv_ref.at[:, pl.ds(n * BLOCK, BLOCK)], wstage.at[n % 2], wsems.at[n % 2])
+        give = lambda n: pltpu.make_async_copy(dstage.at[n % 2], dw_ref.at[n], dsems.at[n % 2])
+        take(0).start()
+        for n in range(BLOCKS):
+            cs = slice(n * BLOCK, (n + 1) * BLOCK)
+            if n + 1 < nq:
+                take(n + 1).start()
+            if n >= 2:
+                give(n - 2).wait()
+            m = acc[0:MODEL, cs]
+            if n < nq:
+                s = acc[MODEL:MODEL + 1, cs]
+                take(n).wait()
+                w = wstage[n % 2].astype(F32)
+                g, b = w * m, w * s
+                gvec_ref[...] += sum(g[:, 128 * i:128 * (i + 1)] for i in range(BLOCK // 128))
+                bvec_ref[...] += sum(b[:, 128 * i:128 * (i + 1)] for i in range(BLOCK // 128))
+                m = m * gain + bias * s
+            dstage[n % 2] = m.astype(BF16)
+            give(n).start()
+        give(BLOCKS - 2).wait()
+        give(BLOCKS - 1).wait()
+
+
+def attention_backward(da, ohm, oht, qkv, qaug, lse, wproj, relt, shift, xhat, o, vec, wqkv):
     windows = ohm.shape[0]
     wb = block_windows(windows)
+    fixed = lambda *shape: pl.BlockSpec(shape, lambda i: (0,) * len(shape))
+    anywhere = pl.BlockSpec(memory_space=pl.ANY)
     return pl.pallas_call(
         backward_kernel,
         grid=(windows // wb,),
         in_specs=[blocked(wb * AREA, MODEL), blocked(wb, PADDED, 128), once(oht), blocked(wb, PADDED, 3 * MODEL),
-                  blocked(wb, PAIRS, 256, PADDED), blocked(wb, PAIRS, 2, PADDED), once(wproj), once(relt), once(shift)],
-        out_specs=[blocked(wb, PADDED, MODEL), blocked(wb, PADDED, 3 * MODEL),
-                   pl.BlockSpec((2, 64, 128), lambda i: (0, 0, 0))],
-        out_shape=[jax.ShapeDtypeStruct((windows, PADDED, MODEL), BF16), jax.ShapeDtypeStruct((windows, PADDED, 3 * MODEL), BF16),
-                   jax.ShapeDtypeStruct((2, 64, 128), F32)],
-        scratch_shapes=[pltpu.VMEM((wb, PADDED, MODEL), BF16)],
-        cost_estimate=cost(70),
+                  blocked(wb, PAIRS, 256, PADDED), blocked(wb, PAIRS, 2, PADDED), once(wproj), once(relt), once(shift),
+                  blocked(wb, PADDED, MODEL), blocked(wb, PADDED, MODEL), once(vec), anywhere],
+        out_specs=[blocked(wb, PADDED, 3 * MODEL), fixed(2, 64, 128), anywhere, fixed(8, 3 * MODEL), fixed(MODEL, 128), fixed(MODEL, 128)],
+        out_shape=[jax.ShapeDtypeStruct((windows, PADDED, 3 * MODEL), BF16), jax.ShapeDtypeStruct((2, 64, 128), F32),
+                   jax.ShapeDtypeStruct((BLOCKS, MODEL, BLOCK), BF16), jax.ShapeDtypeStruct((8, 3 * MODEL), F32),
+                   jax.ShapeDtypeStruct((MODEL, 128), F32), jax.ShapeDtypeStruct((MODEL, 128), F32)],
+        scratch_shapes=[pltpu.VMEM((wb, PADDED, MODEL), BF16), pltpu.VMEM((wb, PADDED, MODEL), BF16),
+                        pltpu.VMEM((MODEL + 16, wb * PADDED), BF16), pltpu.VMEM((MODEL + 16, 4 * MODEL), F32),
+                        pltpu.VMEM((2, MODEL, BLOCK), BF16), pltpu.VMEM((2, MODEL, BLOCK), BF16),
+                        pltpu.SemaphoreType.DMA((2,)), pltpu.SemaphoreType.DMA((2,))],
+        cost_estimate=cost(95),
         compiler_params=pltpu.CompilerParams(vmem_limit_bytes=VMEM_LIMIT, dimension_semantics=("arbitrary",)),
         name="attention_backward",
-    )(da, ohm, oht, qkv, qaug, lse, wproj, relt, shift)
-
-
-def input_kernel(x_ref, da_ref, dp_ref, gain_ref, wqkv_ref, *rest):
+    )(da, ohm, oht, qkv, qaug, lse, wproj, relt, shift, xhat, o, vec, wqkv)
+
+
+def input_kernel(x_ref, da_ref, dp_ref, vec_ref, wqkv_ref, *rest):
     gx_ref, wide, tall = rest[-3:]
     wb = dp_ref.shape[0]
     wide[...] = mm(dp_ref[...].reshape(wb * PADDED, 3 * MODEL), wqkv_ref[...], NT)
@@ -273,12 +331,12 @@
         hi = min(lo + 112, rows)
         c, r = norm(x_ref[lo:hi, :].astype(F32))
         xhat = c * r
-        dx = tall[lo:hi, :] * gain_ref[...]
+        dx = tall[lo:hi, :] * vec_ref[LN1_GAIN]
         dx = r * (dx - jnp.mean(dx, axis=-1, keepdims=True) - xhat * jnp.mean(dx * xhat, axis=-1, keepdims=True))
         gx_ref[lo:hi, :] = (dx + da_ref[lo:hi, :].astype(F32)).astype(BF16)
 
 
-def input_gradient(x, da, dp, gain, wqkv, at, count, held):
+def input_gradient(x, da, dp, vec, wqkv, at, count, held):
     windows = dp.shape[0]
     wb = block_windows(windows)
     part = lambda *shape: pl.BlockSpec(shape, lambda i: (i + at,) + (0,) * (len(shape) - 1))
@@ -286,7 +344,7 @@
     return pl.pallas_call(
         input_kernel,
         grid=(count,),
-        in_specs=[part(wb * AREA, MODEL), part(wb * AREA, MODEL), part(wb, PADDED, 3 * MODEL), once(gain), once(wqkv)]
+        in_specs=[part(wb * AREA, MODEL), part(wb * AREA, MODEL), part(wb, PADDED, 3 * MODEL), once(vec), once(wqkv)]
         + [pl.BlockSpec(memory_space=pl.ANY)] * len(extra),
         out_specs=part(wb * AREA, MODEL),
         out_shape=jax.ShapeDtypeStruct((windows * AREA, MODEL), BF16),
@@ -295,104 +353,36 @@
         cost_estimate=cost(5 * count),
         compiler_params=pltpu.CompilerParams(vmem_limit_bytes=VMEM_LIMIT, dimension_semantics=("arbitrary",)),
         name="input_gradient",
-    )(x, da, dp, gain, wqkv, *extra)
-
-
-BAND = 384
-
-
-def weight_kernel(xhat_ref, o_ref, dp_ref, dap_ref, w_ref, gain_ref, bias_ref, dw_ref, sum_ref, gvec_ref, bvec_ref, turned):
-    step = pl.program_id(0)
-    qkv_bands = 3 * MODEL // BAND
-
-    @pl.when(step == 0)
-    def _():
-        turned[...] = xhat_ref[...].T
-        gvec_ref[...] = jnp.zeros_like(gvec_ref)
-        bvec_ref[...] = jnp.zeros_like(bvec_ref)
-
-    @pl.when(step == qkv_bands)
-    def _():
-        turned[...] = o_ref[...].T
-
-    @pl.when(step < qkv_bands)
-    def _():
-        m = mm(turned[...], dp_ref[...])
-        s = jnp.sum(dp_ref[...].astype(F32), axis=0, keepdims=True)
-        sum_ref[...] = jnp.broadcast_to(s, sum_ref.shape)
-        dw_ref[...] = (m * gain_ref[...] + bias_ref[...] * s).astype(BF16)
-        w = w_ref[...].astype(F32)
-        g, b = w * m, w * s
-        for n in range(BAND // 128):
-            gvec_ref[...] += g[:, 128 * n:128 * (n + 1)]
-            bvec_ref[...] += b[:, 128 * n:128 * (n + 1)]
-
-    @pl.when(step >= qkv_bands)
-    def _():
-        dw_ref[...] = mm(turned[...], dap_ref[...]).astype(BF16)
-
-
-def weight_gradients(xhat, o, dp, dap, wqkv, gain, bias, owners):
-    rows = xhat.shape[0]
-    nq, np_ = 3 * MODEL // BAND, MODEL // BAND
-    oq, op = nq // owners, np_ // owners
-    last = lambda i: jnp.minimum(i, nq - 1)
-
-    def place(i):
-        j = i - nq
-        q = (i // oq) * (oq + op) + i % oq
-        p = (j // op) * (oq + op) + oq + j % op
-        return (0, jnp.where(i < nq, q, p))
-    return pl.pallas_call(
-        weight_kernel,
-        grid=(nq + np_,),
-        in_specs=[once(xhat), once(o), pl.BlockSpec((rows, BAND), lambda i: (0, last(i))),
-                  pl.BlockSpec((rows, BAND), lambda i: (0, jnp.maximum(i - nq, 0))),
-                  pl.BlockSpec((MODEL, BAND), lambda i: (0, last(i))), once(gain), once(bias)],
-        out_specs=[pl.BlockSpec((MODEL, BAND), place), pl.BlockSpec((8, BAND), lambda i: (0, last(i))),
-                   pl.BlockSpec((MODEL, 128), lambda i: (0, 0)), pl.BlockSpec((MODEL, 128), lambda i: (0, 0))],
-        out_shape=[jax.ShapeDtypeStruct((MODEL, 4 * MODEL), BF16), jax.ShapeDtypeStruct((8, 3 * MODEL), F32),
-                   jax.ShapeDtypeStruct((MODEL, 128), F32), jax.ShapeDtypeStruct((MODEL, 128), F32)],
-        scratch_shapes=[pltpu.VMEM((MODEL, rows), BF16)],
-        cost_estimate=cost(20),
-        compiler_params=pltpu.CompilerParams(vmem_limit_bytes=VMEM_LIMIT, dimension_semantics=("arbitrary",)),
-        name="weight_gradients",
-    )(xhat, o, dp, dap, wqkv, gain, bias)
+    )(x, da, dp, vec, wqkv, *extra)
+
+
+def constant_tables():
+    place = np.arange(PADDED)
+    real = place < AREA
+    r, c = np.where(real, place // WIN, 0), np.where(real, place % WIN, 0)
+    hot = [((WIN - 1 - v)[:, None] == np.arange(16)) & real[:, None] for v in (r, c)]
+    keys = np.concatenate(hot + hot, axis=1).astype(np.float32)
+    shift = np.stack([(v >> b) & 1 for v in (r, c) for b in (3, 2, 1, 0)]).astype(np.int32)
+    return keys, np.concatenate(hot, axis=1).T.astype(np.float32), shift
 
 
 def small_tables(window_extent, rel_h, rel_w):
-    place = jnp.arange(PADDED)
+    keys, oht, shift = constant_tables()
+    place = np.arange(PADDED)
     r, c = place // WIN, place % WIN
-    real = place < AREA
-    hot_r = ((r[:, None] == jnp.arange(16)) & real[:, None]).astype(F32)
-    hot_c = ((c[:, None] == jnp.arange(16)) & real[:, None]).astype(F32)
-    valid = (r < window_extent[:, 0:1]) & (c < window_extent[:, 1:2]) & real
-    first = jnp.where((jnp.arange(16) == 14)[None, None, :], jnp.where(valid, 0.0, NEGATIVE)[:, :, None], hot_r[None])
-    rest = jnp.concatenate([hot_c, hot_r, hot_c, jnp.zeros((PADDED, 64), F32)], axis=1)
-    rest = jnp.broadcast_to(rest[None], (valid.shape[0],) + rest.shape)
-    ohm = jnp.concatenate([first, rest], axis=2).astype(BF16)
-    oht = jnp.concatenate([hot_r, hot_c], axis=1).T.astype(BF16)
-    sh = WIN - 1 - jnp.minimum(r, WIN - 1)
-    sw = WIN - 1 - c
-    shift = jnp.stack([jnp.where(real, (s >> b) & 1, 0) for s in (sh, sw) for b in (3, 2, 1, 0)]).astype(jnp.int32)
-    flip = lambda t: jnp.concatenate([t[::-1], jnp.zeros((5, HEAD_DIM), F32)], axis=0)
-    fh, fw = flip(rel_h), flip(rel_w)
-
-    def hi_lo(v):
-        hi = v.astype(BF16).astype(F32)
-        return hi, v - hi
-
-    def rows(th, tw):
-        z = jnp.zeros((32, HEAD_DIM), F32)
-        return jnp.concatenate([jnp.concatenate([th, z], 1), jnp.concatenate([z, th], 1),
-                                jnp.concatenate([tw, z], 1), jnp.concatenate([z, tw], 1)], axis=0)
-    (hh, hl), (wh, wl) = hi_lo(fh), hi_lo(fw)
-    mix = jnp.concatenate([rows(hh, wh), rows(hl, wl)], axis=1)
-    ident = jnp.concatenate([SCALE * jnp.eye(128, dtype=F32), jnp.zeros((128, 128), F32)], axis=1)
-    mix = jnp.concatenate([mix, ident], axis=0).astype(BF16)
-    relt = jnp.concatenate([hh, wh, hl, wl], axis=0).T.astype(BF16)
-    valid_rows = valid[:, :AREA].reshape(-1, 1).astype(F32)
-    return ohm, oht, shift, mix, relt, valid_rows
+    valid = (r < window_extent[:, 0:1]) & (c < window_extent[:, 1:2]) & (place < AREA)
+    keys = np.concatenate([keys, np.zeros((PADDED, 64), np.float32)], axis=1)
+    flag = np.arange(128) == 14
+    ohm = jnp.where(flag[None, None, :], jnp.where(valid, 0.0, NEGATIVE)[:, :, None], keys[None]).astype(BF16)
+    both = jnp.pad(jnp.stack([rel_h, rel_w]), ((0, 0), (0, 5), (0, 0)))
+    hi = both.astype(BF16).astype(F32)
+    lo = both - hi
+    parity = np.eye(2, dtype=np.float32)
+    spread = lambda t: (t[:, None, :, None, :] * parity[None, :, None, :, None]).reshape(128, 128)
+    ident = np.concatenate([SCALE * np.eye(128), np.zeros((128, 128))], axis=1).astype(np.float32)
+    mix = jnp.concatenate([jnp.concatenate([spread(hi), spread(lo)], axis=1), ident], axis=0).astype(BF16)
+    relt = jnp.concatenate([hi.reshape(64, HEAD_DIM), lo.reshape(64, HEAD_DIM)], axis=0).T.astype(BF16)
+    return ohm, jnp.asarray(oht, BF16), jnp.asarray(shift), mix, relt
 
 
 def gelu_parts(z):
@@ -409,7 +399,7 @@
 CHUNK = 64 * 12
 
 
-def mlp_kernel(rows, widths, offset_ref, x1_ref, go_ref, mask_ref, gain_ref, bias_ref, upb_ref, downb_ref, *rest):
+def mlp_kernel(rows, widths, offset_ref, x1_ref, go_ref, mask_ref, par_ref, upb_ref, *rest):
     n = len(widths)
     ups, downs = rest[:n], rest[n:2 * n]
     out_ref, da_ref, dw_ref, dbu_ref, vec_ref, h2, dm, h2t, dmt, macc, dacc, accu, accd, stage, sems = rest[2 * n:]
@@ -433,7 +423,7 @@
         rs = pl.ds(pl.multiple_of(i * ch, ch), ch)
         x1 = jnp.where(live(i), x1_ref[rs, :], 0.0)
         c, r = norm(x1)
-        h2[rs, :] = (c * r * gain_ref[...] + bias_ref[...]).astype(BF16)
+        h2[rs, :] = (c * r * par_ref[LN2_GAIN] + par_ref[LN2_BIAS]).astype(BF16)
         d = jnp.where(live(i) & (mask_ref[rs, :] > 0.0), go_ref[rs, :].astype(F32), 0.0)
         dm[rs, :] = d.astype(BF16)
         vec_ref[0:8, :] += fold8(d)
@@ -467,11 +457,11 @@
         c, r = norm(x1)
         xhat = c * r
         valid = live(i) & (mask_ref[rs, :] > 0.0)
-        out_ref[rs, :] = jnp.where(valid, x1 + macc[rs, :] + downb_ref[...], 0.0).astype(BF16)
+        out_ref[rs, :] = jnp.where(valid, x1 + macc[rs, :] + par_ref[DOWN_BIAS], 0.0).astype(BF16)
         dh = dacc[rs, :]
         vec_ref[8:16, :] += fold8(dh * xhat)
         vec_ref[16:24, :] += fold8(dh)
-        dx = dh * gain_ref[...]
+        dx = dh * par_ref[LN2_GAIN]
         dx = r * (dx - jnp.mean(dx, axis=-1, keepdims=True) - xhat * jnp.mean(dx * xhat, axis=-1, keepdims=True))
         da = (dx + dm[rs, :].astype(F32)).astype(BF16)
         da_ref[rs, :] = da
@@ -495,7 +485,7 @@
         copy(2 * each - 1).wait()
 
 
-def mlp(x1, go, mask, gain, bias, upb, downb, ups, downs, offsets):
+def mlp(x1, go, mask, par, upb, ups, downs, offsets):
     rows, d = x1.shape
     widths = tuple(u.shape[1] for u in ups)
     ff = sum(widths)
@@ -508,7 +498,7 @@
         grid_spec=pltpu.PrefetchScalarGridSpec(
             num_scalar_prefetch=1,
             grid=(pl.cdiv(rows, rb),),
-            in_specs=[rowspec(d), rowspec(d), rowspec(1)] + [full(a) for a in (gain, bias, upb, downb, *ups, *downs)],
+            in_specs=[rowspec(d), rowspec(d), rowspec(1)] + [full(a) for a in (par, upb, *ups, *downs)],
             out_specs=[rowspec(d), rowspec(d), pl.BlockSpec(memory_space=pl.ANY),
                        pl.BlockSpec((8, ff), lambda i, _: (0, 0)), pl.BlockSpec((32, d), lambda i, _: (0, 0))],
             scratch_shapes=[pltpu.VMEM((rb, d), BF16), pltpu.VMEM((rb, d), BF16), pltpu.VMEM((d, rb), BF16), pltpu.VMEM((d, rb), BF16),
@@ -519,7 +509,7 @@
         cost_estimate=cost(170),
         compiler_params=pltpu.CompilerParams(vmem_limit_bytes=VMEM_LIMIT, dimension_semantics=("arbitrary",)),
         name="mlp",
-    )(offsets, x1, go, mask, gain, bias, upb, downb, *ups, *downs)
+    )(offsets, x1, go, mask, par, upb, *ups, *downs)
 
 
 def bits(n):
@@ -538,44 +528,86 @@
     return (a.astype(F32) + b.astype(F32)).astype(BF16)
 
 
-def halve_rows(held, at, bit, sizes):
+def split_dp(held, at, bit):
     mine = bit_of("dp", bit)
-    keep = lax.dynamic_index_in_dim(held, mine, at, keepdims=False)
-    send = lax.dynamic_index_in_dim(held, 1 - mine, at, keepdims=False)
-    return add(keep, swap(send, "dp", bit, sizes))
-
-
-def halve_columns(held, bit, sizes):
+    return tuple(lax.dynamic_index_in_dim(held, m, at, keepdims=False) for m in (mine, 1 - mine))
+
+
+def split_mlp(held, owners, bit):
     mine = bit_of("mlp", bit) == 1
-    half = held.shape[-1] // 2
-    low, high = held[..., :half], held[..., half:]
-    return add(jnp.where(mine, high, low), swap(jnp.where(mine, low, high), "mlp", bit, sizes))
-
-
-def reduce_scatter(grad, sizes):
+    sides = []
+    for side in range(2):
+        runs = [n for n, o in enumerate(owners) if (o >> bit) & 1 == side]
+        sides.append(jnp.concatenate([held[n:n + 1] for n in runs], axis=0))
+    return jnp.where(mine, sides[1], sides[0]), jnp.where(mine, sides[0], sides[1])
+
+
+def reduce_steps(blocks, owners, sizes):
     nb, nm = bits(sizes["dp"]), bits(sizes["mlp"])
-    held = grad.reshape((2,) * nb + (grad.shape[0] // sizes["dp"], grad.shape[1]))
-    held = halve_rows(held, nb - 1, 0, sizes)
-    columns = lambda v: functools.reduce(lambda u, b: halve_columns(u, b, sizes), reversed(range(nm)), v)
-    if nb < 3:
-        return functools.reduce(lambda u, b: halve_rows(u, b - 1, b, sizes), reversed(range(1, nb)), columns(held))
-    first, second = held[0], held[1]
-    at = nb - 3
-    first = columns(first)
-    second = halve_rows(second, at, 1, sizes)
-    first = halve_rows(first, at, 1, sizes)
-    second = columns(second)
-    for b in range(2, nb - 1):
-        first, second = (halve_rows(v, nb - 2 - b, b, sizes) for v in (first, second))
+    count, rows, cols = blocks.shape
+    held = blocks.reshape((count,) + (2,) * nb + (rows // sizes["dp"], cols))
+    keep, send = split_dp(held, nb, 0)
+    got = yield [("dp", 0, send)]
+    held = add(keep, got[0])
+    orders = ([("mlp", b) for b in reversed(range(nm))] + [("dp", 1)], [("dp", 1)] + [("mlp", b) for b in reversed(range(nm))])
+    halves = [held[:, 0], held[:, 1]]
+    left = [list(owners), list(owners)]
+    dims = [nb - 2, nb - 2]
+    plan = list(zip(*orders)) + [(("dp", b), ("dp", b)) for b in range(2, nb - 1)]
+    for both in plan:
+        kept, sends = [], []
+        for n, (axis, bit) in enumerate(both):
+            if axis == "mlp":
+                keep, send = split_mlp(halves[n], left[n], bit)
+                mine = [o for o in left[n] if (o >> bit) & 1 == 0]
+                left[n] = [o & ~(1 << bit) for o in mine]
+            else:
+                keep, send = split_dp(halves[n], dims[n], bit)
+                dims[n] -= 1
+            kept.append(keep)
+            sends.append((axis, bit, send))
+        got = yield sends
+        halves = [add(k, g) for k, g in zip(kept, got)]
     mine = bit_of("dp", nb - 1) == 1
-    return add(jnp.where(mine, second, first), swap(jnp.where(mine, first, second), "dp", nb - 1, sizes))
-
-
-def sum_everywhere(v, sizes):
+    got = yield [("dp", nb - 1, jnp.where(mine, halves[0], halves[1]))]
+    yield add(jnp.where(mine, halves[1], halves[0]), got[0])
+
+
+def sum_steps(v, sizes):
     for axis in ("dp", "mlp"):
         for b in range(bits(sizes[axis])):
-            v = v + swap(v, axis, b, sizes)
-    return v
+            got = yield [(axis, b, v)]
+            v = v + got[0]
+    yield v
+
+
+def pair_steps(v, width):
+    mine = lax.axis_index("mlp") == 1
+    low, high = v[:, :width], v[:, width:]
+    got = yield [("mlp", 0, jnp.where(mine, low, high))]
+    yield add(jnp.where(mine, high, low), got[0])
+
+
+def run_steps(tasks, delays, work, sizes):
+    states = [next(t) if not d else None for t, d in zip(tasks, delays)]
+    results = [None] * len(tasks)
+    turn = 0
+    while any(r is None for r in results):
+        turn += 1
+        sends = [(n, s) for n, state in enumerate(states) if isinstance(state, list) for s in state]
+        values = work(turn, [s[2] for _, s in sends], [swap_by(s[0], s[1], sizes) for _, s in sends])
+        for n, task in enumerate(tasks):
+            if isinstance(states[n], list):
+                states[n] = task.send([v for v, (owner, _) in zip(values, sends) if owner == n])
+                if not isinstance(states[n], list):
+                    results[n] = states[n]
+            elif results[n] is None and turn >= delays[n]:
+                states[n] = next(task)
+    return results
+
+
+def swap_by(axis, bit, sizes):
+    return lambda v: swap(v, axis, bit, sizes)
 
 
 def feed_forward_weights(up, up_bias, down, sizes):
@@ -618,10 +650,9 @@
     owners = sizes["mlp"]
     line = lambda v: v.reshape(1, -1)
     ups, downs, up_bias_here, places, piece = feed_forward_weights(up_weight, up_bias, down_weight, sizes)
-    ohm, oht, shift, mix, relt, valid_rows = small_tables(window_extent, rel_h, rel_w)
-    qkv_bias = jnp.concatenate([query_bias, jnp.zeros_like(query_bias), value_bias])
-    x1, xhat, qkv, qaug, o, lse = attention_forward(
-        tokens, ohm, line(ln1_gain), line(ln1_bias), qkv_weight, line(qkv_bias), mix, shift, proj_weight, line(proj_bias))
+    ohm, oht, shift, mix, relt = small_tables(window_extent, rel_h, rel_w)
+    par = jnp.stack([ln1_gain, ln1_bias, query_bias, value_bias, proj_bias, ln2_gain, ln2_bias, down_bias])
+    x1, xhat, qkv, qaug, o, lse, row_mask = attention_forward(tokens, ohm, par, qkv_weight, mix, shift, proj_weight)
     if owners == 2:
         (ups, downs, x1) = lax.optimization_barrier((ups, downs, x1))
         ups, downs = list(ups) + [swap(ups[1], "dp", 0, sizes)], list(downs) + [swap(downs[1], "dp", 0, sizes)]
@@ -629,31 +660,53 @@
     ff = width * owners
     by_owner = (places // width) * (2 * width) + places % width
     output, da, dw_mlp, up_sums, mid_sums = mlp(
-        x1, grad_out, valid_rows, line(ln2_gain), line(ln2_bias), line(up_bias_here), line(down_bias), ups, downs,
+        x1, grad_out, row_mask, par, line(up_bias_here), ups, downs,
         jnp.concatenate([by_owner, by_owner + width]))
     dw_mlp = lax.psum_scatter(dw_mlp, "dp", scatter_dimension=0, tiled=True)
-    dw_mlp = lax.psum_scatter(dw_mlp, "mlp", scatter_dimension=1, tiled=True)
-    dap, dp_all, grel = attention_backward(da, ohm, oht, qkv, qaug, lse, proj_weight, relt, shift)
-    flat = lambda v: v.reshape(-1, v.shape[-1])
+    if owners != 2:
+        dw_mlp = lax.psum_scatter(dw_mlp, "mlp", scatter_dimension=1, tiled=True)
+    dp_all, grel, dw_late, dp_sums, gain_sums, bias_sums = attention_backward(
+        da, ohm, oht, qkv, qaug, lse, proj_weight, relt, shift, xhat, o, par, qkv_weight)
     up_sum = jnp.sum(up_sums, axis=0).reshape(-1, piece)
     up_sum = sum(jnp.where(jnp.arange(ff) // piece == places[n] // piece, jnp.tile(up_sum[n], ff // piece), 0.0)
                  for n in range(ff // piece))
-    column = lambda v: v.reshape(-1, 1)
-    direct = MODEL % (BAND * owners) == 0
-    dw_late, dp_sums, gain_sums, bias_sums = weight_gradients(
-        flat(xhat), flat(o), flat(dp_all), flat(dap), qkv_weight, column(ln1_gain), column(ln1_bias), owners if direct else 1)
-    if not direct:
-        split_owner = lambda v: v.reshape(MODEL, owners, -1)
-        dw_late = jnp.concatenate([split_owner(dw_late[:, :3 * MODEL]), split_owner(dw_late[:, 3 * MODEL:])], axis=2).reshape(MODEL, -1)
+    block_owners = [0, 0, 0, 1, 1, 1, 0, 1]
+    if owners != 2:
+        qkv_part, proj_part = (jnp.moveaxis(v, 0, 1).reshape(MODEL, owners, -1) for v in (dw_late[:6], dw_late[6:]))
+        dw_late = jnp.moveaxis(jnp.concatenate([qkv_part, proj_part], axis=2), 1, 0)
+        block_owners = list(range(owners))
     rel = grel[0, :, :HEAD_DIM] + grel[1, :, HEAD_DIM:]
     mid = jnp.sum(mid_sums.reshape(4, 8, MODEL), axis=1)
     sums = jnp.concatenate([jnp.sum(gain_sums, axis=1), jnp.sum(bias_sums, axis=1), dp_sums[0], rel.reshape(-1), mid.reshape(-1), up_sum])
-    sums = sum_everywhere(sums, sizes)
-    late = reduce_scatter(dw_late, sizes).astype(F32)
-    grad_tokens = None
     blocks = dp_all.shape[0] // block_windows(dp_all.shape[0])
-    for n in range(blocks):
-        grad_tokens = input_gradient(tokens, da, dp_all, line(ln1_gain), qkv_weight, n, 1, grad_tokens)
+    held = {"gx": None, "da": da, "at": 0}
+
+    def input_part(count):
+        held["gx"] = input_gradient(tokens, held["da"], dp_all, par, qkv_weight, held["at"], count, held["gx"])
+        held["at"] += count
+
+    def work(turn, values, swaps):
+        if held["at"] >= blocks:
+            return [f(v) for f, v in zip(swaps, values)]
+        values, held["da"] = lax.optimization_barrier((values, held["da"]))
+        got = [f(v) for f, v in zip(swaps, values)]
+        input_part(1)
+        got, held["gx"] = lax.optimization_barrier((got, held["gx"]))
+        return got
+
+    tasks = [reduce_steps(dw_late, block_owners, sizes), sum_steps(sums, sizes)]
+    delays = [0, 0]
+    if owners == 2:
+        tasks.append(pair_steps(dw_mlp, 2 * width))
+        delays.append(1)
+    results = run_steps(tasks, delays, work, sizes)
+    late, sums = results[0].astype(F32), results[1]
+    late = jnp.concatenate([late[n] for n in range(late.shape[0])], axis=1)
+    if owners == 2:
+        dw_mlp = results[2]
+    if held["at"] < blocks:
+        input_part(blocks - held["at"])
+    grad_tokens = held["gx"]
     d = MODEL
     table = 2 * WIN - 1
     n_rel = 64 * HEAD_DIM
@@ -669,8 +722,8 @@
         late[:, :cols],
         sums[2 * d:3 * d],
         sums[4 * d:5 * d],
-        rel[0:table][::-1],
-        rel[32:32 + table][::-1],
+        rel[0:table],
+        rel[32:32 + table],
         late[:, cols:],
         mid[3 * d:4 * d],
         mid[d:2 * d],

time: 522 us -> 496 us (0.950)
  waiting for transfers between devices: 30.2 us -> 10.1 us
  Pallas kernels: 415 us -> 404 us
  other arithmetic: 13 us -> 23 us
  local copies, waits for them, and re-layouts: 24.8 us -> 15.6 us
    pallas_call x1 -> x0, Pallas kernels: 42 us -> none  [weight_gradients(): pl.pallas_call(weight_kernel, grid=(nq + np_,), in_specs=[once(xhat), onc...]
    pallas_call x1, Pallas kernels: 70.6 us -> 105 us  [attention_backward(): pl.pallas_call(backward_kernel, grid=(windows // wb,), in_specs=[blocked(...]
    ppermute x18 -> x19, waiting for transfers between devices: 30.2 us -> 10.1 us  [swap(): lax.ppermute(value, axis, [(i, i ^ 1 << bit) for i in range(sizes[axis])])]
    reshape x9 -> x2, local copies, waits for them, and re-layouts: 5.93 us -> 0.18 us  [the longest x1 0.09 us: small_tables(): lo.reshape(64, HEAD_DIM)]
    ppermute x18 -> x19, starting transfers between devices: 17.6 us -> 20.8 us  [swap(): lax.ppermute(value, axis, [(i, i ^ 1 << bit) for i in range(sizes[axis])])]
  transfers between devices with their start and end apart: 20 -> 20, of which waited for: 6 -> 3; matrix products, arithmetic and copies ran while one was open for 6% -> 6% of each run, Pallas kernels for 45% -> 45%
where the time goes in v3:
time: 496 us; the launch traced here: 489 us
  Pallas kernels  404 us (81%)
  other arithmetic  23 us (5%)
  starting transfers between devices  20.8 us (4%)
  local copies, waits for them, and re-layouts  15.6 us (3%)
  between operations  15.2 us (3%)
  waiting for transfers between devices  10.1 us (2%)
    pallas_call x1, Pallas kernels, mlp(): pl.pallas_call(functools.partial(mlp_kernel, rows, widths), grid_spec=plt...  185 us
    pallas_call x1, Pallas kernels, attention_backward(): pl.pallas_call(backward_kernel, grid=(windows // wb,), in_specs=[blocked(...  105 us
    pallas_call x1, Pallas kernels, attention_forward(): pl.pallas_call(forward_kernel, grid=(windows // wb,), in_specs=[blocked(w...  68.3 us
    pallas_call x5, Pallas kernels, input_gradient(): pl.pallas_call(input_kernel, grid=(count,), in_specs=[part(wb * AREA, MOD...  45 us
    ppermute x19, starting transfers between devices, swap(): lax.ppermute(value, axis, [(i, i ^ 1 << bit) for i in range(sizes[axis])])  20.8 us
    ppermute x19, waiting for transfers between devices, swap(): lax.ppermute(value, axis, [(i, i ^ 1 << bit) for i in range(sizes[axis])])  10.1 us
  transfers between devices with their start and end apart: 20, of which 3 were waited for; matrix products, arithmetic and copies ran while one was open for 6% of the time, Pallas kernels for 45%

profile of v3, /device:TPU:0, one launch (start us, length us, event | category | flops | bytes accessed | tf_op | source)
XLA Modules:
  0.0 488.9 jit_solution(4582336526737906594)
XLA Ops:
  7.3 1.9 slice_select_fusion.1
  9.2 3.0 collective-permute-start
  21.1 2.4 select_convert_fusion.ohm_ref
  24.2 68.3 %attention_forward.1 = (f32[3920,768]{1,0:T(8,128)}, bf16[20,208,768]{2,1,0:T(8,128)(2,1)}, bf16[20,208,2304]{2,1,0:T(8,128)(2,1)}, bf16[20,6,256,208]{3,2,1,0:T...) custom-call(bf16[3920,768]{1,0:T(8,128)(2,1)} %x_ref.11, ...), custom_call_target="tpu_custom_call" | custom-call | flops 70000001024 | bytes 1048576 | tf_op jit(solution)/shard_map/attention_forward/pallas_call | solution.py:168
  93.1 1.8 collective-permute-start.2
  97.5 185.4 %mlp.1 = (bf16[3920,768]{1,0:T(8,128)(2,1)}, bf16[3920,768]{1,0:T(8,128)(2,1)}, bf16[768,6144]{1,0:T(8,128)(2,1)}, f32[8,3072]{1,0:T(8,128)}, f32[32,768]{1,0:T(8,128)}) custom-call(s32[8]{0:T(128)} %pad_add_fusion.1.offset_ref, f32[3920,768]{1,0:T(8,128)} %get-tuple-element.79.x1_ref, bf16[3920,768]{1,0:T(8,128)(2,1)} %go_ref.1, ...), custom_call_target="tpu_custom_call" | custom-call | flops 170000007168 | bytes 1048576 | tf_op jit(solution)/shard_map/mlp/pallas_call | solution.py:496
  284.6 105.4 %attention_backward.1 = (bf16[20,208,2304]{2,1,0:T(8,128)(2,1)}, f32[2,64,128]{2,1,0:T(8,128)}, bf16[8,768,384]{2,1,0:T(8,128)(2,1)}, f32[8,2304]{1,0:T(8,128)}, f32[768,128]{1,0:T(8,128)}, /*index=5*/f32[768,128]{1,0:T(8,128)}) custom-call(bf16[3920,768]{1,0:T(8,128)(2,1)} %get-tuple-element.133.da_ref, bf16[20,208,128]{2,1,0:T(8,128)(2,1)} %select_convert_fusion.ohm_ref, ...), custom_call_target="tpu_custom_call" | custom-call | flops 95000002560 | bytes 1048576 | tf_op jit(solution)/shard_map/attention_backward/pallas_call | solution.py:303
  393.5 3.0 constant_dynamic-slice_fusion.1
  396.6 1.7 copy.76
  399.8 8.9 %input_gradient.5.rest_0_ = bf16[3920,768]{1,0:T(8,128)(2,1)} custom-call(bf16[3920,768]{1,0:T(8,128)(2,1)} %x_ref.11, bf16[3920,768]{1,0:T(8,128)(2,1)} %get-tuple-element.133.da_ref, bf16[20,208,2304]{2,1,0:T(8,128)(2,1)} %get-tuple-element.102.dp_ref, f32[8,768]{1,0:T(8,128)} %stack.64.vec_ref.par_ref, bf16[768,2304]{1,0:T(8,128)(2,1)} %wqkv_ref.13), custom_call_target="tpu_custom_call" | custom-call | flops 5000000000 | bytes 1048576 | tf_op jit(solution)/shard_map/input_gradient/pallas_call | solution.py:344
  409.4 2.4 fusion
  413.1 1.8 broadcast_select_fusion.2
  414.9 1.8 collective-permute-start.7
  416.7 1.5 collective-permute-start.8
  419.0 8.9 %input_gradient.6.rest_0_ = bf16[3920,768]{1,0:T(8,128)(2,1)} custom-call(bf16[3920,768]{1,0:T(8,128)(2,1)} %x_ref.11, bf16[3920,768]{1,0:T(8,128)(2,1)} %get-tuple-element.133.da_ref, bf16[20,208,2304]{2,1,0:T(8,128)(2,1)} %get-tuple-element.102.dp_ref, f32[8,768]{1,0:T(8,128)} %stack.64.vec_ref.par_ref, ...), custom_call_target="tpu_custom_call", output_to_operand_aliasing={{}: (5, {})} | custom-call | flops 5000000000 | bytes 1048576 | tf_op jit(solution)/shard_map/input_gradient/pallas_call | solution.py:344
  427.9 5.0 %collective-permute-done.9 = f32[14080]{0:T(1024)S(1)} collective-permute-done((f32[14080]{0:T(1024)}, f32[14080]{0:T(1024)S(1)}, u32[]{:S(2)}, u32[]{:S(2)}) %collective-permute-start.9) | collective-permute-done | bytes 56352 | tf_op jit(solution)/shard_map/ppermute | solution.py:520
  433.0 3.8 collective-permute-done.10
  439.5 1.9 collective-permute-start.11
  442.8 1.6 collective-permute-start.13
  444.4 9.2 %input_gradient.7.rest_0_ = bf16[3920,768]{1,0:T(8,128)(2,1)} custom-call(bf16[3920,768]{1,0:T(8,128)(2,1)} %x_ref.11, bf16[3920,768]{1,0:T(8,128)(2,1)} %get-tuple-element.133.da_ref, bf16[20,208,2304]{2,1,0:T(8,128)(2,1)} %get-tuple-element.102.dp_ref, f32[8,768]{1,0:T(8,128)} %stack.64.vec_ref.par_ref, ...), custom_call_target="tpu_custom_call", output_to_operand_aliasing={{}: (5, {})} | custom-call | flops 5000000000 | bytes 1048576 | tf_op jit(solution)/shard_map/input_gradient/pallas_call | solution.py:344
  454.4 1.6 collective-permute-start.15
  456.0 2.6 collective-permute-start.16
  458.6 8.9 %input_gradient.8.rest_0_ = bf16[3920,768]{1,0:T(8,128)(2,1)} custom-call(bf16[3920,768]{1,0:T(8,128)(2,1)} %x_ref.11, bf16[3920,768]{1,0:T(8,128)(2,1)} %get-tuple-element.133.da_ref, bf16[20,208,2304]{2,1,0:T(8,128)(2,1)} %get-tuple-element.102.dp_ref, f32[8,768]{1,0:T(8,128)} %stack.64.vec_ref.par_ref, ...), custom_call_target="tpu_custom_call", output_to_operand_aliasing={{}: (5, {})} | custom-call | flops 5000000000 | bytes 1048576 | tf_op jit(solution)/shard_map/input_gradient/pallas_call | solution.py:344
  468.6 8.9 %input_gradient.9 = bf16[3920,768]{1,0:T(8,128)(2,1)} custom-call(bf16[3920,768]{1,0:T(8,128)(2,1)} %x_ref.11, bf16[3920,768]{1,0:T(8,128)(2,1)} %get-tuple-element.133.da_ref, bf16[20,208,2304]{2,1,0:T(8,128)(2,1)} %get-tuple-element.102.dp_ref, f32[8,768]{1,0:T(8,128)} %stack.64.vec_ref.par_ref, ...), custom_call_target="tpu_custom_call", output_to_operand_aliasing={{}: (5, {})} | custom-call | flops 5000000000 | bytes 1048576 | tf_op jit(solution)/shard_map/input_gradient/pallas_call | solution.py:344
  (146 shorter events, 31.7 us)
Async XLA Ops:
  7.2 405.9 %reduce-scatter.2.cloned.1.call-start = ((), (), s32[]{:S(2)}) async-start(), calls=%async_computation.1 | async-start | bytes 10027008 | tf_op jit(solution)/shard_map/reduce_scatter | solution.py:665
  9.2 83.3 %collective-permute-start = (bf16[768,768]{1,0:T(8,128)(2,1)S(1)}, bf16[768,768]{1,0:T(8,128)(2,1)}, u32[]{:S(2)}, u32[]{:S(2)}) collective-permute-start(bf16[768,768]{1,0:T(8,128)(2,1)S(1)} %slice_select_fusion.1), channel_id=1, source_target_pairs={{0,1},{1,0},{2,3},{3,2},{4,5},{5,4},{6,7},{7,6},{8,9},{9,8},{10,11... | collective-permute-start | bytes 3538952 | tf_op jit(solution)/shard_map/ppermute | solution.py:520
  13.4 79.2 %collective-permute-start.1 = (bf16[768,768]{1,0:T(8,128)(2,1)}, bf16[768,768]{1,0:T(8,128)(2,1)S(1)}, u32[]{:S(2)}, u32[]{:S(2)}) collective-permute-start(bf16[768,768]{1,0:T(8,128)(2,1)} %slice_select_fusion), channel_id=1, source_target_pairs={{0,1},{1,0},{2,3},{3,2},{4,5},{5,4},{6,7},{7,6},{8,9},{9,8},{10,11... | collective-permute-start | bytes 3538952 | tf_op jit(solution)/shard_map/ppermute | solution.py:520
  24.2 69.0 %copy-start.11 = (f32[1536]{0:T(1024)S(1)}, f32[1536]{0:T(1024)}, u32[]{:S(2)}) copy-start(f32[1536]{0:T(1024)} %param.42) | copy-start | bytes 18436
  92.6 4.9 %collective-permute-start.3 = (bf16[768,768]{1,0:T(8,128)(2,1)}, bf16[768,768]{1,0:T(8,128)(2,1)}, u32[]{:S(2)}, u32[]{:S(2)}) collective-permute-start(bf16[768,768]{1,0:T(8,128)(2,1)} %collective-permute-done.rest_1_), channel_id=1, source_target_pairs={{0,2},{2,0},{4,6},{6,4},{8,10},{10,8},{12,14},{14,12},{16,18},{18,... | collective-permute-start | bytes 3538952 | tf_op jit(solution)/shard_map/ppermute | solution.py:520
  92.6 4.9 collective-permute-start.4
  93.1 3.7 collective-permute-start.2
  284.6 108.7 %copy-start.4 = (f32[32,768]{1,0:T(8,128)S(1)}, f32[32,768]{1,0:T(8,128)}, u32[]{:S(2)}) copy-start(f32[32,768]{1,0:T(8,128)} %get-tuple-element.97) | copy-start | bytes 294916
  284.6 108.8 %copy-start.3 = (f32[8,3072]{1,0:T(8,128)S(1)}, f32[8,3072]{1,0:T(8,128)}, u32[]{:S(2)}) copy-start(f32[8,3072]{1,0:T(8,128)} %get-tuple-element.98) | copy-start | bytes 294916
  399.3 9.5 %collective-permute-start.5 = (bf16[8,2,2,2,48,384]{5,4,2,3,1,0:T(8,128)(2,1)}, bf16[8,2,2,2,48,384]{5,4,2,3,1,0:T(8,128)(2,1)}, u32[]{:S(2)}, u32[]{:S(2)}) collective-permute-start(bf16[8,2,2,2,48,384]{5,4,2,3,1,0:T(8,128)(2,1)} %bitcast.91), channel_id=1, source_target_pairs={{0,2},{2,0},{4,6},{6,4},{8,10},{10,8},{12,14},{14,12},{16,18},{18,... | collective-permute-start | bytes 7077896 | tf_op jit(solution)/shard_map/ppermute | solution.py:520
  399.3 9.4 %collective-permute-start.6 = (f32[14080]{0:T(1024)S(1)}, f32[14080]{0:T(1024)S(1)}, u32[]{:S(2)}, u32[]{:S(2)}) collective-permute-start(f32[14080]{0:T(1024)S(1)} %add_dynamic-update-slice_fusion), channel_id=1, source_target_pairs={{0,2},{2,0},{4,6},{6,4},{8,10},{10,8},{12,14},{14,12},{16,18},{18,... | collective-permute-start | bytes 168968 | tf_op jit(solution)/shard_map/ppermute | solution.py:520
  414.9 21.9 %collective-permute-start.7 = (bf16[4,2,2,48,384]{4,3,0,1,2:T(8,128)(2,1)}, bf16[4,2,2,48,384]{4,3,0,1,2:T(8,128)(2,1)S(1)}, u32[]{:S(2)}, u32[]{:S(2)}) collective-permute-start(bf16[4,2,2,48,384]{4,3,0,1,2:T(8,128)(2,1)} %broadcast_select_fusion), channel_id=1, source_target_pairs={{0,1},{1,0},{2,3},{3,2},{4,5},{5,4},{6,7},{7,6},{8,9},{9,8},{10,11... | collective-permute-start | bytes 1769480 | tf_op jit(solution)/shard_map/ppermute | solution.py:520
  416.7 20.1 %collective-permute-start.8 = (bf16[8,2,48,384]{3,2,1,0:T(8,128)(2,1)S(1)}, bf16[8,2,48,384]{3,2,1,0:T(8,128)(2,1)}, u32[]{:S(2)}, u32[]{:S(2)}) collective-permute-start(bf16[8,2,48,384]{3,2,1,0:T(8,128)(2,1)S(1)} %dynamic-slice_bitcast_fusion), channel_id=1, source_target_pairs={{0,4},{2,6},{4,0},{6,2},{8,12},{10,14},{12,8},{14,10},{16,20},{18,... | collective-permute-start | bytes 1769480 | tf_op jit(solution)/shard_map/ppermute | solution.py:520
  418.2 18.6 %collective-permute-start.10 = (bf16[48,3072]{1,0:T(8,128)(2,1)}, bf16[48,3072]{1,0:T(8,128)(2,1)S(1)}, u32[]{:S(2)}, u32[]{:S(2)}) collective-permute-start(bf16[48,3072]{1,0:T(8,128)(2,1)} %broadcast_select_fusion.2), channel_id=1, source_target_pairs={{0,1},{1,0},{2,3},{3,2},{4,5},{5,4},{6,7},{7,6},{8,9},{9,8},{10,11... | collective-permute-start | bytes 884744 | tf_op jit(solution)/shard_map/ppermute | solution.py:520
  418.8 14.2 %collective-permute-start.9 = (f32[14080]{0:T(1024)}, f32[14080]{0:T(1024)S(1)}, u32[]{:S(2)}, u32[]{:S(2)}) collective-permute-start(f32[14080]{0:T(1024)} %add.145), channel_id=1, source_target_pairs={{0,4},{2,6},{4,0},{6,2},{8,12},{10,14},{12,8},{14,10},{16,20},{18,... | collective-permute-start | bytes 168968 | tf_op jit(solution)/shard_map/ppermute | solution.py:520
  427.9 10.2 %copy-start = (bf16[48,6144]{1,0:T(8,128)(2,1)S(1)}, bf16[48,6144]{1,0:T(8,128)(2,1)}, u32[]{:S(2)}) copy-start(bf16[48,6144]{1,0:T(8,128)(2,1)} %reduce-scatter.2.cloned.1.call-done) | copy-start | bytes 1769476
  439.5 14.1 %collective-permute-start.11 = (bf16[4,2,48,384]{3,2,0,1:T(8,128)(2,1)S(1)}, bf16[4,2,48,384]{3,2,0,1:T(8,128)(2,1)S(1)}, u32[]{:S(2)}, u32[]{:S(2)}) collective-permute-start(bf16[4,2,48,384]{3,2,0,1:T(8,128)(2,1)S(1)} %dynamic-slice_bitcast_fusion.1), channel_id=1, source_target_pairs={{0,4},{2,6},{4,0},{6,2},{8,12},{10,14},{12,8},{14,10},{16,20},{18,... | collective-permute-start | bytes 884744 | tf_op jit(solution)/shard_map/ppermute | solution.py:520
  441.3 12.2 %collective-permute-start.12 = (bf16[4,2,48,384]{3,2,1,0:T(8,128)(2,1)S(1)}, bf16[4,2,48,384]{3,2,1,0:T(8,128)(2,1)S(1)}, u32[]{:S(2)}, u32[]{:S(2)}) collective-permute-start(bf16[4,2,48,384]{3,2,1,0:T(8,128)(2,1)S(1)} %broadcast_select_fusion.1), channel_id=1, source_target_pairs={{0,1},{1,0},{2,3},{3,2},{4,5},{5,4},{6,7},{7,6},{8,9},{9,8},{10,11... | collective-permute-start | bytes 884744 | tf_op jit(solution)/shard_map/ppermute | solution.py:520
  442.8 10.8 %collective-permute-start.13 = (f32[14080]{0:T(1024)S(1)}, f32[14080]{0:T(1024)S(1)}, u32[]{:S(2)}, u32[]{:S(2)}) collective-permute-start(f32[14080]{0:T(1024)S(1)} %add.149), channel_id=1, source_target_pairs={{0,8},{2,10},{4,12},{6,14},{8,0},{10,2},{12,4},{14,6},{16,24},{18,... | collective-permute-start | bytes 168968 | tf_op jit(solution)/shard_map/ppermute | solution.py:520
  453.9 13.7 %collective-permute-start.14 = (bf16[4,48,384]{2,1,0:T(8,128)(2,1)S(1)}, bf16[4,48,384]{2,1,0:T(8,128)(2,1)S(1)}, u32[]{:S(2)}, u32[]{:S(2)}) collective-permute-start(bf16[4,48,384]{2,1,0:T(8,128)(2,1)S(1)} %dynamic-slice_bitcast_fusion.3), channel_id=1, source_target_pairs={{0,8},{2,10},{4,12},{6,14},{8,0},{10,2},{12,4},{14,6},{16,24},{18,... | collective-permute-start | bytes 442376 | tf_op jit(solution)/shard_map/ppermute | solution.py:520
  454.4 13.2 %collective-permute-start.15 = (bf16[4,48,384]{2,1,0:T(8,128)(2,1)S(1)}, bf16[4,48,384]{2,1,0:T(8,128)(2,1)S(1)}, u32[]{:S(2)}, u32[]{:S(2)}) collective-permute-start(bf16[4,48,384]{2,1,0:T(8,128)(2,1)S(1)} %dynamic-slice_bitcast_fusion.2), channel_id=1, source_target_pairs={{0,8},{2,10},{4,12},{6,14},{8,0},{10,2},{12,4},{14,6},{16,24},{18,... | collective-permute-start | bytes 442376 | tf_op jit(solution)/shard_map/ppermute | solution.py:520
  456.0 11.6 %collective-permute-start.16 = (f32[14080]{0:T(1024)S(1)}, f32[14080]{0:T(1024)S(1)}, u32[]{:S(2)}, u32[]{:S(2)}) collective-permute-start(f32[14080]{0:T(1024)S(1)} %add.154), channel_id=1, source_target_pairs={{0,16},{2,18},{4,20},{6,22},{8,24},{10,26},{12,28},{14,30},{16,0},... | collective-permute-start | bytes 168968 | tf_op jit(solution)/shard_map/ppermute | solution.py:520
  467.7 9.9 %collective-permute-start.17 = (bf16[4,48,384]{2,1,0:T(8,128)(2,1)S(1)}, bf16[4,48,384]{2,1,0:T(8,128)(2,1)S(1)}, u32[]{:S(2)}, u32[]{:S(2)}) collective-permute-start(bf16[4,48,384]{2,1,0:T(8,128)(2,1)S(1)} %broadcast_select_fusion.3), channel_id=1, source_target_pairs={{0,16},{2,18},{4,20},{6,22},{8,24},{10,26},{12,28},{14,30},{16,0},... | collective-permute-start | bytes 442376 | tf_op jit(solution)/shard_map/ppermute | solution.py:520
  468.0 9.5 %collective-permute-start.18 = (f32[14080]{0:T(1024)S(1)}, f32[14080]{0:T(1024)S(1)}, u32[]{:S(2)}, u32[]{:S(2)}) collective-permute-start(f32[14080]{0:T(1024)S(1)} %add.157), channel_id=1, source_target_pairs={{0,1},{1,0},{2,3},{3,2},{4,5},{5,4},{6,7},{7,6},{8,9},{9,8},{10,11... | collective-permute-start | bytes 168968 | tf_op jit(solution)/shard_map/ppermute | solution.py:520
  (14 other events, 56.4 us)
Sparse Core Ops, SparseCore 0:
  283.1 112.8 reduce-scatter.1
